TPU v7x, 32 devices: a whole 2x2x4 slice. The times are simulated.
32 devices in a mesh: row: 8 (over y, x, core), col: 4 (over z).
Axes of the slice: x: 2, y: 2, z: 4, core: 2. Of those that a mesh axis runs over, the one named last changes fastest.
Arguments:
- left_factor: bfloat16 [2, 512, 2048], P(None, 'col', 'row'), may hold values from -6 to 6
- right_factor: bfloat16 [2, 512, 1024], P(None, 'row', 'col'), may hold values from -0.1875 to 0.1875
- recorded: bfloat16 [2, 2048, 1024], P(None, 'row', 'col'), may hold values from -6 to 6
- partner: int32 [1024], replicated, may hold values from 0 to 1023, as said below
- delay: int32 [1024], replicated, may hold values from 0 to 63
Outputs:
- left_out: bfloat16 [2, 512, 2048], P(None, 'col', 'row')
- right_out: bfloat16 [2, 512, 1024], P(None, 'row', 'col')
Inputs may be any that keep to these rules, and one draw needn't show every extreme that they name: partner[s] lies in the block of 256 consecutive shots that holds s (blocks start at multiples of 256) or in the block after it, the last block being followed by the first; a shot may be its own partner, and some shots are the partner of many shots.
All inputs are finite; a program needn't handle non-finite values.
Results may differ from a plain program's by a relative error of at most 0.011.
Values may be sent and summed in bfloat16 or wider, within the bound.
No kernel may reach another device: no remote copies, remote signals or barrier semaphores. Data moves between devices by JAX's collectives and lax.ppermute only.
A program may use at most 64 MiB of HBM per device.

v0:
```python
import math

import jax
import jax.numpy as jnp
from jax import lax
from jax.sharding import PartitionSpec as P

ITERS = 2
NDELAY = 64


def passed_along(shard, axis, by):
    size = lax.axis_size(axis)
    return lax.ppermute(shard, axis, [(i, (i + by) % size) for i in range(size)])


def product(left_whole, right_whole):

    def mult(a, b):
        return jnp.einsum("kr,kc->rc", a, b, preferred_element_type=jnp.float32)

    real_part = mult(left_whole[0], right_whole[0]) + mult(left_whole[1], right_whole[1])
    imag_part = mult(left_whole[1], right_whole[0]) - mult(left_whole[0], right_whole[1])
    return jnp.stack([real_part, imag_part]).astype(jnp.bfloat16)


def blend_cols(own_x, other_x, own_cos, own_sin, other_cos, other_sin, rec):
    ownr = own_x[0].astype(jnp.float32)
    owni = own_x[1].astype(jnp.float32)
    othr = other_x[0].astype(jnp.float32)
    othi = other_x[1].astype(jnp.float32)
    recf = rec.astype(jnp.float32)
    real_part = own_cos * ownr - own_sin * owni + other_cos * othr - other_sin * othi - recf[0]
    imag_part = own_cos * owni + own_sin * ownr + other_cos * othi + other_sin * othr - recf[1]
    return jnp.stack([real_part, imag_part]).astype(jnp.bfloat16)


def gradients(left_whole, right_whole, adjoint):

    def lmul(a, g):
        return jnp.einsum("kc,rc->kr", a, g, preferred_element_type=jnp.float32)

    def rmul(a, g):
        return jnp.einsum("kr,rc->kc", a, g, preferred_element_type=jnp.float32)

    glr = lmul(right_whole[0], adjoint[0]) - lmul(right_whole[1], adjoint[1])
    gli = lmul(right_whole[1], adjoint[0]) + lmul(right_whole[0], adjoint[1])
    grr = rmul(left_whole[0], adjoint[0]) + rmul(left_whole[1], adjoint[1])
    gri = rmul(left_whole[1], adjoint[0]) - rmul(left_whole[0], adjoint[1])
    return (jnp.stack([glr, gli]), jnp.stack([grr, gri]))


def on_device(left_factor, right_factor, recorded, partner, delay):
    shots_dev = recorded.shape[2]
    rows_dev = recorded.shape[1]
    shots_all = partner.shape[0]
    rows_all = rows_dev * lax.axis_size("row")
    rank_full = left_factor.shape[1] * lax.axis_size("col")
    eta_left = 0.1 * math.sqrt(rank_full / shots_all)
    eta_right = 0.05 / math.sqrt(rank_full * rows_all)
    start = lax.axis_index("col") * shots_dev
    theta = 2.0 * math.pi * delay.astype(jnp.float32) / NDELAY
    pcos = jnp.cos(theta)
    psin = jnp.sin(theta)
    partner_own = lax.dynamic_slice_in_dim(partner, start, shots_dev, 0)
    own_cos = lax.dynamic_slice_in_dim(pcos, start, shots_dev, 0)
    own_sin = lax.dynamic_slice_in_dim(psin, start, shots_dev, 0)
    lower = start - shots_dev
    ext_ids = jnp.mod(lower + lax.iota(jnp.int32, 2 * shots_dev), shots_all)
    partner_ext = jnp.take(partner, ext_ids)
    targets = start + lax.broadcasted_iota(jnp.int32, (1, shots_dev), 1)
    onehot = (partner_ext[:, None] == targets).astype(jnp.bfloat16)
    next_index = jnp.mod(partner_own - start, shots_all)
    part_cos = jnp.take(pcos, partner_own)
    part_sin = jnp.take(psin, partner_own)
    left_shard = left_factor
    right_shard = right_factor
    left_whole = None
    right_whole = None
    for step in range(ITERS):
        left_whole = lax.all_gather(left_shard, "col", axis=1, tiled=True)
        right_whole = lax.all_gather(right_shard, "row", axis=1, tiled=True)
        tile = product(left_whole, right_whole)
        tile_next = passed_along(tile, "col", -1)
        pair_tiles = jnp.concatenate([tile, tile_next], axis=2)
        other = jnp.take(pair_tiles, next_index, axis=2)
        res = blend_cols(tile, other, own_cos, own_sin, part_cos, part_sin, recorded)
        res_prev = passed_along(res, "col", 1)
        res_ext = jnp.concatenate([res_prev, res], axis=2)
        folded = jnp.einsum("zrs,sc->zrc", res_ext, onehot, preferred_element_type=jnp.float32)
        summed = res.astype(jnp.float32) + folded
        adj_real = own_cos * summed[0] + own_sin * summed[1]
        adj_imag = own_cos * summed[1] - own_sin * summed[0]
        adjoint = jnp.stack([adj_real, adj_imag]).astype(jnp.bfloat16)
        grad_left, grad_right = gradients(left_whole, right_whole, adjoint)
        left_part = lax.psum_scatter(grad_left, "col", scatter_dimension=1, tiled=True)
        right_part = lax.psum_scatter(grad_right, "row", scatter_dimension=1, tiled=True)
        left_shard = (left_shard.astype(jnp.float32) - eta_left * left_part).astype(jnp.bfloat16)
        right_shard = (right_shard.astype(jnp.float32) - eta_right * right_part).astype(
            jnp.bfloat16
        )
    return (left_shard, right_shard)


def solution(mesh):
    in_specs = (P(None, "col", "row"), P(None, "row", "col"), P(None, "row", "col"), P(), P())
    out_specs = (P(None, "col", "row"), P(None, "row", "col"))
    return jax.shard_map(
        on_device, mesh=mesh, in_specs=in_specs, out_specs=out_specs, check_vma=False
    )
```

profile of v0, /device:TPU:0, one launch (start us, length us, event | category | flops | bytes accessed | tf_op | source)
XLA Modules:
  0.0 234.6 jit_solution(15192506505127091848)
XLA Ops:
  8.1 17.6 %all_gather.12 = bf16[2,512,256]{2,1,0:T(8,128)(2,1)S(1)} all-gather(bf16[2,128,256]{2,1,0:T(8,128)(2,1)} %param.9), channel_id=1, replica_groups=mesh['row'=8,'col'=4] {'col'}, dimensions={1}, use_global_device_ids=true | all-gather | bytes 655360 | tf_op jit(solution)/shard_map/all_gather | solution.py:81
  25.6 9.9 %all_gather.13 = bf16[2,512,256]{2,1,0:T(8,128)(2,1)S(1)} all-gather(bf16[2,64,256]{2,1,0:T(8,128)(2,1)S(1)} %copy-done.3), channel_id=1, replica_groups=mesh['row'=8,'col'=4] {'row'}, dimensions={1}, use_global_device_ids=true | all-gather | bytes 589824 | tf_op jit(solution)/shard_map/all_gather | solution.py:82
  36.6 4.2 %collective-permute-start = (bf16[2,256,256]{1,2,0:T(8,128)(2,1)S(1)}, bf16[2,256,256]{1,2,0:T(8,128)(2,1)S(1)}, u32[]{:S(2)}, u32[]{:S(2)}) collective-permute-start(bf16[2,256,256]{1,2,0:T(8,128)(2,1)S(1)} %pad_maximum_fusion.6), channel_id=1, source_target_pairs={{0,3},{1,0},{2,1},{3,2},{4,7},{5,4},{6,5},{7,6},{8,11},{9,8},{10,9... | collective-permute-start | bytes 786440 | tf_op jit(solution)/shard_map/ppermute | solution.py:14
  42.5 1.4 gather_fusion.3
  43.9 1.4 gather_fusion.1
  45.6 1.3 collective-permute-done
  47.5 1.2 gather_fusion.2
  49.7 2.3 gather_fusion
  52.0 7.5 %collective-permute-done.1 = bf16[2,256,256]{1,2,0:T(8,128)(2,1)S(1)} collective-permute-done((bf16[2,256,256]{1,2,0:T(8,128)(2,1)S(1)}, bf16[2,256,256]{1,2,0:T(8,128)(2,1)S(1)}, u32[]{:S(2)}, u32[]{:S(2)}) %collective-permute-start.1) | collective-permute-done | bytes 262176 | tf_op jit(solution)/shard_map/ppermute | solution.py:14
  61.8 1.3 copy.71
  63.7 1.0 pad_maximum_fusion
  67.7 50.6 %all-reduce.5.cloned.1.call-done = f32[2,512,256]{2,0,1:T(2,128)} async-done(((f32[2,512,256]{2,0,1:T(2,128)}), f32[2,512,256]{2,0,1:T(2,128)}) %all-reduce.5.cloned.1.call-update) | async-done | bytes 1048592
  118.3 1.0 fusion.73
  119.3 8.9 %all_gather.14 = bf16[2,512,256]{2,0,1:T(2,128)(2,1)S(1)} all-gather(bf16[2,64,256]{2,0,1:T(2,128)(2,1)S(1)} %fusion.73), channel_id=1, replica_groups=mesh['row'=8,'col'=4] {'row'}, dimensions={1}, use_global_device_ids=true | all-gather | bytes 589824 | tf_op jit(solution)/shard_map/all_gather | solution.py:82
  130.1 15.4 %all_gather.15 = bf16[2,512,256]{1,2,0:T(8,128)(2,1)S(1)} all-gather(bf16[2,128,256]{1,2,0:T(8,128)(2,1)S(1)} %subtract_convert_fusion.2), channel_id=1, replica_groups=mesh['row'=8,'col'=4] {'col'}, dimensions={1}, use_global_device_ids=true | all-gather | bytes 655360 | tf_op jit(solution)/shard_map/all_gather | solution.py:81
  146.6 2.3 collective-permute-start.2
  148.9 5.1 %collective-permute-done.2 = bf16[2,256,256]{1,2,0:T(8,128)(2,1)S(1)} collective-permute-done((bf16[2,256,256]{1,2,0:T(8,128)(2,1)S(1)}, bf16[2,256,256]{1,2,0:T(8,128)(2,1)S(1)}, u32[]{:S(2)}, u32[]{:S(2)}) %collective-permute-start.2) | collective-permute-done | bytes 262176 | tf_op jit(solution)/shard_map/ppermute | solution.py:14
  154.6 1.2 gather_fusion.4
  156.3 1.0 collective-permute-start.3
  157.3 7.4 %collective-permute-done.3 = bf16[2,256,256]{1,2,0:T(8,128)(2,1)S(1)} collective-permute-done((bf16[2,256,256]{1,2,0:T(8,128)(2,1)S(1)}, bf16[2,256,256]{1,2,0:T(8,128)(2,1)S(1)}, u32[]{:S(2)}, u32[]{:S(2)}) %collective-permute-start.3) | collective-permute-done | bytes 262176 | tf_op jit(solution)/shard_map/ppermute | solution.py:14
  166.7 1.8 copy.82
  169.4 1.1 pad_maximum_fusion.2
  170.5 53.2 %all-reduce.7.cloned.1.call-done = f32[2,512,256]{2,0,1:T(2,128)} async-done(((f32[2,512,256]{2,0,1:T(2,128)}), f32[2,512,256]{2,0,1:T(2,128)}) %all-reduce.7.cloned.1.call-update) | async-done | bytes 1048592
  223.7 1.0 fusion.71
  (87 shorter events, 19.0 us)
Async XLA Ops:
  8.0 17.6 %copy-start.3 = (bf16[2,64,256]{2,1,0:T(8,128)(2,1)S(1)}, bf16[2,64,256]{2,1,0:T(8,128)(2,1)}, u32[]{:S(2)}) copy-start(bf16[2,64,256]{2,1,0:T(8,128)(2,1)} %param.10) | copy-start | bytes 196612
  8.0 110.3 %all-reduce.5.cloned.1.call-start = ((), (), s32[]{:S(2)}) async-start(), calls=%async_computation.4 | async-start | bytes 2097152
  36.6 10.3 %collective-permute-start = (bf16[2,256,256]{1,2,0:T(8,128)(2,1)S(1)}, bf16[2,256,256]{1,2,0:T(8,128)(2,1)S(1)}, u32[]{:S(2)}, u32[]{:S(2)}) collective-permute-start(bf16[2,256,256]{1,2,0:T(8,128)(2,1)S(1)} %pad_maximum_fusion.6), channel_id=1, source_target_pairs={{0,3},{1,0},{2,1},{3,2},{4,7},{5,4},{6,5},{7,6},{8,11},{9,8},{10,9... | collective-permute-start | bytes 786440 | tf_op jit(solution)/shard_map/ppermute | solution.py:14
  40.8 0.7 copy-start
  41.7 0.7 copy-start.4
  43.9 1.5 copy-start.2
  49.1 10.4 %collective-permute-start.1 = (bf16[2,256,256]{1,2,0:T(8,128)(2,1)S(1)}, bf16[2,256,256]{1,2,0:T(8,128)(2,1)S(1)}, u32[]{:S(2)}, u32[]{:S(2)}) collective-permute-start(bf16[2,256,256]{1,2,0:T(8,128)(2,1)S(1)} %pad_maximum_fusion.7), channel_id=1, source_target_pairs={{0,1},{1,2},{2,3},{3,0},{4,5},{5,6},{6,7},{7,4},{8,9},{9,10},{10,1... | collective-permute-start | bytes 786440 | tf_op jit(solution)/shard_map/ppermute | solution.py:14
  63.1 65.9 %reduce-scatter.3.cloned.1.call-start = ((), (), s32[]{:S(2)}) async-start(), calls=%async_computation.2 | async-start | bytes 1310720 | tf_op jit(solution)/shard_map/reduce_scatter | solution.py:96
  64.8 0.9 copy-start.1
  64.8 158.9 %all-reduce.7.cloned.1.call-start = ((), (), s32[]{:S(2)}) async-start(), calls=%async_computation.5 | async-start | bytes 2097152
  65.8 0.7 copy-start.5
  146.6 7.4 %collective-permute-start.2 = (bf16[2,256,256]{1,2,0:T(8,128)(2,1)S(1)}, bf16[2,256,256]{1,2,0:T(8,128)(2,1)S(1)}, u32[]{:S(2)}, u32[]{:S(2)}) collective-permute-start(bf16[2,256,256]{1,2,0:T(8,128)(2,1)S(1)} %pad_maximum_fusion.8), channel_id=1, source_target_pairs={{0,3},{1,0},{2,1},{3,2},{4,7},{5,4},{6,5},{7,6},{8,11},{9,8},{10,9... | collective-permute-start | bytes 786440 | tf_op jit(solution)/shard_map/ppermute | solution.py:14
  156.3 8.4 %collective-permute-start.3 = (bf16[2,256,256]{1,2,0:T(8,128)(2,1)S(1)}, bf16[2,256,256]{1,2,0:T(8,128)(2,1)S(1)}, u32[]{:S(2)}, u32[]{:S(2)}) collective-permute-start(bf16[2,256,256]{1,2,0:T(8,128)(2,1)S(1)} %pad_maximum_fusion.9), channel_id=1, source_target_pairs={{0,1},{1,2},{2,3},{3,0},{4,5},{5,6},{6,7},{7,4},{8,9},{9,10},{10,1... | collective-permute-start | bytes 786440 | tf_op jit(solution)/shard_map/ppermute | solution.py:14
  168.5 56.8 %reduce-scatter.5.cloned.1.call-start = ((), (), s32[]{:S(2)}) async-start(), calls=%async_computation.3 | async-start | bytes 1310720 | tf_op jit(solution)/shard_map/reduce_scatter | solution.py:96
Sparse Core Ops, SparseCore 0:
  63.3 55.0 all-reduce.4
  168.7 55.0 all-reduce.6
Sparse Core Ops, SparseCore 1:
  65.9 25.6 reduce-scatter.2
  171.4 25.5 reduce-scatter.4
where the time goes:
time: 235 us
  waiting for transfers between devices  125 us (53%)
  blocking collectives  51.7 us (22%)
  local copies, waits for them, and re-layouts  17.7 us (8%)
  between operations  16.6 us (7%)
  starting transfers between devices  8.2 us (3%)
  other arithmetic  7.84 us (3%)
  matrix products  7.33 us (3%)
    unnamed x6, waiting for transfers between devices  104 us
    all_gather x2, blocking collectives, on_device(): left_whole = lax.all_gather(left_shard, 'col', axis=1, tiled=True)  33 us
    ppermute x4, waiting for transfers between devices, passed_along(): lax.ppermute(shard, axis, [(i, (i + by) % size) for i in range(size)])  21.3 us
    all_gather x2, blocking collectives, on_device(): right_whole = lax.all_gather(right_shard, 'row', axis=1, tiled=True)  18.7 us
    ppermute x4, starting transfers between devices, passed_along(): lax.ppermute(shard, axis, [(i, (i + by) % size) for i in range(size)])  8.03 us
    unnamed x17, local copies, waits for them, and re-layouts  5.08 us
  transfers between devices with their start and end apart: 8, of which 6 were waited for; matrix products, arithmetic and copies ran while one was open for 6% of the time, Pallas kernels for 0%

commit v1 on v0

v1 whole, which is shorter than its diff:
```python
import math

import jax
import jax.numpy as jnp
from jax import lax
from jax.sharding import PartitionSpec as P

ITERS = 2
NDELAY = 64
BF = jnp.bfloat16
F32 = jnp.float32


def exchanged(shard, axis, flip):
    size = lax.axis_size(axis)
    return lax.ppermute(shard, axis, [(i, i ^ flip) for i in range(size)])


def passed_along(shard, axis, by):
    size = lax.axis_size(axis)
    return lax.ppermute(shard, axis, [(i, (i + by) % size) for i in range(size)])


def in_order(parts, me, axis):
    stacked = jnp.stack(parts)
    order = jnp.bitwise_xor(lax.iota(jnp.int32, len(parts)), me)
    out = [lax.dynamic_index_in_dim(stacked, order[i], 0, False) for i in range(len(parts))]
    return jnp.concatenate(out, axis=1)


def gathered(shard, axis):
    size = lax.axis_size(axis)
    parts = [shard] + [exchanged(shard, axis, d) for d in range(1, size)]
    return in_order(parts, lax.axis_index(axis), axis)


def scattered_sum(whole, axis):
    size = lax.axis_size(axis)
    me = lax.axis_index(axis)
    width = whole.shape[1] // size
    total = lax.dynamic_slice_in_dim(whole, me * width, width, 1)
    for d in range(1, size):
        part = lax.dynamic_slice_in_dim(whole, (me ^ d) * width, width, 1).astype(BF)
        total = total + exchanged(part, axis, d).astype(F32)
    return total


def mult(spec, a, b):
    return jnp.einsum(spec, a, b, preferred_element_type=F32)


def on_device(left_factor, right_factor, recorded, partner, delay):
    shots_dev = recorded.shape[2]
    rows_dev = recorded.shape[1]
    shots_all = partner.shape[0]
    rows_all = rows_dev * lax.axis_size("row")
    rank_full = left_factor.shape[1] * lax.axis_size("col")
    eta_left = 0.1 * math.sqrt(rank_full / shots_all)
    eta_right = 0.05 / math.sqrt(rank_full * rows_all)
    block = lax.axis_index("col")
    blocks = lax.axis_size("col")

    def of_block(vector, by):
        return lax.dynamic_slice_in_dim(vector, jnp.mod(block + by, blocks) * shots_dev, shots_dev, 0)

    def picks(by):
        start = jnp.mod(block + by, blocks) * shots_dev
        near = jnp.mod(of_block(partner, by) - start, shots_all)
        return (lax.broadcasted_iota(jnp.int32, (2 * shots_dev, shots_dev), 0) == near[None, :]).astype(BF)

    def phases(values):
        theta = 2.0 * math.pi * values / NDELAY
        return jnp.cos(theta), jnp.sin(theta)

    pick_prev, pick_own, pick_next = picks(-1), picks(0), picks(1)
    delay_own, delay_next = of_block(delay, 0).astype(F32), of_block(delay, 1).astype(F32)
    both = jnp.concatenate([delay_own, delay_next]).astype(BF)
    delay_part = mult("c,cs->s", both, pick_own)
    cos_own, sin_own = phases(delay_own)
    cos_next, sin_next = phases(delay_next)
    cos_part, sin_part = phases(delay_part)

    def mixed(right_own, right_next):
        pair = jnp.concatenate([right_own, right_next], axis=2)
        part = mult("zkc,cs->zks", pair, pick_own)
        own = right_own.astype(F32)
        real = cos_own * own[0] + sin_own * own[1] + cos_part * part[0] + sin_part * part[1]
        imag = cos_own * own[1] - sin_own * own[0] + cos_part * part[1] - sin_part * part[0]
        return jnp.stack([real, imag]).astype(BF)

    def folded(w_prev, w_own, pick_before, pick_here, cos, sin):
        s = w_own.astype(F32)
        s = s + mult("zks,cs->zkc", w_prev, pick_before[shots_dev:]) + mult("zks,cs->zkc", w_own, pick_here[:shots_dev])
        return jnp.stack([cos * s[0] - sin * s[1], cos * s[1] + sin * s[0]])

    rec = recorded.astype(F32)
    left = left_factor
    right = right_factor
    right_next = passed_along(right, "col", -1)
    for step in range(ITERS):
        mixed_shard = mixed(right, right_next)
        q = gathered(mixed_shard, "row")
        lw = gathered(left, "col")
        br = mult("kr,kc->rc", lw[0], q[0]) + mult("kr,kc->rc", lw[1], q[1]) - rec[0]
        bi = mult("kr,kc->rc", lw[1], q[0]) - mult("kr,kc->rc", lw[0], q[1]) - rec[1]
        br, bi = br.astype(BF), bi.astype(BF)
        wr = mult("kr,rc->kc", lw[0], br) + mult("kr,rc->kc", lw[1], bi)
        wi = mult("kr,rc->kc", lw[1], br) - mult("kr,rc->kc", lw[0], bi)
        glr = mult("kc,rc->kr", q[0], br) - mult("kc,rc->kr", q[1], bi)
        gli = mult("kc,rc->kr", q[1], br) + mult("kc,rc->kr", q[0], bi)
        w_own = scattered_sum(jnp.stack([wr, wi]), "row").astype(BF)
        w_prev = passed_along(w_own, "col", 1)
        left = (left.astype(F32) - eta_left * scattered_sum(jnp.stack([glr, gli]), "col")).astype(BF)
        if step + 1 < ITERS:
            w_next = passed_along(w_own, "col", -1)
            grad_next = folded(w_own, w_next, pick_own, pick_next, cos_next, sin_next)
            right_next = (right_next.astype(F32) - eta_right * grad_next).astype(BF)
        grad_own = folded(w_prev, w_own, pick_prev, pick_own, cos_own, sin_own)
        right = (right.astype(F32) - eta_right * grad_own).astype(BF)
    return (left, right)


def solution(mesh):
    in_specs = (P(None, "col", "row"), P(None, "row", "col"), P(None, "row", "col"), P(), P())
    out_specs = (P(None, "col", "row"), P(None, "row", "col"))
    return jax.shard_map(
        on_device, mesh=mesh, in_specs=in_specs, out_specs=out_specs, check_vma=False
    )
```

time: 235 us -> 131 us (0.56)
  waiting for transfers between devices: 125 us -> 43.1 us
  blocking collectives: 51.7 us -> 0 us
  starting transfers between devices: 8.2 us -> 50.1 us
  local copies, waits for them, and re-layouts: 17.7 us -> 2.52 us
  between operations: 16.6 us -> 24.2 us
  other arithmetic: 7.84 us -> 2.74 us
    unnamed x6 -> x0, waiting for transfers between devices: 104 us -> none
    all_gather x4 -> x0, blocking collectives: 51.7 us -> none  [the longest x2 33 us: on_device(): left_whole = lax.all_gather(left_shard, 'col', axis=1, tiled=True)]
    ppermute x0 -> x40, starting transfers between devices: none -> 44.2 us  [exchanged(): return lax.ppermute(shard, axis, [(i, i ^ flip) for i in range(size)])]
    ppermute x0 -> x40, waiting for transfers between devices: none -> 30.9 us  [exchanged(): return lax.ppermute(shard, axis, [(i, i ^ flip) for i in range(size)])]
    ppermute x4, waiting for transfers between devices: 21.3 us -> 12.2 us  [passed_along(): lax.ppermute(shard, axis, [(i, (i + by) % size) for i in range(size)])]
    gather x5 -> x0, local copies, waits for them, and re-layouts: 7.47 us -> none  [the longest x2 2.46 us: on_device(): other = jnp.take(pair_tiles, next_index, axis=2)]
    unnamed x17 -> x36, local copies, waits for them, and re-layouts: 5.08 us -> 1.09 us
    another operation x2, local copies, waits for them, and re-layouts: 3.11 us -> 0.01 us  [in_order(): stacked = jnp.stack(parts)]
  transfers between devices with their start and end apart: 8 -> 44, of which waited for: 6 -> 17; matrix products, arithmetic and copies ran while one was open for 6% -> 5% of each run, Pallas kernels for 0% -> 0%
where the time goes in v1:
time: 131 us
  starting transfers between devices  50.1 us (38%)
  waiting for transfers between devices  43.1 us (33%)
  between operations  24.2 us (18%)
  matrix products  7.92 us (6%)
  other arithmetic  2.74 us (2%)
  local copies, waits for them, and re-layouts  2.52 us (2%)
    ppermute x40, starting transfers between devices, exchanged(): return lax.ppermute(shard, axis, [(i, i ^ flip) for i in range(size)])  44.2 us
    ppermute x40, waiting for transfers between devices, exchanged(): return lax.ppermute(shard, axis, [(i, i ^ flip) for i in range(size)])  30.9 us
    ppermute x4, waiting for transfers between devices, passed_along(): lax.ppermute(shard, axis, [(i, (i + by) % size) for i in range(size)])  12.2 us
    dot_general x33, matrix products, mult(): return jnp.einsum(spec, a, b, preferred_element_type=F32)  7.92 us
    ppermute x4, starting transfers between devices, passed_along(): lax.ppermute(shard, axis, [(i, (i + by) % size) for i in range(size)])  5.88 us
  transfers between devices with their start and end apart: 44, of which 17 were waited for; matrix products, arithmetic and copies ran while one was open for 5% of the time, Pallas kernels for 0%

profile of v1, /device:TPU:0, one launch (start us, length us, event | category | flops | bytes accessed | tf_op | source)
XLA Modules:
  0.0 130.5 jit_solution(11599513425146609786)
XLA Ops:
  0.6 5.1 %collective-permute-start.10 = (bf16[2,128,256]{2,1,0:T(8,128)(2,1)}, bf16[2,128,256]{2,1,0:T(8,128)(2,1)S(1)}, u32[]{:S(2)}, u32[]{:S(2)}) collective-permute-start(bf16[2,128,256]{2,1,0:T(8,128)(2,1)} %param.5), channel_id=1, source_target_pairs={{0,3},{1,2},{2,1},{3,0},{4,7},{5,6},{6,5},{7,4},{8,11},{9,10},{10,... | collective-permute-start | bytes 393224 | tf_op jit(solution)/shard_map/ppermute | solution.py:16
  6.4 3.7 %collective-permute-start = (bf16[2,64,256]{2,1,0:T(8,128)(2,1)}, bf16[2,64,256]{2,1,0:T(8,128)(2,1)S(1)}, u32[]{:S(2)}, u32[]{:S(2)}) collective-permute-start(bf16[2,64,256]{2,1,0:T(8,128)(2,1)} %param.6), channel_id=1, source_target_pairs={{0,3},{1,0},{2,1},{3,2},{4,7},{5,4},{6,5},{7,6},{8,11},{9,8},{10,9... | collective-permute-start | bytes 196616 | tf_op jit(solution)/shard_map/ppermute | solution.py:21
  35.3 1.6 %collective-permute-start.2 = (bf16[2,64,256]{2,1,0:T(8,128)(2,1)S(1)}, bf16[2,64,256]{2,1,0:T(8,128)(2,1)S(1)}, u32[]{:S(2)}, u32[]{:S(2)}) collective-permute-start(bf16[2,64,256]{2,1,0:T(8,128)(2,1)S(1)} %pad_maximum_fusion.4), channel_id=1, source_target_pairs={{0,8},{4,12},{8,0},{12,4},{16,24},{20,28},{24,16},{28,20},{1,9},{5... | collective-permute-start | bytes 196616 | tf_op jit(solution)/shard_map/ppermute | solution.py:16
  37.9 2.0 %collective-permute-done.2 = bf16[2,64,256]{2,1,0:T(8,128)(2,1)S(1)} collective-permute-done((bf16[2,64,256]{2,1,0:T(8,128)(2,1)S(1)}, bf16[2,64,256]{2,1,0:T(8,128)(2,1)S(1)}, u32[]{:S(2)}, u32[]{:S(2)}) %collective-permute-start.2) | collective-permute-done | bytes 65568 | tf_op jit(solution)/shard_map/ppermute | solution.py:16
  39.9 1.5 %collective-permute-start.4 = (bf16[2,64,256]{2,1,0:T(8,128)(2,1)S(1)}, bf16[2,64,256]{2,1,0:T(8,128)(2,1)S(1)}, u32[]{:S(2)}, u32[]{:S(2)}) collective-permute-start(bf16[2,64,256]{2,1,0:T(8,128)(2,1)S(1)} %pad_maximum_fusion.4), channel_id=1, source_target_pairs={{0,16},{4,20},{8,24},{12,28},{16,0},{20,4},{24,8},{28,12},{1,17},{... | collective-permute-start | bytes 196616 | tf_op jit(solution)/shard_map/ppermute | solution.py:16
  42.3 1.8 %collective-permute-done.4 = bf16[2,64,256]{2,1,0:T(8,128)(2,1)S(1)} collective-permute-done((bf16[2,64,256]{2,1,0:T(8,128)(2,1)S(1)}, bf16[2,64,256]{2,1,0:T(8,128)(2,1)S(1)}, u32[]{:S(2)}, u32[]{:S(2)}) %collective-permute-start.4) | collective-permute-done | bytes 65568 | tf_op jit(solution)/shard_map/ppermute | solution.py:16
  44.1 3.3 %collective-permute-start.6 = (bf16[2,64,256]{2,1,0:T(8,128)(2,1)S(1)}, bf16[2,64,256]{2,1,0:T(8,128)(2,1)S(1)}, u32[]{:S(2)}, u32[]{:S(2)}) collective-permute-start(bf16[2,64,256]{2,1,0:T(8,128)(2,1)S(1)} %pad_maximum_fusion.4), channel_id=1, source_target_pairs={{0,24},{4,28},{8,16},{12,20},{16,8},{20,12},{24,0},{28,4},{1,25},{... | collective-permute-start | bytes 196616 | tf_op jit(solution)/shard_map/ppermute | solution.py:16
  47.7 2.0 %collective-permute-done.6 = bf16[2,64,256]{2,1,0:T(8,128)(2,1)S(1)} collective-permute-done((bf16[2,64,256]{2,1,0:T(8,128)(2,1)S(1)}, bf16[2,64,256]{2,1,0:T(8,128)(2,1)S(1)}, u32[]{:S(2)}, u32[]{:S(2)}) %collective-permute-start.6) | collective-permute-done | bytes 65568 | tf_op jit(solution)/shard_map/ppermute | solution.py:16
  49.7 2.4 %collective-permute-done.7 = bf16[2,64,256]{2,1,0:T(8,128)(2,1)S(1)} collective-permute-done((bf16[2,64,256]{2,1,0:T(8,128)(2,1)S(1)}, bf16[2,64,256]{2,1,0:T(8,128)(2,1)S(1)}, u32[]{:S(2)}, u32[]{:S(2)}) %collective-permute-start.7) | collective-permute-done | bytes 65568 | tf_op jit(solution)/shard_map/ppermute | solution.py:16
  57.2 1.6 %collective-permute-start.18 = (bf16[2,64,256]{2,1,0:T(8,128)(2,1)S(1)}, bf16[2,64,256]{2,1,0:T(8,128)(2,1)S(1)}, u32[]{:S(2)}, u32[]{:S(2)}) collective-permute-start(bf16[2,64,256]{2,1,0:T(8,128)(2,1)S(1)} %get-tuple-element.20), channel_id=1, source_target_pairs={{0,20},{4,16},{8,28},{12,24},{16,4},{20,0},{24,12},{28,8},{1,21},{... | collective-permute-start | bytes 196616 | tf_op jit(solution)/shard_map/ppermute | solution.py:16
  58.7 1.7 %collective-permute-start.17 = (bf16[2,64,256]{2,1,0:T(8,128)(2,1)S(1)}, bf16[2,64,256]{2,1,0:T(8,128)(2,1)S(1)}, u32[]{:S(2)}, u32[]{:S(2)}) collective-permute-start(bf16[2,64,256]{2,1,0:T(8,128)(2,1)S(1)} %get-tuple-element.19), channel_id=1, source_target_pairs={{0,16},{4,20},{8,24},{12,28},{16,0},{20,4},{24,8},{28,12},{1,17},{... | collective-permute-start | bytes 196616 | tf_op jit(solution)/shard_map/ppermute | solution.py:16
  63.1 1.7 %collective-permute-done.17 = bf16[2,64,256]{2,1,0:T(8,128)(2,1)S(1)} collective-permute-done((bf16[2,64,256]{2,1,0:T(8,128)(2,1)S(1)}, bf16[2,64,256]{2,1,0:T(8,128)(2,1)S(1)}, u32[]{:S(2)}, u32[]{:S(2)}) %collective-permute-start.17) | collective-permute-done | bytes 65568 | tf_op jit(solution)/shard_map/ppermute | solution.py:16
  64.8 2.7 %collective-permute-start.11 = (bf16[2,128,256]{2,1,0:T(8,128)(2,1)S(1)}, bf16[2,128,256]{2,1,0:T(8,128)(2,1)S(1)}, u32[]{:S(2)}, u32[]{:S(2)}) collective-permute-start(bf16[2,128,256]{2,1,0:T(8,128)(2,1)S(1)} %get-tuple-element.13), channel_id=1, source_target_pairs={{0,1},{1,0},{2,3},{3,2},{4,5},{5,4},{6,7},{7,6},{8,9},{9,8},{10,11... | collective-permute-start | bytes 393224 | tf_op jit(solution)/shard_map/ppermute | solution.py:16
  67.5 1.7 %collective-permute-start.22 = (bf16[2,64,256]{2,1,0:T(8,128)(2,1)S(1)}, bf16[2,64,256]{2,1,0:T(8,128)(2,1)S(1)}, u32[]{:S(2)}, u32[]{:S(2)}) collective-permute-start(bf16[2,64,256]{2,1,0:T(8,128)(2,1)S(1)} %fusion.135), channel_id=1, source_target_pairs={{0,3},{1,0},{2,1},{3,2},{4,7},{5,4},{6,5},{7,6},{8,11},{9,8},{10,9... | collective-permute-start | bytes 196616 | tf_op jit(solution)/shard_map/ppermute | solution.py:21
  69.8 9.8 %collective-permute-done.21 = bf16[2,64,256]{2,1,0:T(8,128)(2,1)S(1)} collective-permute-done((bf16[2,64,256]{2,1,0:T(8,128)(2,1)S(1)}, bf16[2,64,256]{2,1,0:T(8,128)(2,1)S(1)}, u32[]{:S(2)}, u32[]{:S(2)}) %collective-permute-start.21) | collective-permute-done | bytes 65568 | tf_op jit(solution)/shard_map/ppermute | solution.py:21
  85.8 1.5 %collective-permute-start.29 = (bf16[2,64,256]{2,1,0:T(8,128)(2,1)S(1)}, bf16[2,64,256]{2,1,0:T(8,128)(2,1)S(1)}, u32[]{:S(2)}, u32[]{:S(2)}) collective-permute-start(bf16[2,64,256]{2,1,0:T(8,128)(2,1)S(1)} %pad_maximum_fusion.5), channel_id=1, source_target_pairs={{0,28},{4,24},{8,20},{12,16},{16,12},{20,8},{24,4},{28,0},{1,29},{... | collective-permute-start | bytes 196616 | tf_op jit(solution)/shard_map/ppermute | solution.py:16
  87.9 4.1 %collective-permute-start.30 = (bf16[2,128,256]{2,1,0:T(8,128)(2,1)S(1)}, bf16[2,128,256]{2,1,0:T(8,128)(2,1)S(1)}, u32[]{:S(2)}, u32[]{:S(2)}) collective-permute-start(bf16[2,128,256]{2,1,0:T(8,128)(2,1)S(1)} %fusion.42), channel_id=1, source_target_pairs={{0,1},{1,0},{2,3},{3,2},{4,5},{5,4},{6,7},{7,6},{8,9},{9,8},{10,11... | collective-permute-start | bytes 393224 | tf_op jit(solution)/shard_map/ppermute | solution.py:16
  92.2 3.5 %collective-permute-done.32 = bf16[2,128,256]{2,1,0:T(8,128)(2,1)S(1)} collective-permute-done((bf16[2,128,256]{2,1,0:T(8,128)(2,1)S(1)}, bf16[2,128,256]{2,1,0:T(8,128)(2,1)S(1)}, u32[]{:S(2)}, u32[]{:S(2)}) %collective-permute-start.32) | collective-permute-done | bytes 131104 | tf_op jit(solution)/shard_map/ppermute | solution.py:16
  95.7 4.3 %collective-permute-done.31 = bf16[2,128,256]{2,1,0:T(8,128)(2,1)S(1)} collective-permute-done((bf16[2,128,256]{2,1,0:T(8,128)(2,1)S(1)}, bf16[2,128,256]{2,1,0:T(8,128)(2,1)S(1)}, u32[]{:S(2)}, u32[]{:S(2)}) %collective-permute-start.31) | collective-permute-done | bytes 131104 | tf_op jit(solution)/shard_map/ppermute | solution.py:16
  105.2 1.5 %collective-permute-start.40 = (bf16[2,64,256]{2,1,0:T(8,128)(2,1)S(1)}, bf16[2,64,256]{2,1,0:T(8,128)(2,1)S(1)}, u32[]{:S(2)}, u32[]{:S(2)}) collective-permute-start(bf16[2,64,256]{2,1,0:T(8,128)(2,1)S(1)} %get-tuple-element.8), channel_id=1, source_target_pairs={{0,20},{4,16},{8,28},{12,24},{16,4},{20,0},{24,12},{28,8},{1,21},{... | collective-permute-start | bytes 196616 | tf_op jit(solution)/shard_map/ppermute | solution.py:16
  113.2 3.9 %collective-permute-start.35 = (bf16[2,128,256]{2,1,0:T(8,128)(2,1)S(1)}, bf16[2,128,256]{2,1,0:T(8,128)(2,1)S(1)}, u32[]{:S(2)}, u32[]{:S(2)}) collective-permute-start(bf16[2,128,256]{2,1,0:T(8,128)(2,1)S(1)} %get-tuple-element.12), channel_id=1, source_target_pairs={{0,3},{1,2},{2,1},{3,0},{4,7},{5,6},{6,5},{7,4},{8,11},{9,10},{10,... | collective-permute-start | bytes 393224 | tf_op jit(solution)/shard_map/ppermute | solution.py:16
  117.7 2.3 %collective-permute-done.43 = bf16[2,64,256]{2,1,0:T(8,128)(2,1)S(1)} collective-permute-done((bf16[2,64,256]{2,1,0:T(8,128)(2,1)S(1)}, bf16[2,64,256]{2,1,0:T(8,128)(2,1)S(1)}, u32[]{:S(2)}, u32[]{:S(2)}) %collective-permute-start.43) | collective-permute-done | bytes 65568 | tf_op jit(solution)/shard_map/ppermute | solution.py:21
  121.1 1.7 %collective-permute-done.35 = bf16[2,128,256]{2,1,0:T(8,128)(2,1)S(1)} collective-permute-done((bf16[2,128,256]{2,1,0:T(8,128)(2,1)S(1)}, bf16[2,128,256]{2,1,0:T(8,128)(2,1)S(1)}, u32[]{:S(2)}, u32[]{:S(2)}) %collective-permute-start.35) | collective-permute-done | bytes 131104 | tf_op jit(solution)/shard_map/ppermute | solution.py:16
  122.8 6.9 %collective-permute-done.34 = bf16[2,128,256]{2,1,0:T(8,128)(2,1)S(1)} collective-permute-done((bf16[2,128,256]{2,1,0:T(8,128)(2,1)S(1)}, bf16[2,128,256]{2,1,0:T(8,128)(2,1)S(1)}, u32[]{:S(2)}, u32[]{:S(2)}) %collective-permute-start.34) | collective-permute-done | bytes 131104 | tf_op jit(solution)/shard_map/ppermute | solution.py:16
  (177 shorter events, 34.0 us)
Async XLA Ops:
  0.6 51.7 %collective-permute-start.10 = (bf16[2,128,256]{2,1,0:T(8,128)(2,1)}, bf16[2,128,256]{2,1,0:T(8,128)(2,1)S(1)}, u32[]{:S(2)}, u32[]{:S(2)}) collective-permute-start(bf16[2,128,256]{2,1,0:T(8,128)(2,1)} %param.5), channel_id=1, source_target_pairs={{0,3},{1,2},{2,1},{3,0},{4,7},{5,6},{6,5},{7,4},{8,11},{9,10},{10,... | collective-permute-start | bytes 393224 | tf_op jit(solution)/shard_map/ppermute | solution.py:16
  5.8 46.6 %collective-permute-start.9 = (bf16[2,128,256]{2,1,0:T(8,128)(2,1)}, bf16[2,128,256]{2,1,0:T(8,128)(2,1)S(1)}, u32[]{:S(2)}, u32[]{:S(2)}) collective-permute-start(bf16[2,128,256]{2,1,0:T(8,128)(2,1)} %param.5), channel_id=1, source_target_pairs={{0,2},{1,3},{2,0},{3,1},{4,6},{5,7},{6,4},{7,5},{8,10},{9,11},{10,... | collective-permute-start | bytes 393224 | tf_op jit(solution)/shard_map/ppermute | solution.py:16
  5.8 46.6 %collective-permute-start.8 = (bf16[2,128,256]{2,1,0:T(8,128)(2,1)}, bf16[2,128,256]{2,1,0:T(8,128)(2,1)S(1)}, u32[]{:S(2)}, u32[]{:S(2)}) collective-permute-start(bf16[2,128,256]{2,1,0:T(8,128)(2,1)} %param.5), channel_id=1, source_target_pairs={{0,1},{1,0},{2,3},{3,2},{4,5},{5,4},{6,7},{7,6},{8,9},{9,8},{10,11... | collective-permute-start | bytes 393224 | tf_op jit(solution)/shard_map/ppermute | solution.py:16
  6.4 28.5 %collective-permute-start = (bf16[2,64,256]{2,1,0:T(8,128)(2,1)}, bf16[2,64,256]{2,1,0:T(8,128)(2,1)S(1)}, u32[]{:S(2)}, u32[]{:S(2)}) collective-permute-start(bf16[2,64,256]{2,1,0:T(8,128)(2,1)} %param.6), channel_id=1, source_target_pairs={{0,3},{1,0},{2,1},{3,2},{4,7},{5,4},{6,5},{7,6},{8,11},{9,8},{10,9... | collective-permute-start | bytes 196616 | tf_op jit(solution)/shard_map/ppermute | solution.py:21
  41.4 6.1 %collective-permute-start.5 = (bf16[2,64,256]{2,1,0:T(8,128)(2,1)S(1)}, bf16[2,64,256]{2,1,0:T(8,128)(2,1)S(1)}, u32[]{:S(2)}, u32[]{:S(2)}) collective-permute-start(bf16[2,64,256]{2,1,0:T(8,128)(2,1)S(1)} %pad_maximum_fusion.4), channel_id=1, source_target_pairs={{0,20},{4,16},{8,28},{12,24},{16,4},{20,0},{24,12},{28,8},{1,21},{... | collective-permute-start | bytes 196616 | tf_op jit(solution)/shard_map/ppermute | solution.py:16
  57.2 5.8 %collective-permute-start.18 = (bf16[2,64,256]{2,1,0:T(8,128)(2,1)S(1)}, bf16[2,64,256]{2,1,0:T(8,128)(2,1)S(1)}, u32[]{:S(2)}, u32[]{:S(2)}) collective-permute-start(bf16[2,64,256]{2,1,0:T(8,128)(2,1)S(1)} %get-tuple-element.20), channel_id=1, source_target_pairs={{0,20},{4,16},{8,28},{12,24},{16,4},{20,0},{24,12},{28,8},{1,21},{... | collective-permute-start | bytes 196616 | tf_op jit(solution)/shard_map/ppermute | solution.py:16
  58.7 6.0 %collective-permute-start.17 = (bf16[2,64,256]{2,1,0:T(8,128)(2,1)S(1)}, bf16[2,64,256]{2,1,0:T(8,128)(2,1)S(1)}, u32[]{:S(2)}, u32[]{:S(2)}) collective-permute-start(bf16[2,64,256]{2,1,0:T(8,128)(2,1)S(1)} %get-tuple-element.19), channel_id=1, source_target_pairs={{0,16},{4,20},{8,24},{12,28},{16,0},{20,4},{24,8},{28,12},{1,17},{... | collective-permute-start | bytes 196616 | tf_op jit(solution)/shard_map/ppermute | solution.py:16
  61.2 6.3 %collective-permute-start.15 = (bf16[2,64,256]{2,1,0:T(8,128)(2,1)S(1)}, bf16[2,64,256]{2,1,0:T(8,128)(2,1)S(1)}, u32[]{:S(2)}, u32[]{:S(2)}) collective-permute-start(bf16[2,64,256]{2,1,0:T(8,128)(2,1)S(1)} %get-tuple-element.17), channel_id=1, source_target_pairs={{0,8},{4,12},{8,0},{12,4},{16,24},{20,28},{24,16},{28,20},{1,9},{5... | collective-permute-start | bytes 196616 | tf_op jit(solution)/shard_map/ppermute | solution.py:16
  63.0 18.7 %collective-permute-start.13 = (bf16[2,128,256]{2,1,0:T(8,128)(2,1)S(1)}, bf16[2,128,256]{2,1,0:T(8,128)(2,1)S(1)}, u32[]{:S(2)}, u32[]{:S(2)}) collective-permute-start(bf16[2,128,256]{2,1,0:T(8,128)(2,1)S(1)} %get-tuple-element.15), channel_id=1, source_target_pairs={{0,3},{1,2},{2,1},{3,0},{4,7},{5,6},{6,5},{7,4},{8,11},{9,10},{10,... | collective-permute-start | bytes 393224 | tf_op jit(solution)/shard_map/ppermute | solution.py:16
  64.8 17.9 %collective-permute-start.12 = (bf16[2,128,256]{2,1,0:T(8,128)(2,1)S(1)}, bf16[2,128,256]{2,1,0:T(8,128)(2,1)S(1)}, u32[]{:S(2)}, u32[]{:S(2)}) collective-permute-start(bf16[2,128,256]{2,1,0:T(8,128)(2,1)S(1)} %get-tuple-element.14), channel_id=1, source_target_pairs={{0,2},{1,3},{2,0},{3,1},{4,6},{5,7},{6,4},{7,5},{8,10},{9,11},{10,... | collective-permute-start | bytes 393224 | tf_op jit(solution)/shard_map/ppermute | solution.py:16
  64.8 18.6 %collective-permute-start.11 = (bf16[2,128,256]{2,1,0:T(8,128)(2,1)S(1)}, bf16[2,128,256]{2,1,0:T(8,128)(2,1)S(1)}, u32[]{:S(2)}, u32[]{:S(2)}) collective-permute-start(bf16[2,128,256]{2,1,0:T(8,128)(2,1)S(1)} %get-tuple-element.13), channel_id=1, source_target_pairs={{0,1},{1,0},{2,3},{3,2},{4,5},{5,4},{6,7},{7,6},{8,9},{9,8},{10,11... | collective-permute-start | bytes 393224 | tf_op jit(solution)/shard_map/ppermute | solution.py:16
  67.5 12.6 %collective-permute-start.22 = (bf16[2,64,256]{2,1,0:T(8,128)(2,1)S(1)}, bf16[2,64,256]{2,1,0:T(8,128)(2,1)S(1)}, u32[]{:S(2)}, u32[]{:S(2)}) collective-permute-start(bf16[2,64,256]{2,1,0:T(8,128)(2,1)S(1)} %fusion.135), channel_id=1, source_target_pairs={{0,3},{1,0},{2,1},{3,2},{4,7},{5,4},{6,5},{7,6},{8,11},{9,8},{10,9... | collective-permute-start | bytes 196616 | tf_op jit(solution)/shard_map/ppermute | solution.py:21
  69.3 10.4 %collective-permute-start.21 = (bf16[2,64,256]{2,1,0:T(8,128)(2,1)S(1)}, bf16[2,64,256]{2,1,0:T(8,128)(2,1)S(1)}, u32[]{:S(2)}, u32[]{:S(2)}) collective-permute-start(bf16[2,64,256]{2,1,0:T(8,128)(2,1)S(1)} %fusion.135), channel_id=1, source_target_pairs={{0,1},{1,2},{2,3},{3,0},{4,5},{5,6},{6,7},{7,4},{8,9},{9,10},{10,1... | collective-permute-start | bytes 196616 | tf_op jit(solution)/shard_map/ppermute | solution.py:21
  81.7 5.7 %collective-permute-start.25 = (bf16[2,64,256]{2,1,0:T(8,128)(2,1)S(1)}, bf16[2,64,256]{2,1,0:T(8,128)(2,1)S(1)}, u32[]{:S(2)}, u32[]{:S(2)}) collective-permute-start(bf16[2,64,256]{2,1,0:T(8,128)(2,1)S(1)} %pad_maximum_fusion.5), channel_id=1, source_target_pairs={{0,12},{4,8},{8,4},{12,0},{16,28},{20,24},{24,20},{28,16},{1,13},{... | collective-permute-start | bytes 196616 | tf_op jit(solution)/shard_map/ppermute | solution.py:16
  84.5 7.5 %collective-permute-start.28 = (bf16[2,64,256]{2,1,0:T(8,128)(2,1)S(1)}, bf16[2,64,256]{2,1,0:T(8,128)(2,1)S(1)}, u32[]{:S(2)}, u32[]{:S(2)}) collective-permute-start(bf16[2,64,256]{2,1,0:T(8,128)(2,1)S(1)} %pad_maximum_fusion.5), channel_id=1, source_target_pairs={{0,24},{4,28},{8,16},{12,20},{16,8},{20,12},{24,0},{28,4},{1,25},{... | collective-permute-start | bytes 196616 | tf_op jit(solution)/shard_map/ppermute | solution.py:16
  85.8 6.2 %collective-permute-start.29 = (bf16[2,64,256]{2,1,0:T(8,128)(2,1)S(1)}, bf16[2,64,256]{2,1,0:T(8,128)(2,1)S(1)}, u32[]{:S(2)}, u32[]{:S(2)}) collective-permute-start(bf16[2,64,256]{2,1,0:T(8,128)(2,1)S(1)} %pad_maximum_fusion.5), channel_id=1, source_target_pairs={{0,28},{4,24},{8,20},{12,16},{16,12},{20,8},{24,4},{28,0},{1,29},{... | collective-permute-start | bytes 196616 | tf_op jit(solution)/shard_map/ppermute | solution.py:16
  87.4 8.3 %collective-permute-start.32 = (bf16[2,128,256]{2,1,0:T(8,128)(2,1)S(1)}, bf16[2,128,256]{2,1,0:T(8,128)(2,1)S(1)}, u32[]{:S(2)}, u32[]{:S(2)}) collective-permute-start(bf16[2,128,256]{2,1,0:T(8,128)(2,1)S(1)} %fusion.42), channel_id=1, source_target_pairs={{0,3},{1,2},{2,1},{3,0},{4,7},{5,6},{6,5},{7,4},{8,11},{9,10},{10,... | collective-permute-start | bytes 393224 | tf_op jit(solution)/shard_map/ppermute | solution.py:16
  87.6 12.4 %collective-permute-start.31 = (bf16[2,128,256]{2,1,0:T(8,128)(2,1)S(1)}, bf16[2,128,256]{2,1,0:T(8,128)(2,1)S(1)}, u32[]{:S(2)}, u32[]{:S(2)}) collective-permute-start(bf16[2,128,256]{2,1,0:T(8,128)(2,1)S(1)} %fusion.42), channel_id=1, source_target_pairs={{0,2},{1,3},{2,0},{3,1},{4,6},{5,7},{6,4},{7,5},{8,10},{9,11},{10,... | collective-permute-start | bytes 393224 | tf_op jit(solution)/shard_map/ppermute | solution.py:16
  87.9 12.1 %collective-permute-start.30 = (bf16[2,128,256]{2,1,0:T(8,128)(2,1)S(1)}, bf16[2,128,256]{2,1,0:T(8,128)(2,1)S(1)}, u32[]{:S(2)}, u32[]{:S(2)}) collective-permute-start(bf16[2,128,256]{2,1,0:T(8,128)(2,1)S(1)} %fusion.42), channel_id=1, source_target_pairs={{0,1},{1,0},{2,3},{3,2},{4,5},{5,4},{6,7},{7,6},{8,9},{9,8},{10,11... | collective-permute-start | bytes 393224 | tf_op jit(solution)/shard_map/ppermute | solution.py:16
  103.7 6.0 %collective-permute-start.41 = (bf16[2,64,256]{2,1,0:T(8,128)(2,1)S(1)}, bf16[2,64,256]{2,1,0:T(8,128)(2,1)S(1)}, u32[]{:S(2)}, u32[]{:S(2)}) collective-permute-start(bf16[2,64,256]{2,1,0:T(8,128)(2,1)S(1)} %get-tuple-element.9), channel_id=1, source_target_pairs={{0,24},{4,28},{8,16},{12,20},{16,8},{20,12},{24,0},{28,4},{1,25},{... | collective-permute-start | bytes 196616 | tf_op jit(solution)/shard_map/ppermute | solution.py:16
  113.1 7.0 %collective-permute-start.43 = (bf16[2,64,256]{2,1,0:T(8,128)(2,1)S(1)}, bf16[2,64,256]{2,1,0:T(8,128)(2,1)S(1)}, u32[]{:S(2)}, u32[]{:S(2)}) collective-permute-start(bf16[2,64,256]{2,1,0:T(8,128)(2,1)S(1)} %fusion.136), channel_id=1, source_target_pairs={{0,1},{1,2},{2,3},{3,0},{4,5},{5,6},{6,7},{7,4},{8,9},{9,10},{10,1... | collective-permute-start | bytes 196616 | tf_op jit(solution)/shard_map/ppermute | solution.py:21
  113.2 9.6 %collective-permute-start.35 = (bf16[2,128,256]{2,1,0:T(8,128)(2,1)S(1)}, bf16[2,128,256]{2,1,0:T(8,128)(2,1)S(1)}, u32[]{:S(2)}, u32[]{:S(2)}) collective-permute-start(bf16[2,128,256]{2,1,0:T(8,128)(2,1)S(1)} %get-tuple-element.12), channel_id=1, source_target_pairs={{0,3},{1,2},{2,1},{3,0},{4,7},{5,6},{6,5},{7,4},{8,11},{9,10},{10,... | collective-permute-start | bytes 393224 | tf_op jit(solution)/shard_map/ppermute | solution.py:16
  117.1 12.7 %collective-permute-start.34 = (bf16[2,128,256]{2,1,0:T(8,128)(2,1)S(1)}, bf16[2,128,256]{2,1,0:T(8,128)(2,1)S(1)}, u32[]{:S(2)}, u32[]{:S(2)}) collective-permute-start(bf16[2,128,256]{2,1,0:T(8,128)(2,1)S(1)} %get-tuple-element.11), channel_id=1, source_target_pairs={{0,2},{1,3},{2,0},{3,1},{4,6},{5,7},{6,4},{7,5},{8,10},{9,11},{10,... | collective-permute-start | bytes 393224 | tf_op jit(solution)/shard_map/ppermute | solution.py:16
  117.1 12.7 %collective-permute-start.33 = (bf16[2,128,256]{2,1,0:T(8,128)(2,1)S(1)}, bf16[2,128,256]{2,1,0:T(8,128)(2,1)S(1)}, u32[]{:S(2)}, u32[]{:S(2)}) collective-permute-start(bf16[2,128,256]{2,1,0:T(8,128)(2,1)S(1)} %get-tuple-element.10), channel_id=1, source_target_pairs={{0,1},{1,0},{2,3},{3,2},{4,5},{5,4},{6,7},{7,6},{8,9},{9,8},{10,11... | collective-permute-start | bytes 393224 | tf_op jit(solution)/shard_map/ppermute | solution.py:16
  (25 other events, 142.3 us)

commit v2 on v1

--- a/solution.py
+++ b/solution.py
@@ -21,27 +21,57 @@
     return lax.ppermute(shard, axis, [(i, (i + by) % size) for i in range(size)])
 
 
-def in_order(parts, me, axis):
-    stacked = jnp.stack(parts)
-    order = jnp.bitwise_xor(lax.iota(jnp.int32, len(parts)), me)
-    out = [lax.dynamic_index_in_dim(stacked, order[i], 0, False) for i in range(len(parts))]
-    return jnp.concatenate(out, axis=1)
+def placed(parts, me):
+    width = parts[0].shape[1]
+    whole = jnp.zeros(
+        (parts[0].shape[0], width * len(parts)) + parts[0].shape[2:], parts[0].dtype
+    )
+    for d, part in enumerate(parts):
+        whole = lax.dynamic_update_slice_in_dim(whole, part, (me ^ d) * width, 1)
+    return whole
 
 
-def gathered(shard, axis):
-    size = lax.axis_size(axis)
-    parts = [shard] + [exchanged(shard, axis, d) for d in range(1, size)]
-    return in_order(parts, lax.axis_index(axis), axis)
+def gathered_left(shard):
+    size = lax.axis_size("col")
+    parts = [shard] + [exchanged(shard, "col", d) for d in range(1, size)]
+    return placed(parts, lax.axis_index("col"))
 
 
-def scattered_sum(whole, axis):
-    size = lax.axis_size(axis)
-    me = lax.axis_index(axis)
+def gathered_right(shard):
+    size = lax.axis_size("row")
+    me = lax.axis_index("row")
+    same = shard[:, None]
+    parts = [same] + [exchanged(same, "row", d) for d in range(2, size, 2)]
+    half = placed(parts, me >> 1)
+    other = exchanged(half, "row", 1)
+    whole = jnp.zeros((half.shape[0], half.shape[1], 2) + half.shape[2:], half.dtype)
+    whole = lax.dynamic_update_slice_in_dim(whole, half[:, :, None], me & 1, 2)
+    whole = lax.dynamic_update_slice_in_dim(whole, other[:, :, None], (me & 1) ^ 1, 2)
+    return whole.reshape(half.shape[0], -1, half.shape[3])
+
+
+def scattered_left(whole):
+    size = lax.axis_size("col")
+    me = lax.axis_index("col")
     width = whole.shape[1] // size
     total = lax.dynamic_slice_in_dim(whole, me * width, width, 1)
     for d in range(1, size):
         part = lax.dynamic_slice_in_dim(whole, (me ^ d) * width, width, 1).astype(BF)
-        total = total + exchanged(part, axis, d).astype(F32)
+        total = total + exchanged(part, "col", d).astype(F32)
+    return total
+
+
+def scattered_right(whole):
+    size = lax.axis_size("row")
+    me = lax.axis_index("row")
+    cut = whole.reshape(whole.shape[0], size // 2, 2, -1, whole.shape[2])
+    mine = lax.dynamic_index_in_dim(cut, me & 1, 2, False)
+    theirs = lax.dynamic_index_in_dim(cut, (me & 1) ^ 1, 2, False).astype(BF)
+    pair = mine + exchanged(theirs, "row", 1).astype(F32)
+    total = lax.dynamic_index_in_dim(pair, me >> 1, 1, False)
+    for d in range(2, size, 2):
+        part = lax.dynamic_index_in_dim(pair, (me ^ d) >> 1, 1, False).astype(BF)
+        total = total + exchanged(part, "row", d).astype(F32)
     return total
 
 
@@ -99,8 +129,8 @@
     right_next = passed_along(right, "col", -1)
     for step in range(ITERS):
         mixed_shard = mixed(right, right_next)
-        q = gathered(mixed_shard, "row")
-        lw = gathered(left, "col")
+        q = gathered_right(mixed_shard)
+        lw = gathered_left(left)
         br = mult("kr,kc->rc", lw[0], q[0]) + mult("kr,kc->rc", lw[1], q[1]) - rec[0]
         bi = mult("kr,kc->rc", lw[1], q[0]) - mult("kr,kc->rc", lw[0], q[1]) - rec[1]
         br, bi = br.astype(BF), bi.astype(BF)
@@ -108,9 +138,9 @@
         wi = mult("kr,rc->kc", lw[1], br) - mult("kr,rc->kc", lw[0], bi)
         glr = mult("kc,rc->kr", q[0], br) - mult("kc,rc->kr", q[1], bi)
         gli = mult("kc,rc->kr", q[1], br) + mult("kc,rc->kr", q[0], bi)
-        w_own = scattered_sum(jnp.stack([wr, wi]), "row").astype(BF)
+        w_own = scattered_right(jnp.stack([wr, wi])).astype(BF)
         w_prev = passed_along(w_own, "col", 1)
-        left = (left.astype(F32) - eta_left * scattered_sum(jnp.stack([glr, gli]), "col")).astype(BF)
+        left = (left.astype(F32) - eta_left * scattered_left(jnp.stack([glr, gli]))).astype(BF)
         if step + 1 < ITERS:
             w_next = passed_along(w_own, "col", -1)
             grad_next = folded(w_own, w_next, pick_own, pick_next, cos_next, sin_next)

time: 131 us -> 113 us (0.86)
  between operations: 24.2 us -> 1.44 us
  other arithmetic: 2.74 us -> 5.36 us
    ppermute x40 -> x28, waiting for transfers between devices: 30.9 us -> 35.9 us  [exchanged(): return lax.ppermute(shard, axis, [(i, i ^ flip) for i in range(size)])]
    ppermute x4, waiting for transfers between devices: 12.2 us -> 7.98 us  [passed_along(): lax.ppermute(shard, axis, [(i, (i + by) % size) for i in range(size)])]
    ppermute x4, starting transfers between devices: 5.88 us -> 9.72 us  [passed_along(): lax.ppermute(shard, axis, [(i, (i + by) % size) for i in range(size)])]
    ppermute x40 -> x28, starting transfers between devices: 44.2 us -> 40.9 us  [exchanged(): return lax.ppermute(shard, axis, [(i, i ^ flip) for i in range(size)])]
    unnamed x36 -> x24, local copies, waits for them, and re-layouts: 1.09 us -> 2.62 us
  transfers between devices with their start and end apart: 44 -> 32, of which waited for: 17 -> 18; matrix products, arithmetic and copies ran while one was open for 5% -> 7% of each run, Pallas kernels for 0% -> 0%
where the time goes in v2:
time: 113 us
  starting transfers between devices  50.7 us (45%)
  waiting for transfers between devices  43.9 us (39%)
  matrix products  7.92 us (7%)
  other arithmetic  5.36 us (5%)
  local copies, waits for them, and re-layouts  3.23 us (3%)
  between operations  1.44 us (1%)
    ppermute x28, starting transfers between devices, exchanged(): return lax.ppermute(shard, axis, [(i, i ^ flip) for i in range(size)])  40.9 us
    ppermute x28, waiting for transfers between devices, exchanged(): return lax.ppermute(shard, axis, [(i, i ^ flip) for i in range(size)])  35.9 us
    ppermute x4, starting transfers between devices, passed_along(): lax.ppermute(shard, axis, [(i, (i + by) % size) for i in range(size)])  9.72 us
    ppermute x4, waiting for transfers between devices, passed_along(): lax.ppermute(shard, axis, [(i, (i + by) % size) for i in range(size)])  7.98 us
    dot_general x33, matrix products, mult(): return jnp.einsum(spec, a, b, preferred_element_type=F32)  7.92 us
    unnamed x24, local copies, waits for them, and re-layouts  2.62 us
  transfers between devices with their start and end apart: 32, of which 18 were waited for; matrix products, arithmetic and copies ran while one was open for 7% of the time, Pallas kernels for 0%

profile of v2, /device:TPU:0, one launch (start us, length us, event | category | flops | bytes accessed | tf_op | source)
XLA Modules:
  0.0 112.5 jit_solution(8062745127810632164)
XLA Ops:
  0.6 3.1 %collective-permute-start.5 = (bf16[2,128,256]{2,1,0:T(8,128)(2,1)}, bf16[2,128,256]{2,1,0:T(8,128)(2,1)S(1)}, u32[]{:S(2)}, u32[]{:S(2)}) collective-permute-start(bf16[2,128,256]{2,1,0:T(8,128)(2,1)} %param.5), channel_id=1, source_target_pairs={{0,1},{1,0},{2,3},{3,2},{4,5},{5,4},{6,7},{7,6},{8,9},{9,8},{10,11... | collective-permute-start | bytes 393224 | tf_op jit(solution)/shard_map/ppermute | solution.py:16
  3.7 2.5 %collective-permute-start.7 = (bf16[2,128,256]{2,1,0:T(8,128)(2,1)}, bf16[2,128,256]{2,1,0:T(8,128)(2,1)S(1)}, u32[]{:S(2)}, u32[]{:S(2)}) collective-permute-start(bf16[2,128,256]{2,1,0:T(8,128)(2,1)} %param.5), channel_id=1, source_target_pairs={{0,3},{1,2},{2,1},{3,0},{4,7},{5,6},{6,5},{7,4},{8,11},{9,10},{10,... | collective-permute-start | bytes 393224 | tf_op jit(solution)/shard_map/ppermute | solution.py:16
  6.3 2.9 %collective-permute-start = (bf16[2,64,256]{2,1,0:T(8,128)(2,1)}, bf16[2,64,256]{2,1,0:T(8,128)(2,1)S(1)}, u32[]{:S(2)}, u32[]{:S(2)}) collective-permute-start(bf16[2,64,256]{2,1,0:T(8,128)(2,1)} %param.6), channel_id=1, source_target_pairs={{0,3},{1,0},{2,1},{3,2},{4,7},{5,4},{6,5},{7,6},{8,11},{9,8},{10,9... | collective-permute-start | bytes 196616 | tf_op jit(solution)/shard_map/ppermute | solution.py:21
  11.7 2.1 %collective-permute-done = bf16[2,64,256]{2,1,0:T(8,128)(2,1)S(1)} collective-permute-done((bf16[2,64,256]{2,1,0:T(8,128)(2,1)}, bf16[2,64,256]{2,1,0:T(8,128)(2,1)S(1)}, u32[]{:S(2)}, u32[]{:S(2)}) %collective-permute-start) | collective-permute-done | bytes 65568 | tf_op jit(solution)/shard_map/ppermute | solution.py:21
  15.9 1.6 %collective-permute-start.2 = (bf16[2,1,64,256]{3,2,1,0:T(8,128)(2,1)S(1)}, bf16[2,1,64,256]{3,2,1,0:T(8,128)(2,1)S(1)}, u32[]{:S(2)}, u32[]{:S(2)}) collective-permute-start(bf16[2,1,64,256]{3,2,1,0:T(8,128)(2,1)S(1)} %get-tuple-element.34), channel_id=1, source_target_pairs={{0,16},{4,20},{8,24},{12,28},{16,0},{20,4},{24,8},{28,12},{1,17},{... | collective-permute-start | bytes 196616 | tf_op jit(solution)/shard_map/ppermute | solution.py:16
  18.6 2.4 %collective-permute-start.3 = (bf16[2,1,64,256]{3,2,1,0:T(8,128)(2,1)S(1)}, bf16[2,1,64,256]{3,2,1,0:T(8,128)(2,1)S(1)}, u32[]{:S(2)}, u32[]{:S(2)}) collective-permute-start(bf16[2,1,64,256]{3,2,1,0:T(8,128)(2,1)S(1)} %get-tuple-element.34), channel_id=1, source_target_pairs={{0,24},{4,28},{8,16},{12,20},{16,8},{20,12},{24,0},{28,4},{1,25},{... | collective-permute-start | bytes 196616 | tf_op jit(solution)/shard_map/ppermute | solution.py:16
  21.0 2.7 %collective-permute-done.3 = bf16[2,1,64,256]{3,2,1,0:T(8,128)(2,1)S(1)} collective-permute-done((bf16[2,1,64,256]{3,2,1,0:T(8,128)(2,1)S(1)}, bf16[2,1,64,256]{3,2,1,0:T(8,128)(2,1)S(1)}, u32[]{:S(2)}, u32[]{:S(2)}) %collective-permute-start.3) | collective-permute-done | bytes 65568 | tf_op jit(solution)/shard_map/ppermute | solution.py:16
  29.5 6.3 %collective-permute-start.8 = (bf16[2,128,256]{2,1,0:T(8,128)(2,1)}, bf16[2,128,256]{2,1,0:T(8,128)(2,1)}, u32[]{:S(2)}, u32[]{:S(2)}) collective-permute-start(bf16[2,128,256]{2,1,0:T(8,128)(2,1)} %get-tuple-element.9), channel_id=1, source_target_pairs={{0,1},{1,0},{2,3},{3,2},{4,5},{5,4},{6,7},{7,6},{8,9},{9,8},{10,11... | collective-permute-start | bytes 393224 | tf_op jit(solution)/shard_map/ppermute | solution.py:16
  35.8 2.4 %collective-permute-start.10 = (bf16[2,128,256]{2,1,0:T(8,128)(2,1)}, bf16[2,128,256]{2,1,0:T(8,128)(2,1)}, u32[]{:S(2)}, u32[]{:S(2)}) collective-permute-start(bf16[2,128,256]{2,1,0:T(8,128)(2,1)} %get-tuple-element.11), channel_id=1, source_target_pairs={{0,3},{1,2},{2,1},{3,0},{4,7},{5,6},{6,5},{7,4},{8,11},{9,10},{10,... | collective-permute-start | bytes 393224 | tf_op jit(solution)/shard_map/ppermute | solution.py:16
  38.3 2.5 %collective-permute-done.8 = bf16[2,128,256]{2,1,0:T(8,128)(2,1)} collective-permute-done((bf16[2,128,256]{2,1,0:T(8,128)(2,1)}, bf16[2,128,256]{2,1,0:T(8,128)(2,1)}, u32[]{:S(2)}, u32[]{:S(2)}) %collective-permute-start.8) | collective-permute-done | bytes 131104 | tf_op jit(solution)/shard_map/ppermute | solution.py:16
  40.7 7.9 %collective-permute-done.9 = bf16[2,128,256]{2,1,0:T(8,128)(2,1)} collective-permute-done((bf16[2,128,256]{2,1,0:T(8,128)(2,1)}, bf16[2,128,256]{2,1,0:T(8,128)(2,1)}, u32[]{:S(2)}, u32[]{:S(2)}) %collective-permute-start.9) | collective-permute-done | bytes 131104 | tf_op jit(solution)/shard_map/ppermute | solution.py:16
  49.8 2.1 %collective-permute-start.22 = (bf16[2,128,256]{2,1,0:T(8,128)(2,1)S(1)}, bf16[2,128,256]{2,1,0:T(8,128)(2,1)S(1)}, u32[]{:S(2)}, u32[]{:S(2)}) collective-permute-start(bf16[2,128,256]{2,1,0:T(8,128)(2,1)S(1)} %get-tuple-element.3), channel_id=1, source_target_pairs={{0,2},{1,3},{2,0},{3,1},{4,6},{5,7},{6,4},{7,5},{8,10},{9,11},{10,... | collective-permute-start | bytes 393224 | tf_op jit(solution)/shard_map/ppermute | solution.py:16
  52.8 2.3 %collective-permute-start.23 = (bf16[2,128,256]{2,1,0:T(8,128)(2,1)S(1)}, bf16[2,128,256]{2,1,0:T(8,128)(2,1)S(1)}, u32[]{:S(2)}, u32[]{:S(2)}) collective-permute-start(bf16[2,128,256]{2,1,0:T(8,128)(2,1)S(1)} %get-tuple-element.3), channel_id=1, source_target_pairs={{0,3},{1,2},{2,1},{3,0},{4,7},{5,6},{6,5},{7,4},{8,11},{9,10},{10,... | collective-permute-start | bytes 393224 | tf_op jit(solution)/shard_map/ppermute | solution.py:16
  55.2 1.6 %collective-permute-start.12 = (bf16[2,64,256]{2,1,0:T(8,128)(2,1)S(1)}, bf16[2,64,256]{2,1,0:T(8,128)(2,1)S(1)}, u32[]{:S(2)}, u32[]{:S(2)}) collective-permute-start(bf16[2,64,256]{2,1,0:T(8,128)(2,1)S(1)} %get-tuple-element.17), channel_id=1, source_target_pairs={{0,8},{4,12},{8,0},{12,4},{16,24},{20,28},{24,16},{28,20},{1,9},{5... | collective-permute-start | bytes 196616 | tf_op jit(solution)/shard_map/ppermute | solution.py:16
  60.0 1.9 %collective-permute-done.14 = bf16[2,64,256]{2,1,0:T(8,128)(2,1)S(1)} collective-permute-done((bf16[2,64,256]{2,1,0:T(8,128)(2,1)S(1)}, bf16[2,64,256]{2,1,0:T(8,128)(2,1)S(1)}, u32[]{:S(2)}, u32[]{:S(2)}) %collective-permute-start.14) | collective-permute-done | bytes 65568 | tf_op jit(solution)/shard_map/ppermute | solution.py:16
  62.8 6.7 %collective-permute-start.16 = (bf16[2,64,256]{2,1,0:T(8,128)(2,1)S(1)}, bf16[2,64,256]{2,1,0:T(8,128)(2,1)S(1)}, u32[]{:S(2)}, u32[]{:S(2)}) collective-permute-start(bf16[2,64,256]{2,1,0:T(8,128)(2,1)S(1)} %fusion.96), channel_id=1, source_target_pairs={{0,3},{1,0},{2,1},{3,2},{4,7},{5,4},{6,5},{7,6},{8,11},{9,8},{10,9... | collective-permute-start | bytes 196616 | tf_op jit(solution)/shard_map/ppermute | solution.py:21
  69.8 5.8 %collective-permute-done.15 = bf16[2,64,256]{2,1,0:T(8,128)(2,1)S(1)} collective-permute-done((bf16[2,64,256]{2,1,0:T(8,128)(2,1)S(1)}, bf16[2,64,256]{2,1,0:T(8,128)(2,1)S(1)}, u32[]{:S(2)}, u32[]{:S(2)}) %collective-permute-start.15) | collective-permute-done | bytes 65568 | tf_op jit(solution)/shard_map/ppermute | solution.py:21
  78.7 1.6 %collective-permute-start.17 = (bf16[2,1,64,256]{3,2,1,0:T(8,128)(2,1)S(1)}, bf16[2,1,64,256]{3,2,1,0:T(8,128)(2,1)S(1)}, u32[]{:S(2)}, u32[]{:S(2)}) collective-permute-start(bf16[2,1,64,256]{3,2,1,0:T(8,128)(2,1)S(1)} %get-tuple-element.32), channel_id=1, source_target_pairs={{0,8},{4,12},{8,0},{12,4},{16,24},{20,28},{24,16},{28,20},{1,9},{5... | collective-permute-start | bytes 196616 | tf_op jit(solution)/shard_map/ppermute | solution.py:16
  80.3 1.6 %collective-permute-start.18 = (bf16[2,1,64,256]{3,2,1,0:T(8,128)(2,1)S(1)}, bf16[2,1,64,256]{3,2,1,0:T(8,128)(2,1)S(1)}, u32[]{:S(2)}, u32[]{:S(2)}) collective-permute-start(bf16[2,1,64,256]{3,2,1,0:T(8,128)(2,1)S(1)} %get-tuple-element.32), channel_id=1, source_target_pairs={{0,16},{4,20},{8,24},{12,28},{16,0},{20,4},{24,8},{28,12},{1,17},{... | collective-permute-start | bytes 196616 | tf_op jit(solution)/shard_map/ppermute | solution.py:16
  83.0 1.6 %collective-permute-done.18 = bf16[2,1,64,256]{3,2,1,0:T(8,128)(2,1)S(1)} collective-permute-done((bf16[2,1,64,256]{3,2,1,0:T(8,128)(2,1)S(1)}, bf16[2,1,64,256]{3,2,1,0:T(8,128)(2,1)S(1)}, u32[]{:S(2)}, u32[]{:S(2)}) %collective-permute-start.18) | collective-permute-done | bytes 65568 | tf_op jit(solution)/shard_map/ppermute | solution.py:16
  84.6 2.4 %collective-permute-done.19 = bf16[2,1,64,256]{3,2,1,0:T(8,128)(2,1)S(1)} collective-permute-done((bf16[2,1,64,256]{3,2,1,0:T(8,128)(2,1)S(1)}, bf16[2,1,64,256]{3,2,1,0:T(8,128)(2,1)S(1)}, u32[]{:S(2)}, u32[]{:S(2)}) %collective-permute-start.19) | collective-permute-done | bytes 65568 | tf_op jit(solution)/shard_map/ppermute | solution.py:16
  97.9 3.2 %collective-permute-start.26 = (bf16[2,128,256]{2,1,0:T(8,128)(2,1)S(1)}, bf16[2,128,256]{2,1,0:T(8,128)(2,1)S(1)}, u32[]{:S(2)}, u32[]{:S(2)}) collective-permute-start(bf16[2,128,256]{2,1,0:T(8,128)(2,1)S(1)} %get-tuple-element.8), channel_id=1, source_target_pairs={{0,3},{1,2},{2,1},{3,0},{4,7},{5,6},{6,5},{7,4},{8,11},{9,10},{10,... | collective-permute-start | bytes 393224 | tf_op jit(solution)/shard_map/ppermute | solution.py:16
  101.2 2.3 %collective-permute-done.24 = bf16[2,128,256]{2,1,0:T(8,128)(2,1)S(1)} collective-permute-done((bf16[2,128,256]{2,1,0:T(8,128)(2,1)S(1)}, bf16[2,128,256]{2,1,0:T(8,128)(2,1)S(1)}, u32[]{:S(2)}, u32[]{:S(2)}) %collective-permute-start.24) | collective-permute-done | bytes 131104 | tf_op jit(solution)/shard_map/ppermute | solution.py:16
  103.5 7.2 %collective-permute-done.25 = bf16[2,128,256]{2,1,0:T(8,128)(2,1)S(1)} collective-permute-done((bf16[2,128,256]{2,1,0:T(8,128)(2,1)S(1)}, bf16[2,128,256]{2,1,0:T(8,128)(2,1)S(1)}, u32[]{:S(2)}, u32[]{:S(2)}) %collective-permute-start.25) | collective-permute-done | bytes 131104 | tf_op jit(solution)/shard_map/ppermute | solution.py:16
  (152 shorter events, 34.6 us)
Async XLA Ops:
  0.6 23.2 %collective-permute-start.5 = (bf16[2,128,256]{2,1,0:T(8,128)(2,1)}, bf16[2,128,256]{2,1,0:T(8,128)(2,1)S(1)}, u32[]{:S(2)}, u32[]{:S(2)}) collective-permute-start(bf16[2,128,256]{2,1,0:T(8,128)(2,1)} %param.5), channel_id=1, source_target_pairs={{0,1},{1,0},{2,3},{3,2},{4,5},{5,4},{6,7},{7,6},{8,9},{9,8},{10,11... | collective-permute-start | bytes 393224 | tf_op jit(solution)/shard_map/ppermute | solution.py:16
  3.7 20.2 %collective-permute-start.7 = (bf16[2,128,256]{2,1,0:T(8,128)(2,1)}, bf16[2,128,256]{2,1,0:T(8,128)(2,1)S(1)}, u32[]{:S(2)}, u32[]{:S(2)}) collective-permute-start(bf16[2,128,256]{2,1,0:T(8,128)(2,1)} %param.5), channel_id=1, source_target_pairs={{0,3},{1,2},{2,1},{3,0},{4,7},{5,6},{6,5},{7,4},{8,11},{9,10},{10,... | collective-permute-start | bytes 393224 | tf_op jit(solution)/shard_map/ppermute | solution.py:16
  6.2 17.6 %collective-permute-start.6 = (bf16[2,128,256]{2,1,0:T(8,128)(2,1)}, bf16[2,128,256]{2,1,0:T(8,128)(2,1)S(1)}, u32[]{:S(2)}, u32[]{:S(2)}) collective-permute-start(bf16[2,128,256]{2,1,0:T(8,128)(2,1)} %param.5), channel_id=1, source_target_pairs={{0,2},{1,3},{2,0},{3,1},{4,6},{5,7},{6,4},{7,5},{8,10},{9,11},{10,... | collective-permute-start | bytes 393224 | tf_op jit(solution)/shard_map/ppermute | solution.py:16
  6.3 7.5 %collective-permute-start = (bf16[2,64,256]{2,1,0:T(8,128)(2,1)}, bf16[2,64,256]{2,1,0:T(8,128)(2,1)S(1)}, u32[]{:S(2)}, u32[]{:S(2)}) collective-permute-start(bf16[2,64,256]{2,1,0:T(8,128)(2,1)} %param.6), channel_id=1, source_target_pairs={{0,3},{1,0},{2,1},{3,2},{4,7},{5,4},{6,5},{7,6},{8,11},{9,8},{10,9... | collective-permute-start | bytes 196616 | tf_op jit(solution)/shard_map/ppermute | solution.py:21
  15.9 5.2 %collective-permute-start.2 = (bf16[2,1,64,256]{3,2,1,0:T(8,128)(2,1)S(1)}, bf16[2,1,64,256]{3,2,1,0:T(8,128)(2,1)S(1)}, u32[]{:S(2)}, u32[]{:S(2)}) collective-permute-start(bf16[2,1,64,256]{3,2,1,0:T(8,128)(2,1)S(1)} %get-tuple-element.34), channel_id=1, source_target_pairs={{0,16},{4,20},{8,24},{12,28},{16,0},{20,4},{24,8},{28,12},{1,17},{... | collective-permute-start | bytes 196616 | tf_op jit(solution)/shard_map/ppermute | solution.py:16
  18.6 5.2 %collective-permute-start.3 = (bf16[2,1,64,256]{3,2,1,0:T(8,128)(2,1)S(1)}, bf16[2,1,64,256]{3,2,1,0:T(8,128)(2,1)S(1)}, u32[]{:S(2)}, u32[]{:S(2)}) collective-permute-start(bf16[2,1,64,256]{3,2,1,0:T(8,128)(2,1)S(1)} %get-tuple-element.34), channel_id=1, source_target_pairs={{0,24},{4,28},{8,16},{12,20},{16,8},{20,12},{24,0},{28,4},{1,25},{... | collective-permute-start | bytes 196616 | tf_op jit(solution)/shard_map/ppermute | solution.py:16
  28.0 27.1 %collective-permute-start.11 = (bf16[2,4,64,256]{3,2,0,1:T(8,128)(2,1)S(1)}, bf16[2,4,64,256]{3,2,0,1:T(8,128)(2,1)S(1)}, u32[]{:S(2)}, u32[]{:S(2)}) collective-permute-start(bf16[2,4,64,256]{3,2,0,1:T(8,128)(2,1)S(1)} %fusion.23), channel_id=1, source_target_pairs={{0,4},{4,0},{8,12},{12,8},{16,20},{20,16},{24,28},{28,24},{1,5},{5... | collective-permute-start | bytes 786440 | tf_op jit(solution)/shard_map/ppermute | solution.py:16
  29.5 11.2 %collective-permute-start.8 = (bf16[2,128,256]{2,1,0:T(8,128)(2,1)}, bf16[2,128,256]{2,1,0:T(8,128)(2,1)}, u32[]{:S(2)}, u32[]{:S(2)}) collective-permute-start(bf16[2,128,256]{2,1,0:T(8,128)(2,1)} %get-tuple-element.9), channel_id=1, source_target_pairs={{0,1},{1,0},{2,3},{3,2},{4,5},{5,4},{6,7},{7,6},{8,9},{9,8},{10,11... | collective-permute-start | bytes 393224 | tf_op jit(solution)/shard_map/ppermute | solution.py:16
  35.8 12.8 %collective-permute-start.9 = (bf16[2,128,256]{2,1,0:T(8,128)(2,1)}, bf16[2,128,256]{2,1,0:T(8,128)(2,1)}, u32[]{:S(2)}, u32[]{:S(2)}) collective-permute-start(bf16[2,128,256]{2,1,0:T(8,128)(2,1)} %get-tuple-element.10), channel_id=1, source_target_pairs={{0,2},{1,3},{2,0},{3,1},{4,6},{5,7},{6,4},{7,5},{8,10},{9,11},{10,... | collective-permute-start | bytes 393224 | tf_op jit(solution)/shard_map/ppermute | solution.py:16
  35.8 12.8 %collective-permute-start.10 = (bf16[2,128,256]{2,1,0:T(8,128)(2,1)}, bf16[2,128,256]{2,1,0:T(8,128)(2,1)}, u32[]{:S(2)}, u32[]{:S(2)}) collective-permute-start(bf16[2,128,256]{2,1,0:T(8,128)(2,1)} %get-tuple-element.11), channel_id=1, source_target_pairs={{0,3},{1,2},{2,1},{3,0},{4,7},{5,6},{6,5},{7,4},{8,11},{9,10},{10,... | collective-permute-start | bytes 393224 | tf_op jit(solution)/shard_map/ppermute | solution.py:16
  49.8 30.5 %collective-permute-start.22 = (bf16[2,128,256]{2,1,0:T(8,128)(2,1)S(1)}, bf16[2,128,256]{2,1,0:T(8,128)(2,1)S(1)}, u32[]{:S(2)}, u32[]{:S(2)}) collective-permute-start(bf16[2,128,256]{2,1,0:T(8,128)(2,1)S(1)} %get-tuple-element.3), channel_id=1, source_target_pairs={{0,2},{1,3},{2,0},{3,1},{4,6},{5,7},{6,4},{7,5},{8,10},{9,11},{10,... | collective-permute-start | bytes 393224 | tf_op jit(solution)/shard_map/ppermute | solution.py:16
  51.9 6.6 %collective-permute-start.21 = (bf16[2,128,256]{2,1,0:T(8,128)(2,1)S(1)}, bf16[2,128,256]{2,1,0:T(8,128)(2,1)S(1)}, u32[]{:S(2)}, u32[]{:S(2)}) collective-permute-start(bf16[2,128,256]{2,1,0:T(8,128)(2,1)S(1)} %get-tuple-element.3), channel_id=1, source_target_pairs={{0,1},{1,0},{2,3},{3,2},{4,5},{5,4},{6,7},{7,6},{8,9},{9,8},{10,11... | collective-permute-start | bytes 393224 | tf_op jit(solution)/shard_map/ppermute | solution.py:16
  52.8 34.3 %collective-permute-start.23 = (bf16[2,128,256]{2,1,0:T(8,128)(2,1)S(1)}, bf16[2,128,256]{2,1,0:T(8,128)(2,1)S(1)}, u32[]{:S(2)}, u32[]{:S(2)}) collective-permute-start(bf16[2,128,256]{2,1,0:T(8,128)(2,1)S(1)} %get-tuple-element.3), channel_id=1, source_target_pairs={{0,3},{1,2},{2,1},{3,0},{4,7},{5,6},{6,5},{7,4},{8,11},{9,10},{10,... | collective-permute-start | bytes 393224 | tf_op jit(solution)/shard_map/ppermute | solution.py:16
  56.8 5.2 %collective-permute-start.14 = (bf16[2,64,256]{2,1,0:T(8,128)(2,1)S(1)}, bf16[2,64,256]{2,1,0:T(8,128)(2,1)S(1)}, u32[]{:S(2)}, u32[]{:S(2)}) collective-permute-start(bf16[2,64,256]{2,1,0:T(8,128)(2,1)S(1)} %get-tuple-element.18), channel_id=1, source_target_pairs={{0,24},{4,28},{8,16},{12,20},{16,8},{20,12},{24,0},{28,4},{1,25},{... | collective-permute-start | bytes 196616 | tf_op jit(solution)/shard_map/ppermute | solution.py:16
  62.8 13.3 %collective-permute-start.16 = (bf16[2,64,256]{2,1,0:T(8,128)(2,1)S(1)}, bf16[2,64,256]{2,1,0:T(8,128)(2,1)S(1)}, u32[]{:S(2)}, u32[]{:S(2)}) collective-permute-start(bf16[2,64,256]{2,1,0:T(8,128)(2,1)S(1)} %fusion.96), channel_id=1, source_target_pairs={{0,3},{1,0},{2,1},{3,2},{4,7},{5,4},{6,5},{7,6},{8,11},{9,8},{10,9... | collective-permute-start | bytes 196616 | tf_op jit(solution)/shard_map/ppermute | solution.py:21
  69.5 6.1 %collective-permute-start.15 = (bf16[2,64,256]{2,1,0:T(8,128)(2,1)S(1)}, bf16[2,64,256]{2,1,0:T(8,128)(2,1)S(1)}, u32[]{:S(2)}, u32[]{:S(2)}) collective-permute-start(bf16[2,64,256]{2,1,0:T(8,128)(2,1)S(1)} %fusion.96), channel_id=1, source_target_pairs={{0,1},{1,2},{2,3},{3,0},{4,5},{5,6},{6,7},{7,4},{8,9},{9,10},{10,1... | collective-permute-start | bytes 196616 | tf_op jit(solution)/shard_map/ppermute | solution.py:21
  81.9 5.2 %collective-permute-start.19 = (bf16[2,1,64,256]{3,2,1,0:T(8,128)(2,1)S(1)}, bf16[2,1,64,256]{3,2,1,0:T(8,128)(2,1)S(1)}, u32[]{:S(2)}, u32[]{:S(2)}) collective-permute-start(bf16[2,1,64,256]{3,2,1,0:T(8,128)(2,1)S(1)} %get-tuple-element.32), channel_id=1, source_target_pairs={{0,24},{4,28},{8,16},{12,20},{16,8},{20,12},{24,0},{28,4},{1,25},{... | collective-permute-start | bytes 196616 | tf_op jit(solution)/shard_map/ppermute | solution.py:16
  93.0 4.9 %collective-permute-start.28 = (bf16[2,64,256]{2,1,0:T(8,128)(2,1)S(1)}, bf16[2,64,256]{2,1,0:T(8,128)(2,1)S(1)}, u32[]{:S(2)}, u32[]{:S(2)}) collective-permute-start(bf16[2,64,256]{2,1,0:T(8,128)(2,1)S(1)} %get-tuple-element.12), channel_id=1, source_target_pairs={{0,8},{4,12},{8,0},{12,4},{16,24},{20,28},{24,16},{28,20},{1,9},{5... | collective-permute-start | bytes 196616 | tf_op jit(solution)/shard_map/ppermute | solution.py:16
  93.6 7.5 %collective-permute-start.30 = (bf16[2,64,256]{2,1,0:T(8,128)(2,1)S(1)}, bf16[2,64,256]{2,1,0:T(8,128)(2,1)S(1)}, u32[]{:S(2)}, u32[]{:S(2)}) collective-permute-start(bf16[2,64,256]{2,1,0:T(8,128)(2,1)S(1)} %get-tuple-element.13), channel_id=1, source_target_pairs={{0,24},{4,28},{8,16},{12,20},{16,8},{20,12},{24,0},{28,4},{1,25},{... | collective-permute-start | bytes 196616 | tf_op jit(solution)/shard_map/ppermute | solution.py:16
  95.0 6.0 %collective-permute-start.29 = (bf16[2,64,256]{2,1,0:T(8,128)(2,1)S(1)}, bf16[2,64,256]{2,1,0:T(8,128)(2,1)S(1)}, u32[]{:S(2)}, u32[]{:S(2)}) collective-permute-start(bf16[2,64,256]{2,1,0:T(8,128)(2,1)S(1)} %get-tuple-element.14), channel_id=1, source_target_pairs={{0,16},{4,20},{8,24},{12,28},{16,0},{20,4},{24,8},{28,12},{1,17},{... | collective-permute-start | bytes 196616 | tf_op jit(solution)/shard_map/ppermute | solution.py:16
  96.6 6.9 %collective-permute-start.24 = (bf16[2,128,256]{2,1,0:T(8,128)(2,1)S(1)}, bf16[2,128,256]{2,1,0:T(8,128)(2,1)S(1)}, u32[]{:S(2)}, u32[]{:S(2)}) collective-permute-start(bf16[2,128,256]{2,1,0:T(8,128)(2,1)S(1)} %get-tuple-element.6), channel_id=1, source_target_pairs={{0,1},{1,0},{2,3},{3,2},{4,5},{5,4},{6,7},{7,6},{8,9},{9,8},{10,11... | collective-permute-start | bytes 393224 | tf_op jit(solution)/shard_map/ppermute | solution.py:16
  96.7 13.9 %collective-permute-start.25 = (bf16[2,128,256]{2,1,0:T(8,128)(2,1)S(1)}, bf16[2,128,256]{2,1,0:T(8,128)(2,1)S(1)}, u32[]{:S(2)}, u32[]{:S(2)}) collective-permute-start(bf16[2,128,256]{2,1,0:T(8,128)(2,1)S(1)} %get-tuple-element.7), channel_id=1, source_target_pairs={{0,2},{1,3},{2,0},{3,1},{4,6},{5,7},{6,4},{7,5},{8,10},{9,11},{10,... | collective-permute-start | bytes 393224 | tf_op jit(solution)/shard_map/ppermute | solution.py:16
  97.9 12.7 %collective-permute-start.26 = (bf16[2,128,256]{2,1,0:T(8,128)(2,1)S(1)}, bf16[2,128,256]{2,1,0:T(8,128)(2,1)S(1)}, u32[]{:S(2)}, u32[]{:S(2)}) collective-permute-start(bf16[2,128,256]{2,1,0:T(8,128)(2,1)S(1)} %get-tuple-element.8), channel_id=1, source_target_pairs={{0,3},{1,2},{2,1},{3,0},{4,7},{5,6},{6,5},{7,4},{8,11},{9,10},{10,... | collective-permute-start | bytes 393224 | tf_op jit(solution)/shard_map/ppermute | solution.py:16
  101.1 10.3 %collective-permute-start.31 = (bf16[2,64,256]{2,1,0:T(8,128)(2,1)S(1)}, bf16[2,64,256]{2,1,0:T(8,128)(2,1)S(1)}, u32[]{:S(2)}, u32[]{:S(2)}) collective-permute-start(bf16[2,64,256]{2,1,0:T(8,128)(2,1)S(1)} %fusion.93), channel_id=1, source_target_pairs={{0,1},{1,2},{2,3},{3,0},{4,5},{5,6},{6,7},{7,4},{8,9},{9,10},{10,1... | collective-permute-start | bytes 196616 | tf_op jit(solution)/shard_map/ppermute | solution.py:21
  (20 other events, 48.8 us)

commit v3 on v2

--- a/solution.py
+++ b/solution.py
@@ -31,22 +31,26 @@
     return whole
 
 
-def gathered_left(shard):
+def gathered_left(shard, small):
     size = lax.axis_size("col")
-    parts = [shard] + [exchanged(shard, "col", d) for d in range(1, size)]
-    return placed(parts, lax.axis_index("col"))
+    near = exchanged(shard, "col", 1)
+    shard, small = lax.optimization_barrier((shard, small))
+    parts = [shard, near] + [exchanged(shard, "col", d) for d in range(2, size)]
+    return placed(parts, lax.axis_index("col")), small
+
+
+def same_core():
+    size = lax.axis_size("row")
+    return [list(range(core, size, 2)) for core in range(2)]
 
 
 def gathered_right(shard):
-    size = lax.axis_size("row")
-    me = lax.axis_index("row")
-    same = shard[:, None]
-    parts = [same] + [exchanged(same, "row", d) for d in range(2, size, 2)]
-    half = placed(parts, me >> 1)
+    core = lax.axis_index("row") & 1
+    half = lax.all_gather(shard, "row", axis=1, axis_index_groups=same_core())
     other = exchanged(half, "row", 1)
     whole = jnp.zeros((half.shape[0], half.shape[1], 2) + half.shape[2:], half.dtype)
-    whole = lax.dynamic_update_slice_in_dim(whole, half[:, :, None], me & 1, 2)
-    whole = lax.dynamic_update_slice_in_dim(whole, other[:, :, None], (me & 1) ^ 1, 2)
+    whole = lax.dynamic_update_slice_in_dim(whole, half[:, :, None], core, 2)
+    whole = lax.dynamic_update_slice_in_dim(whole, other[:, :, None], core ^ 1, 2)
     return whole.reshape(half.shape[0], -1, half.shape[3])
 
 
@@ -54,25 +58,23 @@
     size = lax.axis_size("col")
     me = lax.axis_index("col")
     width = whole.shape[1] // size
-    total = lax.dynamic_slice_in_dim(whole, me * width, width, 1)
+    terms = [lax.dynamic_slice_in_dim(whole, me * width, width, 1)]
     for d in range(1, size):
         part = lax.dynamic_slice_in_dim(whole, (me ^ d) * width, width, 1).astype(BF)
-        total = total + exchanged(part, "col", d).astype(F32)
-    return total
+        terms.append(exchanged(part, "col", d))
+    return terms
 
 
 def scattered_right(whole):
     size = lax.axis_size("row")
-    me = lax.axis_index("row")
+    core = lax.axis_index("row") & 1
     cut = whole.reshape(whole.shape[0], size // 2, 2, -1, whole.shape[2])
-    mine = lax.dynamic_index_in_dim(cut, me & 1, 2, False)
-    theirs = lax.dynamic_index_in_dim(cut, (me & 1) ^ 1, 2, False).astype(BF)
+    mine = lax.dynamic_index_in_dim(cut, core, 2, False)
+    theirs = lax.dynamic_index_in_dim(cut, core ^ 1, 2, False).astype(BF)
     pair = mine + exchanged(theirs, "row", 1).astype(F32)
-    total = lax.dynamic_index_in_dim(pair, me >> 1, 1, False)
-    for d in range(2, size, 2):
-        part = lax.dynamic_index_in_dim(pair, (me ^ d) >> 1, 1, False).astype(BF)
-        total = total + exchanged(part, "row", d).astype(F32)
-    return total
+    parts = jnp.moveaxis(pair, 1, 0).astype(BF)
+    parts = lax.all_to_all(parts, "row", 0, 0, axis_index_groups=same_core())
+    return jnp.sum(parts.astype(F32), axis=0)
 
 
 def mult(spec, a, b):
@@ -127,10 +129,10 @@
     left = left_factor
     right = right_factor
     right_next = passed_along(right, "col", -1)
+    lw, right_next = gathered_left(left, right_next)
     for step in range(ITERS):
         mixed_shard = mixed(right, right_next)
         q = gathered_right(mixed_shard)
-        lw = gathered_left(left)
         br = mult("kr,kc->rc", lw[0], q[0]) + mult("kr,kc->rc", lw[1], q[1]) - rec[0]
         bi = mult("kr,kc->rc", lw[1], q[0]) - mult("kr,kc->rc", lw[0], q[1]) - rec[1]
         br, bi = br.astype(BF), bi.astype(BF)
@@ -139,13 +141,18 @@
         glr = mult("kc,rc->kr", q[0], br) - mult("kc,rc->kr", q[1], bi)
         gli = mult("kc,rc->kr", q[1], br) + mult("kc,rc->kr", q[0], bi)
         w_own = scattered_right(jnp.stack([wr, wi])).astype(BF)
-        w_prev = passed_along(w_own, "col", 1)
-        left = (left.astype(F32) - eta_left * scattered_left(jnp.stack([glr, gli]))).astype(BF)
-        if step + 1 < ITERS:
-            w_next = passed_along(w_own, "col", -1)
-            grad_next = folded(w_own, w_next, pick_own, pick_next, cos_next, sin_next)
+        last = step + 1 == ITERS
+        terms = scattered_left(jnp.stack([glr, gli]))
+        terms, w_own = lax.optimization_barrier((terms, w_own))
+        beside = [passed_along(w_own, "col", by) for by in ((1,) if last else (1, -1))]
+        left = (left.astype(F32) - eta_left * sum(t.astype(F32) for t in terms)).astype(BF)
+        if last:
+            left, beside = lax.optimization_barrier((left, beside))
+        else:
+            lw, beside = gathered_left(left, beside)
+            grad_next = folded(w_own, beside[1], pick_own, pick_next, cos_next, sin_next)
             right_next = (right_next.astype(F32) - eta_right * grad_next).astype(BF)
-        grad_own = folded(w_prev, w_own, pick_prev, pick_own, cos_own, sin_own)
+        grad_own = folded(beside[0], w_own, pick_prev, pick_own, cos_own, sin_own)
         right = (right.astype(F32) - eta_right * grad_own).astype(BF)
     return (left, right)
 

time: 113 us -> 93.9 us (0.83)
  blocking collectives: 0 us -> 17.9 us
  waiting for transfers between devices: 43.9 us -> 26.6 us
  starting transfers between devices: 50.7 us -> 34.1 us
  local copies, waits for them, and re-layouts: 3.23 us -> 1.82 us
  other arithmetic: 5.36 us -> 3.96 us
    ppermute x28 -> x16, waiting for transfers between devices: 35.9 us -> 12 us  [exchanged(): return lax.ppermute(shard, axis, [(i, i ^ flip) for i in range(size)])]
    ppermute x28 -> x16, starting transfers between devices: 40.9 us -> 17.4 us  [exchanged(): return lax.ppermute(shard, axis, [(i, i ^ flip) for i in range(size)])]
    all_gather x0 -> x2, blocking collectives: none -> 17.9 us  [gathered_right(): half = lax.all_gather(shard, 'row', axis=1, axis_index_groups=same_core())]
    all_to_all x0 -> x2, starting transfers between devices: none -> 6.81 us  [scattered_right(): parts = lax.all_to_all(parts, 'row', 0, 0, axis_index_groups=same_core())]
    all_to_all x0 -> x2, waiting for transfers between devices: none -> 6.59 us  [scattered_right(): parts = lax.all_to_all(parts, 'row', 0, 0, axis_index_groups=same_core())]
    convert_element_type x5 -> x6, other arithmetic: 0.88 us -> 2.42 us  [the longest x2 1.52 us: scattered_right(): parts = jnp.moveaxis(pair, 1, 0).astype(BF)]
    unnamed x24 -> x10, local copies, waits for them, and re-layouts: 2.62 us -> 1.34 us
  transfers between devices with their start and end apart: 32 -> 22, of which waited for: 18 -> 11; matrix products, arithmetic and copies ran while one was open for 7% -> 6% of each run, Pallas kernels for 0% -> 0%
where the time goes in v3:
time: 93.9 us; the launch traced here: 93.5 us
  starting transfers between devices  34.1 us (36%)
  waiting for transfers between devices  26.6 us (28%)
  blocking collectives  17.9 us (19%)
  matrix products  7.9 us (8%)
  other arithmetic  3.96 us (4%)
  local copies, waits for them, and re-layouts  1.82 us (2%)
  between operations  1.35 us (1%)
    all_gather x2, blocking collectives, gathered_right(): half = lax.all_gather(shard, 'row', axis=1, axis_index_groups=same_core())  17.9 us
    ppermute x16, starting transfers between devices, exchanged(): return lax.ppermute(shard, axis, [(i, i ^ flip) for i in range(size)])  17.4 us
    ppermute x16, waiting for transfers between devices, exchanged(): return lax.ppermute(shard, axis, [(i, i ^ flip) for i in range(size)])  12 us
    ppermute x4, starting transfers between devices, passed_along(): lax.ppermute(shard, axis, [(i, (i + by) % size) for i in range(size)])  9.88 us
    ppermute x4, waiting for transfers between devices, passed_along(): lax.ppermute(shard, axis, [(i, (i + by) % size) for i in range(size)])  8.03 us
    dot_general x33, matrix products, mult(): return jnp.einsum(spec, a, b, preferred_element_type=F32)  7.9 us
    all_to_all x2, starting transfers between devices, scattered_right(): parts = lax.all_to_all(parts, 'row', 0, 0, axis_index_groups=same_core())  6.81 us
    all_to_all x2, waiting for transfers between devices, scattered_right(): parts = lax.all_to_all(parts, 'row', 0, 0, axis_index_groups=same_core())  6.59 us
  transfers between devices with their start and end apart: 22, of which 11 were waited for; matrix products, arithmetic and copies ran while one was open for 6% of the time, Pallas kernels for 0%

profile of v3, /device:TPU:0, one launch (start us, length us, event | category | flops | bytes accessed | tf_op | source)
XLA Modules:
  0.0 93.5 jit_solution(8782927871148151797)
XLA Ops:
  0.6 5.1 %collective-permute-start = (bf16[2,64,256]{2,1,0:T(8,128)(2,1)}, bf16[2,64,256]{2,1,0:T(8,128)(2,1)S(1)}, u32[]{:S(2)}, u32[]{:S(2)}) collective-permute-start(bf16[2,64,256]{2,1,0:T(8,128)(2,1)} %param.6), channel_id=1, source_target_pairs={{0,3},{1,0},{2,1},{3,2},{4,7},{5,4},{6,5},{7,6},{8,11},{9,8},{10,9... | collective-permute-start | bytes 196616 | tf_op jit(solution)/shard_map/ppermute | solution.py:21
  8.6 1.4 %collective-permute-start.3 = (bf16[2,128,256]{2,1,0:T(8,128)(2,1)S(1)}, bf16[2,128,256]{2,1,0:T(8,128)(2,1)S(1)}, u32[]{:S(2)}, u32[]{:S(2)}) collective-permute-start(bf16[2,128,256]{2,1,0:T(8,128)(2,1)S(1)} %copy-done), channel_id=1, source_target_pairs={{0,2},{1,3},{2,0},{3,1},{4,6},{5,7},{6,4},{7,5},{8,10},{9,11},{10,... | collective-permute-start | bytes 393224 | tf_op jit(solution)/shard_map/ppermute | solution.py:16
  9.9 3.0 %collective-permute-start.4 = (bf16[2,128,256]{2,1,0:T(8,128)(2,1)S(1)}, bf16[2,128,256]{2,1,0:T(8,128)(2,1)S(1)}, u32[]{:S(2)}, u32[]{:S(2)}) collective-permute-start(bf16[2,128,256]{2,1,0:T(8,128)(2,1)S(1)} %copy-done), channel_id=1, source_target_pairs={{0,3},{1,2},{2,1},{3,0},{4,7},{5,6},{6,5},{7,4},{8,11},{9,10},{10,... | collective-permute-start | bytes 393224 | tf_op jit(solution)/shard_map/ppermute | solution.py:16
  13.2 9.1 %all_gather.8 = bf16[2,4,64,256]{3,2,1,0:T(8,128)(2,1)S(1)} all-gather(bf16[2,1,64,256]{3,2,1,0:T(8,128)(2,1)S(1)} %pad_maximum_fusion), channel_id=1, replica_groups={{0,8,16,24},{4,12,20,28},{1,9,17,25},{5,13,21,29},{2,10,18,26},{6,14,22..., dimensions={1}, use_global_device_ids=true | all-gather | bytes 327680 | tf_op jit(solution)/shard_map/all_gather | solution.py:49
  22.6 1.3 %collective-permute-done.1 = bf16[2,4,64,256]{3,2,1,0:T(8,128)(2,1)S(1)} collective-permute-done((bf16[2,4,64,256]{3,2,1,0:T(8,128)(2,1)S(1)}, bf16[2,4,64,256]{3,2,1,0:T(8,128)(2,1)S(1)}, u32[]{:S(2)}, u32[]{:S(2)}) %collective-permute-start.1) | collective-permute-done | bytes 262176 | tf_op jit(solution)/shard_map/ppermute | solution.py:16
  28.0 1.3 %collective-permute-start.6 = (bf16[2,128,256]{2,1,0:T(8,128)(2,1)S(1)}, bf16[2,128,256]{2,1,0:T(8,128)(2,1)S(1)}, u32[]{:S(2)}, u32[]{:S(2)}) collective-permute-start(bf16[2,128,256]{2,1,0:T(8,128)(2,1)S(1)} %get-tuple-element.43), channel_id=1, source_target_pairs={{0,2},{1,3},{2,0},{3,1},{4,6},{5,7},{6,4},{7,5},{8,10},{9,11},{10,... | collective-permute-start | bytes 393224 | tf_op jit(solution)/shard_map/ppermute | solution.py:16
  29.3 2.5 %collective-permute-start.7 = (bf16[2,128,256]{2,1,0:T(8,128)(2,1)S(1)}, bf16[2,128,256]{2,1,0:T(8,128)(2,1)S(1)}, u32[]{:S(2)}, u32[]{:S(2)}) collective-permute-start(bf16[2,128,256]{2,1,0:T(8,128)(2,1)S(1)} %get-tuple-element.41), channel_id=1, source_target_pairs={{0,3},{1,2},{2,1},{3,0},{4,7},{5,6},{6,5},{7,4},{8,11},{9,10},{10,... | collective-permute-start | bytes 393224 | tf_op jit(solution)/shard_map/ppermute | solution.py:16
  32.5 3.4 %all-to-all-start = ((bf16[4,2,64,256]{3,2,1,0:T(8,128)(2,1)}), bf16[4,2,64,256]{3,2,1,0:T(8,128)(2,1)S(1)}, u32[]{:S(2)}, u32[]{:S(2)}) async-start(bf16[4,2,64,256]{3,2,1,0:T(8,128)(2,1)} %fusion.25), calls=%async_computation | async-start | bytes 524288 | tf_op jit(solution)/shard_map/all_to_all | solution.py:76
  36.1 5.2 %all-to-all-done = bf16[4,2,64,256]{3,2,1,0:T(8,128)(2,1)S(1)} async-done(((bf16[4,2,64,256]{3,2,1,0:T(8,128)(2,1)}), bf16[4,2,64,256]{3,2,1,0:T(8,128)(2,1)S(1)}, u32[]{:S(2)}, u32[]{:S(2)}) %all-to-all-start) | async-done | bytes 262176 | tf_op jit(solution)/shard_map/all_to_all | solution.py:76
  41.4 2.1 %collective-permute-start.10 = (bf16[2,64,256]{2,1,0:T(8,128)(2,1)S(1)}, bf16[2,64,256]{2,1,0:T(8,128)(2,1)S(1)}, u32[]{:S(2)}, u32[]{:S(2)}) collective-permute-start(bf16[2,64,256]{2,1,0:T(8,128)(2,1)S(1)} %reduce_sum.24), channel_id=1, source_target_pairs={{0,3},{1,0},{2,1},{3,2},{4,7},{5,4},{6,5},{7,6},{8,11},{9,8},{10,9... | collective-permute-start | bytes 196616 | tf_op jit(solution)/shard_map/ppermute | solution.py:21
  43.6 2.0 %collective-permute-start.12 = (bf16[2,128,256]{2,1,0:T(8,128)(2,1)S(1)}, bf16[2,128,256]{2,1,0:T(8,128)(2,1)S(1)}, u32[]{:S(2)}, u32[]{:S(2)}) collective-permute-start(bf16[2,128,256]{2,1,0:T(8,128)(2,1)S(1)} %subtract_convert_fusion.1), channel_id=1, source_target_pairs={{0,1},{1,0},{2,3},{3,2},{4,5},{5,4},{6,7},{7,6},{8,9},{9,8},{10,11... | collective-permute-start | bytes 393224 | tf_op jit(solution)/shard_map/ppermute | solution.py:16
  46.1 4.2 %collective-permute-done.9 = bf16[2,64,256]{2,1,0:T(8,128)(2,1)S(1)} collective-permute-done((bf16[2,64,256]{2,1,0:T(8,128)(2,1)S(1)}, bf16[2,64,256]{2,1,0:T(8,128)(2,1)S(1)}, u32[]{:S(2)}, u32[]{:S(2)}) %collective-permute-start.9) | collective-permute-done | bytes 65568 | tf_op jit(solution)/shard_map/ppermute | solution.py:21
  50.4 1.7 %collective-permute-start.14 = (bf16[2,128,256]{2,1,0:T(8,128)(2,1)S(1)}, bf16[2,128,256]{2,1,0:T(8,128)(2,1)S(1)}, u32[]{:S(2)}, u32[]{:S(2)}) collective-permute-start(bf16[2,128,256]{2,1,0:T(8,128)(2,1)S(1)} %subtract_convert_fusion.1), channel_id=1, source_target_pairs={{0,3},{1,2},{2,1},{3,0},{4,7},{5,6},{6,5},{7,4},{8,11},{9,10},{10,... | collective-permute-start | bytes 393224 | tf_op jit(solution)/shard_map/ppermute | solution.py:16
  53.2 8.8 %all_gather.9 = bf16[2,4,64,256]{3,2,1,0:T(8,128)(2,1)S(1)} all-gather(bf16[2,1,64,256]{3,2,1,0:T(8,128)(2,1)S(1)} %pad_maximum_fusion.1), channel_id=1, replica_groups={{0,8,16,24},{4,12,20,28},{1,9,17,25},{5,13,21,29},{2,10,18,26},{6,14,22..., dimensions={1}, use_global_device_ids=true | all-gather | bytes 327680 | tf_op jit(solution)/shard_map/all_gather | solution.py:49
  62.2 1.3 %collective-permute-done.11 = bf16[2,4,64,256]{3,2,1,0:T(8,128)(2,1)S(1)} collective-permute-done((bf16[2,4,64,256]{3,2,1,0:T(8,128)(2,1)S(1)}, bf16[2,4,64,256]{3,2,1,0:T(8,128)(2,1)S(1)}, u32[]{:S(2)}, u32[]{:S(2)}) %collective-permute-start.11) | collective-permute-done | bytes 262176 | tf_op jit(solution)/shard_map/ppermute | solution.py:16
  66.9 0.9 collective-permute-done.18
  68.5 3.4 %all-to-all-start.1 = ((bf16[4,2,64,256]{3,2,1,0:T(8,128)(2,1)}), bf16[4,2,64,256]{3,2,1,0:T(8,128)(2,1)S(1)}, u32[]{:S(2)}, u32[]{:S(2)}) async-start(bf16[4,2,64,256]{3,2,1,0:T(8,128)(2,1)} %fusion.27), calls=%async_computation.1 | async-start | bytes 524288 | tf_op jit(solution)/shard_map/all_to_all | solution.py:76
  72.0 1.9 %collective-permute-start.15 = (bf16[2,128,256]{2,1,0:T(8,128)(2,1)S(1)}, bf16[2,128,256]{2,1,0:T(8,128)(2,1)S(1)}, u32[]{:S(2)}, u32[]{:S(2)}) collective-permute-start(bf16[2,128,256]{2,1,0:T(8,128)(2,1)S(1)} %get-tuple-element.39), channel_id=1, source_target_pairs={{0,1},{1,0},{2,3},{3,2},{4,5},{5,4},{6,7},{7,6},{8,9},{9,8},{10,11... | collective-permute-start | bytes 393224 | tf_op jit(solution)/shard_map/ppermute | solution.py:16
  73.9 0.9 collective-permute-start.16
  74.8 1.6 %collective-permute-start.17 = (bf16[2,128,256]{2,1,0:T(8,128)(2,1)S(1)}, bf16[2,128,256]{2,1,0:T(8,128)(2,1)S(1)}, u32[]{:S(2)}, u32[]{:S(2)}) collective-permute-start(bf16[2,128,256]{2,1,0:T(8,128)(2,1)S(1)} %get-tuple-element.38), channel_id=1, source_target_pairs={{0,3},{1,2},{2,1},{3,0},{4,7},{5,6},{6,5},{7,4},{8,11},{9,10},{10,... | collective-permute-start | bytes 393224 | tf_op jit(solution)/shard_map/ppermute | solution.py:16
  76.4 1.4 %all-to-all-done.1 = bf16[4,2,64,256]{3,2,1,0:T(8,128)(2,1)S(1)} async-done(((bf16[4,2,64,256]{3,2,1,0:T(8,128)(2,1)}), bf16[4,2,64,256]{3,2,1,0:T(8,128)(2,1)S(1)}, u32[]{:S(2)}, u32[]{:S(2)}) %all-to-all-start.1) | async-done | bytes 262176 | tf_op jit(solution)/shard_map/all_to_all | solution.py:76
  78.4 7.9 %collective-permute-done.16 = bf16[2,128,256]{2,1,0:T(8,128)(2,1)S(1)} collective-permute-done((bf16[2,128,256]{2,1,0:T(8,128)(2,1)S(1)}, bf16[2,128,256]{2,1,0:T(8,128)(2,1)S(1)}, u32[]{:S(2)}, u32[]{:S(2)}) %collective-permute-start.16) | collective-permute-done | bytes 131104 | tf_op jit(solution)/shard_map/ppermute | solution.py:16
  86.4 2.7 %collective-permute-start.19 = (bf16[2,64,256]{2,1,0:T(8,128)(2,1)S(1)}, bf16[2,64,256]{2,1,0:T(8,128)(2,1)S(1)}, u32[]{:S(2)}, u32[]{:S(2)}) collective-permute-start(bf16[2,64,256]{2,1,0:T(8,128)(2,1)S(1)} %reduce_sum.25), channel_id=1, source_target_pairs={{0,1},{1,2},{2,3},{3,0},{4,5},{5,6},{6,7},{7,4},{8,9},{9,10},{10,1... | collective-permute-start | bytes 196616 | tf_op jit(solution)/shard_map/ppermute | solution.py:21
  89.8 2.7 %collective-permute-done.19 = bf16[2,64,256]{2,1,0:T(8,128)(2,1)S(1)} collective-permute-done((bf16[2,64,256]{2,1,0:T(8,128)(2,1)S(1)}, bf16[2,64,256]{2,1,0:T(8,128)(2,1)S(1)}, u32[]{:S(2)}, u32[]{:S(2)}) %collective-permute-start.19) | collective-permute-done | bytes 65568 | tf_op jit(solution)/shard_map/ppermute | solution.py:21
  (113 shorter events, 16.5 us)
Async XLA Ops:
  0.6 5.1 %copy-start.2 = (bf16[2,64,256]{2,1,0:T(8,128)(2,1)S(1)}, bf16[2,64,256]{2,1,0:T(8,128)(2,1)}, u32[]{:S(2)}) copy-start(bf16[2,64,256]{2,1,0:T(8,128)(2,1)} %param.6) | copy-start | bytes 196612
  0.6 7.0 %copy-start.1 = (bf16[2,256,256]{2,1,0:T(8,128)(2,1)S(1)}, bf16[2,256,256]{2,1,0:T(8,128)(2,1)}, u32[]{:S(2)}) copy-start(bf16[2,256,256]{2,1,0:T(8,128)(2,1)} %param.7) | copy-start | bytes 786436
  0.6 7.9 %collective-permute-start = (bf16[2,64,256]{2,1,0:T(8,128)(2,1)}, bf16[2,64,256]{2,1,0:T(8,128)(2,1)S(1)}, u32[]{:S(2)}, u32[]{:S(2)}) collective-permute-start(bf16[2,64,256]{2,1,0:T(8,128)(2,1)} %param.6), channel_id=1, source_target_pairs={{0,3},{1,0},{2,1},{3,2},{4,7},{5,4},{6,5},{7,6},{8,11},{9,8},{10,9... | collective-permute-start | bytes 196616 | tf_op jit(solution)/shard_map/ppermute | solution.py:21
  5.8 16.7 %collective-permute-start.2 = (bf16[2,128,256]{2,1,0:T(8,128)(2,1)}, bf16[2,128,256]{2,1,0:T(8,128)(2,1)S(1)}, u32[]{:S(2)}, u32[]{:S(2)}) collective-permute-start(bf16[2,128,256]{2,1,0:T(8,128)(2,1)} %param.5), channel_id=1, source_target_pairs={{0,1},{1,0},{2,3},{3,2},{4,5},{5,4},{6,7},{7,6},{8,9},{9,8},{10,11... | collective-permute-start | bytes 393224 | tf_op jit(solution)/shard_map/ppermute | solution.py:16
  8.6 13.9 %collective-permute-start.3 = (bf16[2,128,256]{2,1,0:T(8,128)(2,1)S(1)}, bf16[2,128,256]{2,1,0:T(8,128)(2,1)S(1)}, u32[]{:S(2)}, u32[]{:S(2)}) collective-permute-start(bf16[2,128,256]{2,1,0:T(8,128)(2,1)S(1)} %copy-done), channel_id=1, source_target_pairs={{0,2},{1,3},{2,0},{3,1},{4,6},{5,7},{6,4},{7,5},{8,10},{9,11},{10,... | collective-permute-start | bytes 393224 | tf_op jit(solution)/shard_map/ppermute | solution.py:16
  9.9 12.6 %collective-permute-start.4 = (bf16[2,128,256]{2,1,0:T(8,128)(2,1)S(1)}, bf16[2,128,256]{2,1,0:T(8,128)(2,1)S(1)}, u32[]{:S(2)}, u32[]{:S(2)}) collective-permute-start(bf16[2,128,256]{2,1,0:T(8,128)(2,1)S(1)} %copy-done), channel_id=1, source_target_pairs={{0,3},{1,2},{2,1},{3,0},{4,7},{5,6},{6,5},{7,4},{8,11},{9,10},{10,... | collective-permute-start | bytes 393224 | tf_op jit(solution)/shard_map/ppermute | solution.py:16
  22.3 1.5 %collective-permute-start.1 = (bf16[2,4,64,256]{3,2,1,0:T(8,128)(2,1)S(1)}, bf16[2,4,64,256]{3,2,1,0:T(8,128)(2,1)S(1)}, u32[]{:S(2)}, u32[]{:S(2)}) collective-permute-start(bf16[2,4,64,256]{3,2,1,0:T(8,128)(2,1)S(1)} %all_gather.8), channel_id=1, source_target_pairs={{0,4},{4,0},{8,12},{12,8},{16,20},{20,16},{24,28},{28,24},{1,5},{5... | collective-permute-start | bytes 786440 | tf_op jit(solution)/shard_map/ppermute | solution.py:16
  26.5 5.3 %collective-permute-start.8 = (bf16[2,4,64,256]{3,2,0,1:T(8,128)(2,1)S(1)}, bf16[2,4,64,256]{3,2,0,1:T(8,128)(2,1)S(1)}, u32[]{:S(2)}, u32[]{:S(2)}) collective-permute-start(bf16[2,4,64,256]{3,2,0,1:T(8,128)(2,1)S(1)} %fusion.26), channel_id=1, source_target_pairs={{0,4},{4,0},{8,12},{12,8},{16,20},{20,16},{24,28},{28,24},{1,5},{5... | collective-permute-start | bytes 786440 | tf_op jit(solution)/shard_map/ppermute | solution.py:16
  27.3 14.0 %collective-permute-start.5 = (bf16[2,128,256]{2,1,0:T(8,128)(2,1)S(1)}, bf16[2,128,256]{2,1,0:T(8,128)(2,1)S(1)}, u32[]{:S(2)}, u32[]{:S(2)}) collective-permute-start(bf16[2,128,256]{2,1,0:T(8,128)(2,1)S(1)} %get-tuple-element.42), channel_id=1, source_target_pairs={{0,1},{1,0},{2,3},{3,2},{4,5},{5,4},{6,7},{7,6},{8,9},{9,8},{10,11... | collective-permute-start | bytes 393224 | tf_op jit(solution)/shard_map/ppermute | solution.py:16
  28.0 13.4 %collective-permute-start.6 = (bf16[2,128,256]{2,1,0:T(8,128)(2,1)S(1)}, bf16[2,128,256]{2,1,0:T(8,128)(2,1)S(1)}, u32[]{:S(2)}, u32[]{:S(2)}) collective-permute-start(bf16[2,128,256]{2,1,0:T(8,128)(2,1)S(1)} %get-tuple-element.43), channel_id=1, source_target_pairs={{0,2},{1,3},{2,0},{3,1},{4,6},{5,7},{6,4},{7,5},{8,10},{9,11},{10,... | collective-permute-start | bytes 393224 | tf_op jit(solution)/shard_map/ppermute | solution.py:16
  29.3 12.1 %collective-permute-start.7 = (bf16[2,128,256]{2,1,0:T(8,128)(2,1)S(1)}, bf16[2,128,256]{2,1,0:T(8,128)(2,1)S(1)}, u32[]{:S(2)}, u32[]{:S(2)}) collective-permute-start(bf16[2,128,256]{2,1,0:T(8,128)(2,1)S(1)} %get-tuple-element.41), channel_id=1, source_target_pairs={{0,3},{1,2},{2,1},{3,0},{4,7},{5,6},{6,5},{7,4},{8,11},{9,10},{10,... | collective-permute-start | bytes 393224 | tf_op jit(solution)/shard_map/ppermute | solution.py:16
  32.5 8.8 %all-to-all-start = ((bf16[4,2,64,256]{3,2,1,0:T(8,128)(2,1)}), bf16[4,2,64,256]{3,2,1,0:T(8,128)(2,1)S(1)}, u32[]{:S(2)}, u32[]{:S(2)}) async-start(bf16[4,2,64,256]{3,2,1,0:T(8,128)(2,1)} %fusion.25), calls=%async_computation | async-start | bytes 524288 | tf_op jit(solution)/shard_map/all_to_all | solution.py:76
  41.4 4.8 %collective-permute-start.10 = (bf16[2,64,256]{2,1,0:T(8,128)(2,1)S(1)}, bf16[2,64,256]{2,1,0:T(8,128)(2,1)S(1)}, u32[]{:S(2)}, u32[]{:S(2)}) collective-permute-start(bf16[2,64,256]{2,1,0:T(8,128)(2,1)S(1)} %reduce_sum.24), channel_id=1, source_target_pairs={{0,3},{1,0},{2,1},{3,2},{4,7},{5,4},{6,5},{7,6},{8,11},{9,8},{10,9... | collective-permute-start | bytes 196616 | tf_op jit(solution)/shard_map/ppermute | solution.py:21
  43.5 6.9 %collective-permute-start.9 = (bf16[2,64,256]{2,1,0:T(8,128)(2,1)S(1)}, bf16[2,64,256]{2,1,0:T(8,128)(2,1)S(1)}, u32[]{:S(2)}, u32[]{:S(2)}) collective-permute-start(bf16[2,64,256]{2,1,0:T(8,128)(2,1)S(1)} %reduce_sum.24), channel_id=1, source_target_pairs={{0,1},{1,2},{2,3},{3,0},{4,5},{5,6},{6,7},{7,4},{8,9},{9,10},{10,1... | collective-permute-start | bytes 196616 | tf_op jit(solution)/shard_map/ppermute | solution.py:21
  43.6 18.5 %collective-permute-start.12 = (bf16[2,128,256]{2,1,0:T(8,128)(2,1)S(1)}, bf16[2,128,256]{2,1,0:T(8,128)(2,1)S(1)}, u32[]{:S(2)}, u32[]{:S(2)}) collective-permute-start(bf16[2,128,256]{2,1,0:T(8,128)(2,1)S(1)} %subtract_convert_fusion.1), channel_id=1, source_target_pairs={{0,1},{1,0},{2,3},{3,2},{4,5},{5,4},{6,7},{7,6},{8,9},{9,8},{10,11... | collective-permute-start | bytes 393224 | tf_op jit(solution)/shard_map/ppermute | solution.py:16
  50.4 11.7 %collective-permute-start.13 = (bf16[2,128,256]{2,1,0:T(8,128)(2,1)S(1)}, bf16[2,128,256]{2,1,0:T(8,128)(2,1)S(1)}, u32[]{:S(2)}, u32[]{:S(2)}) collective-permute-start(bf16[2,128,256]{2,1,0:T(8,128)(2,1)S(1)} %subtract_convert_fusion.1), channel_id=1, source_target_pairs={{0,2},{1,3},{2,0},{3,1},{4,6},{5,7},{6,4},{7,5},{8,10},{9,11},{10,... | collective-permute-start | bytes 393224 | tf_op jit(solution)/shard_map/ppermute | solution.py:16
  50.4 11.8 %collective-permute-start.14 = (bf16[2,128,256]{2,1,0:T(8,128)(2,1)S(1)}, bf16[2,128,256]{2,1,0:T(8,128)(2,1)S(1)}, u32[]{:S(2)}, u32[]{:S(2)}) collective-permute-start(bf16[2,128,256]{2,1,0:T(8,128)(2,1)S(1)} %subtract_convert_fusion.1), channel_id=1, source_target_pairs={{0,3},{1,2},{2,1},{3,0},{4,7},{5,6},{6,5},{7,4},{8,11},{9,10},{10,... | collective-permute-start | bytes 393224 | tf_op jit(solution)/shard_map/ppermute | solution.py:16
  61.9 1.5 %collective-permute-start.11 = (bf16[2,4,64,256]{3,2,1,0:T(8,128)(2,1)S(1)}, bf16[2,4,64,256]{3,2,1,0:T(8,128)(2,1)S(1)}, u32[]{:S(2)}, u32[]{:S(2)}) collective-permute-start(bf16[2,4,64,256]{3,2,1,0:T(8,128)(2,1)S(1)} %all_gather.9), channel_id=1, source_target_pairs={{0,4},{4,0},{8,12},{12,8},{16,20},{20,16},{24,28},{28,24},{1,5},{5... | collective-permute-start | bytes 786440 | tf_op jit(solution)/shard_map/ppermute | solution.py:16
  66.1 1.6 %collective-permute-start.18 = (bf16[2,4,64,256]{3,2,0,1:T(8,128)(2,1)S(1)}, bf16[2,4,64,256]{3,2,0,1:T(8,128)(2,1)S(1)}, u32[]{:S(2)}, u32[]{:S(2)}) collective-permute-start(bf16[2,4,64,256]{3,2,0,1:T(8,128)(2,1)S(1)} %fusion.28), channel_id=1, source_target_pairs={{0,4},{4,0},{8,12},{12,8},{16,20},{20,16},{24,28},{28,24},{1,5},{5... | collective-permute-start | bytes 786440 | tf_op jit(solution)/shard_map/ppermute | solution.py:16
  68.5 9.3 %all-to-all-start.1 = ((bf16[4,2,64,256]{3,2,1,0:T(8,128)(2,1)}), bf16[4,2,64,256]{3,2,1,0:T(8,128)(2,1)S(1)}, u32[]{:S(2)}, u32[]{:S(2)}) async-start(bf16[4,2,64,256]{3,2,1,0:T(8,128)(2,1)} %fusion.27), calls=%async_computation.1 | async-start | bytes 524288 | tf_op jit(solution)/shard_map/all_to_all | solution.py:76
  72.0 6.5 %collective-permute-start.15 = (bf16[2,128,256]{2,1,0:T(8,128)(2,1)S(1)}, bf16[2,128,256]{2,1,0:T(8,128)(2,1)S(1)}, u32[]{:S(2)}, u32[]{:S(2)}) collective-permute-start(bf16[2,128,256]{2,1,0:T(8,128)(2,1)S(1)} %get-tuple-element.39), channel_id=1, source_target_pairs={{0,1},{1,0},{2,3},{3,2},{4,5},{5,4},{6,7},{7,6},{8,9},{9,8},{10,11... | collective-permute-start | bytes 393224 | tf_op jit(solution)/shard_map/ppermute | solution.py:16
  73.9 12.5 %collective-permute-start.16 = (bf16[2,128,256]{2,1,0:T(8,128)(2,1)S(1)}, bf16[2,128,256]{2,1,0:T(8,128)(2,1)S(1)}, u32[]{:S(2)}, u32[]{:S(2)}) collective-permute-start(bf16[2,128,256]{2,1,0:T(8,128)(2,1)S(1)} %get-tuple-element.40), channel_id=1, source_target_pairs={{0,2},{1,3},{2,0},{3,1},{4,6},{5,7},{6,4},{7,5},{8,10},{9,11},{10,... | collective-permute-start | bytes 393224 | tf_op jit(solution)/shard_map/ppermute | solution.py:16
  74.8 11.6 %collective-permute-start.17 = (bf16[2,128,256]{2,1,0:T(8,128)(2,1)S(1)}, bf16[2,128,256]{2,1,0:T(8,128)(2,1)S(1)}, u32[]{:S(2)}, u32[]{:S(2)}) collective-permute-start(bf16[2,128,256]{2,1,0:T(8,128)(2,1)S(1)} %get-tuple-element.38), channel_id=1, source_target_pairs={{0,3},{1,2},{2,1},{3,0},{4,7},{5,6},{6,5},{7,4},{8,11},{9,10},{10,... | collective-permute-start | bytes 393224 | tf_op jit(solution)/shard_map/ppermute | solution.py:16
  86.4 6.1 %collective-permute-start.19 = (bf16[2,64,256]{2,1,0:T(8,128)(2,1)S(1)}, bf16[2,64,256]{2,1,0:T(8,128)(2,1)S(1)}, u32[]{:S(2)}, u32[]{:S(2)}) collective-permute-start(bf16[2,64,256]{2,1,0:T(8,128)(2,1)S(1)} %reduce_sum.25), channel_id=1, source_target_pairs={{0,1},{1,2},{2,3},{3,0},{4,5},{5,6},{6,7},{7,4},{8,9},{9,10},{10,1... | collective-permute-start | bytes 196616 | tf_op jit(solution)/shard_map/ppermute | solution.py:21
  (3 other events, 2.3 us)

commit v4 on v1

v4 whole, which is shorter than its diff:
```python
import functools
import math

import jax
import jax.numpy as jnp
from jax import lax
from jax.experimental import pallas as pl
from jax.experimental.pallas import tpu as pltpu
from jax.sharding import PartitionSpec as P

ITERS = 2
NDELAY = 64
BF = jnp.bfloat16
F32 = jnp.float32


def exchanged(shard, axis, flip):
    size = lax.axis_size(axis)
    return lax.ppermute(shard, axis, [(i, i ^ flip) for i in range(size)])


def passed_along(shard, axis, by):
    size = lax.axis_size(axis)
    return lax.ppermute(shard, axis, [(i, (i + by) % size) for i in range(size)])


def same_core():
    size = lax.axis_size("row")
    return [list(range(core, size, 2)) for core in range(2)]


def gathered_left(shard, small, near_waits):
    size = lax.axis_size("col")
    held, small = lax.optimization_barrier((shard, small))
    parts = [shard]
    for d in range(1, size):
        parts.append(exchanged(held if (d == 1) == near_waits else shard, "col", d))
    return parts, small


def on_chip(kernel, outs, scratch=(), cost=1 << 20):
    return pl.pallas_call(
        kernel,
        out_shape=outs,
        scratch_shapes=list(scratch),
        cost_estimate=pl.CostEstimate(flops=cost, bytes_accessed=1 << 20, transcendentals=0),
        compiler_params=pltpu.CompilerParams(vmem_limit_bytes=48 * 1024 * 1024),
    )


def dot(a, b, ca, cb):
    return lax.dot_general(a, b, (((ca,), (cb,)), ((), ())), preferred_element_type=F32)


def stage_kernel(cols, *refs):
    left_refs, refs = refs[:cols], refs[cols:]
    q_own, q_other, rec, theirs, mine, *refs = refs
    left_outs, (lbuf, qbuf, wbuf, gbuf) = refs[:cols], refs[cols:]
    me, core = lax.axis_index("col"), lax.axis_index("row") & 1
    wide, narrow, chips = left_refs[0].shape[1], q_own.shape[2], q_own.shape[0]

    def left_rows(d):
        return pl.ds(pl.multiple_of((me ^ d) * wide, wide), wide)

    def right_rows(chip, which):
        return pl.ds(pl.multiple_of((2 * chip + which) * narrow, narrow), narrow)

    for d in range(cols):
        lbuf[:, left_rows(d), :] = left_refs[d][...]
    for chip in range(chips):
        qbuf[:, right_rows(chip, core), :] = q_own[chip]
        qbuf[:, right_rows(chip, core ^ 1), :] = q_other[chip]
    br = dot(lbuf[0], qbuf[0], 0, 0) + dot(lbuf[1], qbuf[1], 0, 0) - rec[0].astype(F32)
    bi = dot(lbuf[1], qbuf[0], 0, 0) - dot(lbuf[0], qbuf[1], 0, 0) - rec[1].astype(F32)
    br, bi = br.astype(BF), bi.astype(BF)
    wbuf[0] = dot(lbuf[0], br, 1, 0) + dot(lbuf[1], bi, 1, 0)
    wbuf[1] = dot(lbuf[1], br, 1, 0) - dot(lbuf[0], bi, 1, 0)
    for chip in range(chips):
        theirs[chip] = wbuf[:, right_rows(chip, core ^ 1), :].astype(BF)
        mine[chip] = wbuf[:, right_rows(chip, core), :]
    gbuf[0] = dot(qbuf[0], br, 1, 1) - dot(qbuf[1], bi, 1, 1)
    gbuf[1] = dot(qbuf[1], br, 1, 1) + dot(qbuf[0], bi, 1, 1)
    for d in range(cols):
        left_outs[d][...] = gbuf[:, left_rows(d), :].astype(left_outs[d].dtype)


def stage(left_parts, q_own, q_other, rec):
    cols = len(left_parts)
    two, wide, rows = left_parts[0].shape
    shots = q_own.shape[3]
    rank = wide * cols
    part = jax.ShapeDtypeStruct((two, wide, rows), F32)
    sent = jax.ShapeDtypeStruct((two, wide, rows), BF)
    outs = [jax.ShapeDtypeStruct(q_own.shape, BF), jax.ShapeDtypeStruct(q_own.shape, F32), part]
    outs += [sent] * (cols - 1)
    scratch = [
        pltpu.VMEM((two, rank, rows), BF),
        pltpu.VMEM((two, rank, shots), BF),
        pltpu.VMEM((two, rank, shots), F32),
        pltpu.VMEM((two, rank, rows), F32),
    ]
    call = on_chip(functools.partial(stage_kernel, cols), outs, scratch, 24 * rank * rows * shots)
    theirs, mine, *terms = call(*left_parts, q_own, q_other, rec)
    return theirs, mine, terms


def picks(near):
    shots = near.shape[1]
    at = lax.broadcasted_iota(jnp.int32, (2 * shots, shots), 0)
    return (at == near).astype(BF)


def mixed(own, nxt, pick, table):
    shots = pick.shape[1]
    part = [dot(own[z], pick[:shots], 1, 0) + dot(nxt[z], pick[shots:], 1, 0) for z in range(2)]
    own = [own[z].astype(F32) for z in range(2)]
    cos, sin, cosp, sinp = table[0:1], table[1:2], table[4:5], table[5:6]
    real = cos * own[0] + sin * own[1] + cosp * part[0] + sinp * part[1]
    imag = cos * own[1] - sin * own[0] + cosp * part[1] - sinp * part[0]
    return real.astype(BF), imag.astype(BF)


def stepped(right, before, here, pick_before, pick_here, cos, sin, eta):
    shots = pick_here.shape[1]
    s = [
        here[z].astype(F32)
        + dot(before[z], pick_before[shots:], 1, 1)
        + dot(here[z], pick_here[:shots], 1, 1)
        for z in range(2)
    ]
    grad = cos * s[0] - sin * s[1], cos * s[1] + sin * s[0]
    return [(right[z].astype(F32) - eta * grad[z]).astype(BF) for z in range(2)]


def table_kernel(rows, table):
    table[...] = rows[...]


def first_kernel(right, right_next, near, table, q):
    q[0], q[1] = mixed(right, right_next, picks(near[1:2]), table)


def middle_kernel(eta, right, right_next, w_prev, w_own, w_next, near, table, q, new):
    prev, own, nxt = picks(near[0:1]), picks(near[1:2]), picks(near[2:3])
    here = stepped(right, w_prev, w_own, prev, own, table[0:1], table[1:2], eta)
    there = stepped(right_next, w_own, w_next, own, nxt, table[2:3], table[3:4], eta)
    new[0], new[1] = here
    q[0], q[1] = mixed(here, there, own, table)


def last_kernel(eta_left, eta_right, right, w_prev, w_own, near, table, left, *refs):
    *terms, new_left, new_right = refs
    prev, own = picks(near[0:1]), picks(near[1:2])
    here = stepped(right, w_prev, w_own, prev, own, table[0:1], table[1:2], eta_right)
    new_right[0], new_right[1] = here
    grad = sum(t[...].astype(F32) for t in terms)
    new_left[...] = (left[...].astype(F32) - eta_left * grad).astype(BF)


def on_device(left_factor, right_factor, recorded, partner, delay):
    shots_dev = recorded.shape[2]
    rows_dev = recorded.shape[1]
    shots_all = partner.shape[0]
    rows_all = rows_dev * lax.axis_size("row")
    blocks = lax.axis_size("col")
    rank_full = left_factor.shape[1] * blocks
    eta_left = 0.1 * math.sqrt(rank_full / shots_all)
    eta_right = 0.05 / math.sqrt(rank_full * rows_all)
    block = lax.axis_index("col")

    def of_block(vector, by):
        return lax.dynamic_slice_in_dim(vector, jnp.mod(block + by, blocks) * shots_dev, shots_dev, 0)

    def near_of(by):
        start = jnp.mod(block + by, blocks) * shots_dev
        return jnp.mod(of_block(partner, by) - start, shots_all)

    near = jnp.stack([near_of(-1), near_of(0), near_of(1)])
    delays = jnp.concatenate([of_block(delay, 0), of_block(delay, 1)]).astype(F32)
    delay_part = dot(delays.astype(BF), picks(near[1:2]), 0, 0)
    theta = 2.0 * math.pi * jnp.stack([delays[:shots_dev], delays[shots_dev:], delay_part]) / NDELAY
    table = jnp.stack([jnp.cos(theta), jnp.sin(theta)], axis=1).reshape(6, shots_dev)
    table = on_chip(table_kernel, jax.ShapeDtypeStruct(table.shape, F32), cost=1 << 30)(table)

    def over_row(q, parts):
        half = lax.all_gather(q, "row", axis=0, axis_index_groups=same_core())
        half, parts = lax.optimization_barrier((half, parts))
        return half, exchanged(half, "row", 1), parts

    shard = jax.ShapeDtypeStruct(right_factor.shape, BF)
    chip = lax.axis_index("row") >> 1
    left, right = left_factor, right_factor
    right_next = passed_along(right, "col", -1)
    parts, right_next = gathered_left(left, right_next, False)
    q = on_chip(first_kernel, shard)(right, right_next, near, table)
    for step in range(ITERS):
        q_own, q_other, parts = over_row(q, parts)
        theirs, mine, terms = stage(parts, q_own, q_other, recorded)
        pair = (mine + exchanged(theirs, "row", 1).astype(F32)).astype(BF)
        total = lax.dynamic_index_in_dim(pair, chip, 0, False).astype(F32)
        for d in range(1, pair.shape[0]):
            sent = lax.dynamic_index_in_dim(pair, chip ^ d, 0, False)
            total = total + exchanged(sent, "row", 2 * d).astype(F32)
        w_own = total.astype(BF)
        terms = [terms[0]] + [exchanged(terms[d], "col", d) for d in range(1, blocks)]
        if step + 1 < ITERS:
            beside = [passed_along(w_own, "col", by) for by in (1, -1)]
            terms, w_own = lax.optimization_barrier((terms, w_own))
            left = (left.astype(F32) - eta_left * sum(t.astype(F32) for t in terms)).astype(BF)
            parts, (w_prev, w_next) = gathered_left(left, beside, True)
            middle = on_chip(functools.partial(middle_kernel, eta_right), [shard, shard])
            q, right = middle(right, right_next, w_prev, w_own, w_next, near, table)
    w_prev = passed_along(w_own, "col", 1)
    outs = [jax.ShapeDtypeStruct(left.shape, BF), shard]
    final = on_chip(functools.partial(last_kernel, eta_left, eta_right), outs)
    return tuple(final(right, w_prev, w_own, near, table, left, *terms))


def solution(mesh):
    in_specs = (P(None, "col", "row"), P(None, "row", "col"), P(None, "row", "col"), P(), P())
    out_specs = (P(None, "col", "row"), P(None, "row", "col"))
    return jax.shard_map(
        on_device, mesh=mesh, in_specs=in_specs, out_specs=out_specs, check_vma=False
    )
```

time: 131 us -> 85.3 us (0.65)
  between operations: 24.2 us -> 0.87 us
  waiting for transfers between devices: 43.1 us -> 24.2 us
  blocking collectives: 0 us -> 17.5 us
  starting transfers between devices: 50.1 us -> 36.2 us
  matrix products: 7.92 us -> 0.2 us
  Pallas kernels: 0 us -> 4.71 us
  other arithmetic: 2.74 us -> 0.53 us
  local copies, waits for them, and re-layouts: 2.52 us -> 0.85 us
    all_gather x0 -> x2, blocking collectives: none -> 17.5 us  [over_row(): half = lax.all_gather(q, 'row', axis=0, axis_index_groups=same_core())]
    ppermute x40 -> x22, starting transfers between devices: 44.2 us -> 27.8 us  [exchanged(): return lax.ppermute(shard, axis, [(i, i ^ flip) for i in range(size)])]
    ppermute x4, waiting for transfers between devices: 12.2 us -> 1.51 us  [passed_along(): lax.ppermute(shard, axis, [(i, (i + by) % size) for i in range(size)])]
    ppermute x40 -> x22, waiting for transfers between devices: 30.9 us -> 22.7 us  [exchanged(): return lax.ppermute(shard, axis, [(i, i ^ flip) for i in range(size)])]
    dot_general x33 -> x1, matrix products: 7.92 us -> 0.2 us  [dot(): lax.dot_general(a, b, (((ca,), (cb,)), ((), ())), preferred_element_type=...]
    pallas_call x0 -> x6, Pallas kernels: none -> 4.71 us  [the longest x2 2.79 us: stage(): theirs, mine, *terms = call(*left_parts, q_own, q_other, rec)]
    ppermute x4, starting transfers between devices: 5.88 us -> 8.45 us  [passed_along(): lax.ppermute(shard, axis, [(i, (i + by) % size) for i in range(size)])]
    convert_element_type x15 -> x6, other arithmetic: 1.96 us -> 0.32 us  [the longest x2 0.14 us: on_device(): pair = (mine + exchanged(theirs, 'row', 1).astype(F32)).astype(BF)]
  transfers between devices with their start and end apart: 44 -> 26, of which waited for: 17 -> 9; matrix products, arithmetic and copies ran while one was open for 5% -> 1% of each run, Pallas kernels for 0% -> 1%
where the time goes in v4:
time: 85.3 us; the launch traced here: 85.1 us
  starting transfers between devices  36.2 us (42%)
  waiting for transfers between devices  24.2 us (28%)
  blocking collectives  17.5 us (21%)
  Pallas kernels  4.71 us (6%)
  between operations  0.87 us (1%)
    ppermute x22, starting transfers between devices, exchanged(): return lax.ppermute(shard, axis, [(i, i ^ flip) for i in range(size)])  27.8 us
    ppermute x22, waiting for transfers between devices, exchanged(): return lax.ppermute(shard, axis, [(i, i ^ flip) for i in range(size)])  22.7 us
    all_gather x2, blocking collectives, over_row(): half = lax.all_gather(q, 'row', axis=0, axis_index_groups=same_core())  17.5 us
    ppermute x4, starting transfers between devices, passed_along(): lax.ppermute(shard, axis, [(i, (i + by) % size) for i in range(size)])  8.45 us
    pallas_call x2, Pallas kernels, stage(): theirs, mine, *terms = call(*left_parts, q_own, q_other, rec)  2.79 us
  transfers between devices with their start and end apart: 26, of which 9 were waited for; matrix products, arithmetic and copies ran while one was open for 1% of the time, Pallas kernels for 1%

profile of v4, /device:TPU:0, one launch (start us, length us, event | category | flops | bytes accessed | tf_op | source)
XLA Modules:
  0.0 85.1 jit_solution(9330982404618926379)
XLA Ops:
  0.6 5.1 %collective-permute-start = (bf16[2,64,256]{2,1,0:T(8,128)(2,1)}, bf16[2,64,256]{2,1,0:T(8,128)(2,1)S(1)}, u32[]{:S(2)}, u32[]{:S(2)}) collective-permute-start(bf16[2,64,256]{2,1,0:T(8,128)(2,1)} %right.3), channel_id=1, source_target_pairs={{0,3},{1,0},{2,1},{3,2},{4,7},{5,4},{6,5},{7,6},{8,11},{9,8},{10,9... | collective-permute-start | bytes 196616 | tf_op jit(solution)/shard_map/ppermute | solution.py:24
  7.0 1.5 %collective-permute-done.right_next = bf16[2,64,256]{2,1,0:T(8,128)(2,1)S(1)} collective-permute-done((bf16[2,64,256]{2,1,0:T(8,128)(2,1)}, bf16[2,64,256]{2,1,0:T(8,128)(2,1)S(1)}, u32[]{:S(2)}, u32[]{:S(2)}) %collective-permute-start) | collective-permute-done | bytes 65568 | tf_op jit(solution)/shard_map/ppermute | solution.py:24
  8.5 4.2 %collective-permute-start.3 = (bf16[2,128,256]{2,1,0:T(8,128)(2,1)S(1)}, bf16[2,128,256]{2,1,0:T(8,128)(2,1)S(1)}, u32[]{:S(2)}, u32[]{:S(2)}) collective-permute-start(bf16[2,128,256]{2,1,0:T(8,128)(2,1)S(1)} %copy-done.1), channel_id=1, source_target_pairs={{0,3},{1,2},{2,1},{3,0},{4,7},{5,6},{6,5},{7,4},{8,11},{9,10},{10,... | collective-permute-start | bytes 393224 | tf_op jit(solution)/shard_map/ppermute | solution.py:19
  13.0 9.3 %all-gather = bf16[8,64,256]{2,1,0:T(8,128)(2,1)S(1)} all-gather(bf16[2,64,256]{2,1,0:T(8,128)(2,1)S(1)} %shard_map.69), channel_id=2, replica_groups={{0,8,16,24},{4,12,20,28},{1,9,17,25},{5,13,21,29},{2,10,18,26},{6,14,22..., dimensions={0}, use_global_device_ids=true | all-gather | bytes 327680 | tf_op jit(solution)/shard_map/all_gather | solution.py:186
  22.4 1.5 %collective-permute-done.4.refs_5_ = bf16[4,2,64,256]{3,2,1,0:T(8,128)(2,1)S(1)} collective-permute-done((bf16[4,2,64,256]{3,2,1,0:T(8,128)(2,1)S(1)}, bf16[4,2,64,256]{3,2,1,0:T(8,128)(2,1)S(1)}, u32[]{:S(2)}, u32[]{:S(2)}) %collective-permute-start.4) | collective-permute-done | bytes 262176 | tf_op jit(solution)/shard_map/ppermute | solution.py:19
  23.9 1.4 %shard_map.70 = (bf16[4,2,64,256]{3,2,1,0:T(8,128)(2,1)S(1)}, f32[4,2,64,256]{3,2,1,0:T(8,128)S(1)}, f32[2,128,256]{2,1,0:T(8,128)S(1)}, bf16[2,128,256]{2,1,0:T...) custom-call(bf16[2,128,256]{2,1,0:T(8,128)(2,1)S(1)} %copy-done.1, ...), custom_call_target="tpu_custom_call" | custom-call | flops 805306368 | bytes 1048576 | tf_op jit(solution)/shard_map/pallas_call | solution.py:103
  25.5 1.4 %collective-permute-done.8 = bf16[4,2,64,256]{3,2,1,0:T(8,128)(2,1)S(1)} collective-permute-done((bf16[4,2,64,256]{3,2,1,0:T(8,128)(2,1)S(1)}, bf16[4,2,64,256]{3,2,1,0:T(8,128)(2,1)S(1)}, u32[]{:S(2)}, u32[]{:S(2)}) %collective-permute-start.8) | collective-permute-done | bytes 262176 | tf_op jit(solution)/shard_map/ppermute | solution.py:19
  28.3 1.5 %collective-permute-start.11 = (bf16[2,64,256]{2,1,0:T(8,128)(2,1)S(1)}, bf16[2,64,256]{2,1,0:T(8,128)(2,1)S(1)}, u32[]{:S(2)}, u32[]{:S(2)}) collective-permute-start(bf16[2,64,256]{2,1,0:T(8,128)(2,1)S(1)} %get-tuple-element.76), channel_id=1, source_target_pairs={{0,24},{4,28},{8,16},{12,20},{16,8},{20,12},{24,0},{28,4},{1,25},{... | collective-permute-start | bytes 196616 | tf_op jit(solution)/shard_map/ppermute | solution.py:19
  31.1 2.2 %collective-permute-start.6 = (bf16[2,128,256]{2,1,0:T(8,128)(2,1)S(1)}, bf16[2,128,256]{2,1,0:T(8,128)(2,1)S(1)}, u32[]{:S(2)}, u32[]{:S(2)}) collective-permute-start(bf16[2,128,256]{2,1,0:T(8,128)(2,1)S(1)} %get-tuple-element.45), channel_id=1, source_target_pairs={{0,2},{1,3},{2,0},{3,1},{4,6},{5,7},{6,4},{7,5},{8,10},{9,11},{10,... | collective-permute-start | bytes 393224 | tf_op jit(solution)/shard_map/ppermute | solution.py:19
  33.3 1.7 %collective-permute-start.7 = (bf16[2,128,256]{2,1,0:T(8,128)(2,1)S(1)}, bf16[2,128,256]{2,1,0:T(8,128)(2,1)S(1)}, u32[]{:S(2)}, u32[]{:S(2)}) collective-permute-start(bf16[2,128,256]{2,1,0:T(8,128)(2,1)S(1)} %get-tuple-element.46), channel_id=1, source_target_pairs={{0,3},{1,2},{2,1},{3,0},{4,7},{5,6},{6,5},{7,4},{8,11},{9,10},{10,... | collective-permute-start | bytes 393224 | tf_op jit(solution)/shard_map/ppermute | solution.py:19
  35.0 2.2 %collective-permute-start.13 = (bf16[2,64,256]{2,1,0:T(8,128)(2,1)S(1)}, bf16[2,64,256]{2,1,0:T(8,128)(2,1)S(1)}, u32[]{:S(2)}, u32[]{:S(2)}) collective-permute-start(bf16[2,64,256]{2,1,0:T(8,128)(2,1)S(1)} %fusion.6.w_own), channel_id=1, source_target_pairs={{0,3},{1,0},{2,1},{3,2},{4,7},{5,4},{6,5},{7,6},{8,11},{9,8},{10,9... | collective-permute-start | bytes 196616 | tf_op jit(solution)/shard_map/ppermute | solution.py:24
  37.7 4.7 %collective-permute-done.6 = bf16[2,128,256]{2,1,0:T(8,128)(2,1)S(1)} collective-permute-done((bf16[2,128,256]{2,1,0:T(8,128)(2,1)S(1)}, bf16[2,128,256]{2,1,0:T(8,128)(2,1)S(1)}, u32[]{:S(2)}, u32[]{:S(2)}) %collective-permute-start.6) | collective-permute-done | bytes 131104 | tf_op jit(solution)/shard_map/ppermute | solution.py:19
  42.3 2.2 %collective-permute-done.7 = bf16[2,128,256]{2,1,0:T(8,128)(2,1)S(1)} collective-permute-done((bf16[2,128,256]{2,1,0:T(8,128)(2,1)S(1)}, bf16[2,128,256]{2,1,0:T(8,128)(2,1)S(1)}, u32[]{:S(2)}, u32[]{:S(2)}) %collective-permute-start.7) | collective-permute-done | bytes 131104 | tf_op jit(solution)/shard_map/ppermute | solution.py:19
  44.6 3.5 %collective-permute-start.16 = (bf16[2,128,256]{2,1,0:T(8,128)(2,1)S(1)}, bf16[2,128,256]{2,1,0:T(8,128)(2,1)S(1)}, u32[]{:S(2)}, u32[]{:S(2)}) collective-permute-start(bf16[2,128,256]{2,1,0:T(8,128)(2,1)S(1)} %subtract_convert_fusion.refs_0_.left), channel_id=1, source_target_pairs={{0,3},{1,2},{2,1},{3,0},{4,7},{5,6},{6,5},{7,4},{8,11},{9,10},{10,... | collective-permute-start | bytes 393224 | tf_op jit(solution)/shard_map/ppermute | solution.py:19
  48.1 3.0 %collective-permute-start.15 = (bf16[2,128,256]{2,1,0:T(8,128)(2,1)S(1)}, bf16[2,128,256]{2,1,0:T(8,128)(2,1)S(1)}, u32[]{:S(2)}, u32[]{:S(2)}) collective-permute-start(bf16[2,128,256]{2,1,0:T(8,128)(2,1)S(1)} %subtract_convert_fusion.refs_0_.left), channel_id=1, source_target_pairs={{0,2},{1,3},{2,0},{3,1},{4,6},{5,7},{6,4},{7,5},{8,10},{9,11},{10,... | collective-permute-start | bytes 393224 | tf_op jit(solution)/shard_map/ppermute | solution.py:19
  51.8 8.2 %all-gather.1 = bf16[8,64,256]{2,1,0:T(8,128)(2,1)S(1)} all-gather(bf16[2,64,256]{2,1,0:T(8,128)(2,1)S(1)} %get-tuple-element.57), channel_id=3, replica_groups={{0,8,16,24},{4,12,20,28},{1,9,17,25},{5,13,21,29},{2,10,18,26},{6,14,22..., dimensions={0}, use_global_device_ids=true | all-gather | bytes 327680 | tf_op jit(solution)/shard_map/all_gather | solution.py:186
  60.1 1.5 %collective-permute-done.17.refs_5_ = bf16[4,2,64,256]{3,2,1,0:T(8,128)(2,1)S(1)} collective-permute-done((bf16[4,2,64,256]{3,2,1,0:T(8,128)(2,1)S(1)}, bf16[4,2,64,256]{3,2,1,0:T(8,128)(2,1)S(1)}, u32[]{:S(2)}, u32[]{:S(2)}) %collective-permute-start.17) | collective-permute-done | bytes 262176 | tf_op jit(solution)/shard_map/ppermute | solution.py:19
  61.6 1.4 %shard_map.72 = (bf16[4,2,64,256]{3,2,1,0:T(8,128)(2,1)S(1)}, f32[4,2,64,256]{3,2,1,0:T(8,128)S(1)}, f32[2,128,256]{2,1,0:T(8,128)S(1)}, bf16[2,128,256]{2,1,0:T...) custom-call(bf16[2,128,256]{2,1,0:T(8,128)(2,1)S(1)} %subtract_convert_fusion.refs_0_.left, ...), custom_call_target="tpu_custom_call" | custom-call | flops 805306368 | bytes 1048576 | tf_op jit(solution)/shard_map/pallas_call | solution.py:103
  63.2 1.4 %collective-permute-done.18 = bf16[4,2,64,256]{3,2,1,0:T(8,128)(2,1)S(1)} collective-permute-done((bf16[4,2,64,256]{3,2,1,0:T(8,128)(2,1)S(1)}, bf16[4,2,64,256]{3,2,1,0:T(8,128)(2,1)S(1)}, u32[]{:S(2)}, u32[]{:S(2)}) %collective-permute-start.18) | collective-permute-done | bytes 262176 | tf_op jit(solution)/shard_map/ppermute | solution.py:19
  64.7 1.4 %collective-permute-start.19 = (bf16[2,64,256]{2,1,0:T(8,128)(2,1)S(1)}, bf16[2,64,256]{2,1,0:T(8,128)(2,1)S(1)}, u32[]{:S(2)}, u32[]{:S(2)}) collective-permute-start(bf16[2,64,256]{2,1,0:T(8,128)(2,1)S(1)} %get-tuple-element.72), channel_id=1, source_target_pairs={{0,8},{4,12},{8,0},{12,4},{16,24},{20,28},{24,16},{28,20},{1,9},{5... | collective-permute-start | bytes 196616 | tf_op jit(solution)/shard_map/ppermute | solution.py:19
  66.1 1.5 %collective-permute-start.21 = (bf16[2,64,256]{2,1,0:T(8,128)(2,1)S(1)}, bf16[2,64,256]{2,1,0:T(8,128)(2,1)S(1)}, u32[]{:S(2)}, u32[]{:S(2)}) collective-permute-start(bf16[2,64,256]{2,1,0:T(8,128)(2,1)S(1)} %get-tuple-element.73), channel_id=1, source_target_pairs={{0,24},{4,28},{8,16},{12,20},{16,8},{20,12},{24,0},{28,4},{1,25},{... | collective-permute-start | bytes 196616 | tf_op jit(solution)/shard_map/ppermute | solution.py:19
  68.2 1.5 %collective-permute-start.23 = (bf16[2,128,256]{2,1,0:T(8,128)(2,1)S(1)}, bf16[2,128,256]{2,1,0:T(8,128)(2,1)S(1)}, u32[]{:S(2)}, u32[]{:S(2)}) collective-permute-start(bf16[2,128,256]{2,1,0:T(8,128)(2,1)S(1)} %get-tuple-element.67), channel_id=1, source_target_pairs={{0,1},{1,0},{2,3},{3,2},{4,5},{5,4},{6,7},{7,6},{8,9},{9,8},{10,11... | collective-permute-start | bytes 393224 | tf_op jit(solution)/shard_map/ppermute | solution.py:19
  69.7 3.0 %collective-permute-start.24 = (bf16[2,128,256]{2,1,0:T(8,128)(2,1)S(1)}, bf16[2,128,256]{2,1,0:T(8,128)(2,1)S(1)}, u32[]{:S(2)}, u32[]{:S(2)}) collective-permute-start(bf16[2,128,256]{2,1,0:T(8,128)(2,1)S(1)} %get-tuple-element.68), channel_id=1, source_target_pairs={{0,2},{1,3},{2,0},{3,1},{4,6},{5,7},{6,4},{7,5},{8,10},{9,11},{10,... | collective-permute-start | bytes 393224 | tf_op jit(solution)/shard_map/ppermute | solution.py:19
  74.5 9.6 %collective-permute-done.24.refs_2_ = bf16[2,128,256]{2,1,0:T(8,128)(2,1)S(1)} collective-permute-done((bf16[2,128,256]{2,1,0:T(8,128)(2,1)S(1)}, bf16[2,128,256]{2,1,0:T(8,128)(2,1)S(1)}, u32[]{:S(2)}, u32[]{:S(2)}) %collective-permute-start.24) | collective-permute-done | bytes 131104 | tf_op jit(solution)/shard_map/ppermute | solution.py:19
  (63 shorter events, 9.6 us)
Async XLA Ops:
  0.6 7.9 %collective-permute-start = (bf16[2,64,256]{2,1,0:T(8,128)(2,1)}, bf16[2,64,256]{2,1,0:T(8,128)(2,1)S(1)}, u32[]{:S(2)}, u32[]{:S(2)}) collective-permute-start(bf16[2,64,256]{2,1,0:T(8,128)(2,1)} %right.3), channel_id=1, source_target_pairs={{0,3},{1,0},{2,1},{3,2},{4,7},{5,4},{6,5},{7,6},{8,11},{9,8},{10,9... | collective-permute-start | bytes 196616 | tf_op jit(solution)/shard_map/ppermute | solution.py:24
  5.7 16.5 %collective-permute-start.1 = (bf16[2,128,256]{2,1,0:T(8,128)(2,1)}, bf16[2,128,256]{2,1,0:T(8,128)(2,1)S(1)}, u32[]{:S(2)}, u32[]{:S(2)}) collective-permute-start(bf16[2,128,256]{2,1,0:T(8,128)(2,1)} %refs_0_), channel_id=1, source_target_pairs={{0,1},{1,0},{2,3},{3,2},{4,5},{5,4},{6,7},{7,6},{8,9},{9,8},{10,11... | collective-permute-start | bytes 393224 | tf_op jit(solution)/shard_map/ppermute | solution.py:19
  8.5 13.7 %collective-permute-start.3 = (bf16[2,128,256]{2,1,0:T(8,128)(2,1)S(1)}, bf16[2,128,256]{2,1,0:T(8,128)(2,1)S(1)}, u32[]{:S(2)}, u32[]{:S(2)}) collective-permute-start(bf16[2,128,256]{2,1,0:T(8,128)(2,1)S(1)} %copy-done.1), channel_id=1, source_target_pairs={{0,3},{1,2},{2,1},{3,0},{4,7},{5,6},{6,5},{7,4},{8,11},{9,10},{10,... | collective-permute-start | bytes 393224 | tf_op jit(solution)/shard_map/ppermute | solution.py:19
  12.7 9.5 %collective-permute-start.2 = (bf16[2,128,256]{2,1,0:T(8,128)(2,1)S(1)}, bf16[2,128,256]{2,1,0:T(8,128)(2,1)S(1)}, u32[]{:S(2)}, u32[]{:S(2)}) collective-permute-start(bf16[2,128,256]{2,1,0:T(8,128)(2,1)S(1)} %copy-done.1), channel_id=1, source_target_pairs={{0,2},{1,3},{2,0},{3,1},{4,6},{5,7},{6,4},{7,5},{8,10},{9,11},{10,... | collective-permute-start | bytes 393224 | tf_op jit(solution)/shard_map/ppermute | solution.py:19
  22.3 1.6 %collective-permute-start.4 = (bf16[4,2,64,256]{3,2,1,0:T(8,128)(2,1)S(1)}, bf16[4,2,64,256]{3,2,1,0:T(8,128)(2,1)S(1)}, u32[]{:S(2)}, u32[]{:S(2)}) collective-permute-start(bf16[4,2,64,256]{3,2,1,0:T(8,128)(2,1)S(1)} %bitcast.30), channel_id=1, source_target_pairs={{0,4},{4,0},{8,12},{12,8},{16,20},{20,16},{24,28},{28,24},{1,5},{5... | collective-permute-start | bytes 786440 | tf_op jit(solution)/shard_map/ppermute | solution.py:19
  25.3 1.6 %collective-permute-start.8 = (bf16[4,2,64,256]{3,2,1,0:T(8,128)(2,1)S(1)}, bf16[4,2,64,256]{3,2,1,0:T(8,128)(2,1)S(1)}, u32[]{:S(2)}, u32[]{:S(2)}) collective-permute-start(bf16[4,2,64,256]{3,2,1,0:T(8,128)(2,1)S(1)} %get-tuple-element.48), channel_id=1, source_target_pairs={{0,4},{4,0},{8,12},{12,8},{16,20},{20,16},{24,28},{28,24},{1,5},{5... | collective-permute-start | bytes 786440 | tf_op jit(solution)/shard_map/ppermute | solution.py:19
  27.0 6.3 %collective-permute-start.9 = (bf16[2,64,256]{2,1,0:T(8,128)(2,1)S(1)}, bf16[2,64,256]{2,1,0:T(8,128)(2,1)S(1)}, u32[]{:S(2)}, u32[]{:S(2)}) collective-permute-start(bf16[2,64,256]{2,1,0:T(8,128)(2,1)S(1)} %get-tuple-element.75), channel_id=1, source_target_pairs={{0,8},{4,12},{8,0},{12,4},{16,24},{20,28},{24,16},{28,20},{1,9},{5... | collective-permute-start | bytes 196616 | tf_op jit(solution)/shard_map/ppermute | solution.py:19
  28.3 6.7 %collective-permute-start.11 = (bf16[2,64,256]{2,1,0:T(8,128)(2,1)S(1)}, bf16[2,64,256]{2,1,0:T(8,128)(2,1)S(1)}, u32[]{:S(2)}, u32[]{:S(2)}) collective-permute-start(bf16[2,64,256]{2,1,0:T(8,128)(2,1)S(1)} %get-tuple-element.76), channel_id=1, source_target_pairs={{0,24},{4,28},{8,16},{12,20},{16,8},{20,12},{24,0},{28,4},{1,25},{... | collective-permute-start | bytes 196616 | tf_op jit(solution)/shard_map/ppermute | solution.py:19
  29.8 5.2 %collective-permute-start.10 = (bf16[2,64,256]{2,1,0:T(8,128)(2,1)S(1)}, bf16[2,64,256]{2,1,0:T(8,128)(2,1)S(1)}, u32[]{:S(2)}, u32[]{:S(2)}) collective-permute-start(bf16[2,64,256]{2,1,0:T(8,128)(2,1)S(1)} %get-tuple-element.77), channel_id=1, source_target_pairs={{0,16},{4,20},{8,24},{12,28},{16,0},{20,4},{24,8},{28,12},{1,17},{... | collective-permute-start | bytes 196616 | tf_op jit(solution)/shard_map/ppermute | solution.py:19
  30.6 7.1 %collective-permute-start.5 = (bf16[2,128,256]{2,1,0:T(8,128)(2,1)S(1)}, bf16[2,128,256]{2,1,0:T(8,128)(2,1)S(1)}, u32[]{:S(2)}, u32[]{:S(2)}) collective-permute-start(bf16[2,128,256]{2,1,0:T(8,128)(2,1)S(1)} %get-tuple-element.44), channel_id=1, source_target_pairs={{0,1},{1,0},{2,3},{3,2},{4,5},{5,4},{6,7},{7,6},{8,9},{9,8},{10,11... | collective-permute-start | bytes 393224 | tf_op jit(solution)/shard_map/ppermute | solution.py:19
  31.1 11.2 %collective-permute-start.6 = (bf16[2,128,256]{2,1,0:T(8,128)(2,1)S(1)}, bf16[2,128,256]{2,1,0:T(8,128)(2,1)S(1)}, u32[]{:S(2)}, u32[]{:S(2)}) collective-permute-start(bf16[2,128,256]{2,1,0:T(8,128)(2,1)S(1)} %get-tuple-element.45), channel_id=1, source_target_pairs={{0,2},{1,3},{2,0},{3,1},{4,6},{5,7},{6,4},{7,5},{8,10},{9,11},{10,... | collective-permute-start | bytes 393224 | tf_op jit(solution)/shard_map/ppermute | solution.py:19
  33.3 11.2 %collective-permute-start.7 = (bf16[2,128,256]{2,1,0:T(8,128)(2,1)S(1)}, bf16[2,128,256]{2,1,0:T(8,128)(2,1)S(1)}, u32[]{:S(2)}, u32[]{:S(2)}) collective-permute-start(bf16[2,128,256]{2,1,0:T(8,128)(2,1)S(1)} %get-tuple-element.46), channel_id=1, source_target_pairs={{0,3},{1,2},{2,1},{3,0},{4,7},{5,6},{6,5},{7,4},{8,11},{9,10},{10,... | collective-permute-start | bytes 393224 | tf_op jit(solution)/shard_map/ppermute | solution.py:19
  35.0 16.1 %collective-permute-start.13 = (bf16[2,64,256]{2,1,0:T(8,128)(2,1)S(1)}, bf16[2,64,256]{2,1,0:T(8,128)(2,1)S(1)}, u32[]{:S(2)}, u32[]{:S(2)}) collective-permute-start(bf16[2,64,256]{2,1,0:T(8,128)(2,1)S(1)} %fusion.6.w_own), channel_id=1, source_target_pairs={{0,3},{1,0},{2,1},{3,2},{4,7},{5,4},{6,5},{7,6},{8,11},{9,8},{10,9... | collective-permute-start | bytes 196616 | tf_op jit(solution)/shard_map/ppermute | solution.py:24
  37.2 13.9 %collective-permute-start.12 = (bf16[2,64,256]{2,1,0:T(8,128)(2,1)S(1)}, bf16[2,64,256]{2,1,0:T(8,128)(2,1)S(1)}, u32[]{:S(2)}, u32[]{:S(2)}) collective-permute-start(bf16[2,64,256]{2,1,0:T(8,128)(2,1)S(1)} %fusion.6.w_own), channel_id=1, source_target_pairs={{0,1},{1,2},{2,3},{3,0},{4,5},{5,6},{6,7},{7,4},{8,9},{9,10},{10,1... | collective-permute-start | bytes 196616 | tf_op jit(solution)/shard_map/ppermute | solution.py:24
  44.6 15.4 %collective-permute-start.16 = (bf16[2,128,256]{2,1,0:T(8,128)(2,1)S(1)}, bf16[2,128,256]{2,1,0:T(8,128)(2,1)S(1)}, u32[]{:S(2)}, u32[]{:S(2)}) collective-permute-start(bf16[2,128,256]{2,1,0:T(8,128)(2,1)S(1)} %subtract_convert_fusion.refs_0_.left), channel_id=1, source_target_pairs={{0,3},{1,2},{2,1},{3,0},{4,7},{5,6},{6,5},{7,4},{8,11},{9,10},{10,... | collective-permute-start | bytes 393224 | tf_op jit(solution)/shard_map/ppermute | solution.py:19
  48.1 11.9 %collective-permute-start.15 = (bf16[2,128,256]{2,1,0:T(8,128)(2,1)S(1)}, bf16[2,128,256]{2,1,0:T(8,128)(2,1)S(1)}, u32[]{:S(2)}, u32[]{:S(2)}) collective-permute-start(bf16[2,128,256]{2,1,0:T(8,128)(2,1)S(1)} %subtract_convert_fusion.refs_0_.left), channel_id=1, source_target_pairs={{0,2},{1,3},{2,0},{3,1},{4,6},{5,7},{6,4},{7,5},{8,10},{9,11},{10,... | collective-permute-start | bytes 393224 | tf_op jit(solution)/shard_map/ppermute | solution.py:19
  51.1 8.9 %collective-permute-start.14 = (bf16[2,128,256]{2,1,0:T(8,128)(2,1)S(1)}, bf16[2,128,256]{2,1,0:T(8,128)(2,1)S(1)}, u32[]{:S(2)}, u32[]{:S(2)}) collective-permute-start(bf16[2,128,256]{2,1,0:T(8,128)(2,1)S(1)} %subtract_convert_fusion.refs_0_.left), channel_id=1, source_target_pairs={{0,1},{1,0},{2,3},{3,2},{4,5},{5,4},{6,7},{7,6},{8,9},{9,8},{10,11... | collective-permute-start | bytes 393224 | tf_op jit(solution)/shard_map/ppermute | solution.py:19
  64.7 8.1 %collective-permute-start.19 = (bf16[2,64,256]{2,1,0:T(8,128)(2,1)S(1)}, bf16[2,64,256]{2,1,0:T(8,128)(2,1)S(1)}, u32[]{:S(2)}, u32[]{:S(2)}) collective-permute-start(bf16[2,64,256]{2,1,0:T(8,128)(2,1)S(1)} %get-tuple-element.72), channel_id=1, source_target_pairs={{0,8},{4,12},{8,0},{12,4},{16,24},{20,28},{24,16},{28,20},{1,9},{5... | collective-permute-start | bytes 196616 | tf_op jit(solution)/shard_map/ppermute | solution.py:19
  66.1 7.2 %collective-permute-start.21 = (bf16[2,64,256]{2,1,0:T(8,128)(2,1)S(1)}, bf16[2,64,256]{2,1,0:T(8,128)(2,1)S(1)}, u32[]{:S(2)}, u32[]{:S(2)}) collective-permute-start(bf16[2,64,256]{2,1,0:T(8,128)(2,1)S(1)} %get-tuple-element.73), channel_id=1, source_target_pairs={{0,24},{4,28},{8,16},{12,20},{16,8},{20,12},{24,0},{28,4},{1,25},{... | collective-permute-start | bytes 196616 | tf_op jit(solution)/shard_map/ppermute | solution.py:19
  67.5 5.7 %collective-permute-start.20 = (bf16[2,64,256]{2,1,0:T(8,128)(2,1)S(1)}, bf16[2,64,256]{2,1,0:T(8,128)(2,1)S(1)}, u32[]{:S(2)}, u32[]{:S(2)}) collective-permute-start(bf16[2,64,256]{2,1,0:T(8,128)(2,1)S(1)} %get-tuple-element.74), channel_id=1, source_target_pairs={{0,16},{4,20},{8,24},{12,28},{16,0},{20,4},{24,8},{28,12},{1,17},{... | collective-permute-start | bytes 196616 | tf_op jit(solution)/shard_map/ppermute | solution.py:19
  68.2 6.2 %collective-permute-start.23 = (bf16[2,128,256]{2,1,0:T(8,128)(2,1)S(1)}, bf16[2,128,256]{2,1,0:T(8,128)(2,1)S(1)}, u32[]{:S(2)}, u32[]{:S(2)}) collective-permute-start(bf16[2,128,256]{2,1,0:T(8,128)(2,1)S(1)} %get-tuple-element.67), channel_id=1, source_target_pairs={{0,1},{1,0},{2,3},{3,2},{4,5},{5,4},{6,7},{7,6},{8,9},{9,8},{10,11... | collective-permute-start | bytes 393224 | tf_op jit(solution)/shard_map/ppermute | solution.py:19
  69.7 14.3 %collective-permute-start.24 = (bf16[2,128,256]{2,1,0:T(8,128)(2,1)S(1)}, bf16[2,128,256]{2,1,0:T(8,128)(2,1)S(1)}, u32[]{:S(2)}, u32[]{:S(2)}) collective-permute-start(bf16[2,128,256]{2,1,0:T(8,128)(2,1)S(1)} %get-tuple-element.68), channel_id=1, source_target_pairs={{0,2},{1,3},{2,0},{3,1},{4,6},{5,7},{6,4},{7,5},{8,10},{9,11},{10,... | collective-permute-start | bytes 393224 | tf_op jit(solution)/shard_map/ppermute | solution.py:19
  72.8 11.3 %collective-permute-start.25 = (bf16[2,128,256]{2,1,0:T(8,128)(2,1)S(1)}, bf16[2,128,256]{2,1,0:T(8,128)(2,1)S(1)}, u32[]{:S(2)}, u32[]{:S(2)}) collective-permute-start(bf16[2,128,256]{2,1,0:T(8,128)(2,1)S(1)} %get-tuple-element.69), channel_id=1, source_target_pairs={{0,3},{1,2},{2,1},{3,0},{4,7},{5,6},{6,5},{7,4},{8,11},{9,10},{10,... | collective-permute-start | bytes 393224 | tf_op jit(solution)/shard_map/ppermute | solution.py:19
  73.3 10.7 %collective-permute-start.22 = (bf16[2,64,256]{2,1,0:T(8,128)(2,1)S(1)}, bf16[2,64,256]{2,1,0:T(8,128)(2,1)S(1)}, u32[]{:S(2)}, u32[]{:S(2)}) collective-permute-start(bf16[2,64,256]{2,1,0:T(8,128)(2,1)S(1)} %fusion.3.w_own), channel_id=1, source_target_pairs={{0,1},{1,2},{2,3},{3,0},{4,5},{5,6},{6,7},{7,4},{8,9},{9,10},{10,1... | collective-permute-start | bytes 196616 | tf_op jit(solution)/shard_map/ppermute | solution.py:24
  (7 other events, 24.3 us)

commit v5 on v4

--- a/solution.py
+++ b/solution.py
@@ -110,26 +110,27 @@
     return (at == near).astype(BF)
 
 
+def stacked(x):
+    return x[...].reshape(-1, x.shape[2])
+
+
 def mixed(own, nxt, pick, table):
     shots = pick.shape[1]
-    part = [dot(own[z], pick[:shots], 1, 0) + dot(nxt[z], pick[shots:], 1, 0) for z in range(2)]
-    own = [own[z].astype(F32) for z in range(2)]
+    half = own.shape[0] // 2
+    part = dot(own, pick[:shots], 1, 0) + dot(nxt, pick[shots:], 1, 0)
+    own = own.astype(F32)
     cos, sin, cosp, sinp = table[0:1], table[1:2], table[4:5], table[5:6]
-    real = cos * own[0] + sin * own[1] + cosp * part[0] + sinp * part[1]
-    imag = cos * own[1] - sin * own[0] + cosp * part[1] - sinp * part[0]
-    return real.astype(BF), imag.astype(BF)
+    real = cos * own[:half] + sin * own[half:] + cosp * part[:half] + sinp * part[half:]
+    imag = cos * own[half:] - sin * own[:half] + cosp * part[half:] - sinp * part[:half]
+    return jnp.concatenate([real, imag]).astype(BF)
 
 
 def stepped(right, before, here, pick_before, pick_here, cos, sin, eta):
     shots = pick_here.shape[1]
-    s = [
-        here[z].astype(F32)
-        + dot(before[z], pick_before[shots:], 1, 1)
-        + dot(here[z], pick_here[:shots], 1, 1)
-        for z in range(2)
-    ]
-    grad = cos * s[0] - sin * s[1], cos * s[1] + sin * s[0]
-    return [(right[z].astype(F32) - eta * grad[z]).astype(BF) for z in range(2)]
+    half = here.shape[0] // 2
+    s = here.astype(F32) + dot(before, pick_before[shots:], 1, 1) + dot(here, pick_here[:shots], 1, 1)
+    grad = jnp.concatenate([cos * s[:half] - sin * s[half:], cos * s[half:] + sin * s[:half]])
+    return (right.astype(F32) - eta * grad).astype(BF)
 
 
 def table_kernel(rows, table):
@@ -137,22 +138,25 @@
 
 
 def first_kernel(right, right_next, near, table, q):
-    q[0], q[1] = mixed(right, right_next, picks(near[1:2]), table)
+    q[...] = mixed(stacked(right), stacked(right_next), picks(near[1:2]), table).reshape(q.shape)
 
 
 def middle_kernel(eta, right, right_next, w_prev, w_own, w_next, near, table, q, new):
     prev, own, nxt = picks(near[0:1]), picks(near[1:2]), picks(near[2:3])
-    here = stepped(right, w_prev, w_own, prev, own, table[0:1], table[1:2], eta)
-    there = stepped(right_next, w_own, w_next, own, nxt, table[2:3], table[3:4], eta)
-    new[0], new[1] = here
-    q[0], q[1] = mixed(here, there, own, table)
+    w_prev, w_own, w_next = stacked(w_prev), stacked(w_own), stacked(w_next)
+    here = stepped(stacked(right), w_prev, w_own, prev, own, table[0:1], table[1:2], eta)
+    there = stepped(stacked(right_next), w_own, w_next, own, nxt, table[2:3], table[3:4], eta)
+    new[...] = here.reshape(new.shape)
+    q[...] = mixed(here, there, own, table).reshape(q.shape)
 
 
 def last_kernel(eta_left, eta_right, right, w_prev, w_own, near, table, left, *refs):
     *terms, new_left, new_right = refs
     prev, own = picks(near[0:1]), picks(near[1:2])
-    here = stepped(right, w_prev, w_own, prev, own, table[0:1], table[1:2], eta_right)
-    new_right[0], new_right[1] = here
+    here = stepped(
+        stacked(right), stacked(w_prev), stacked(w_own), prev, own, table[0:1], table[1:2], eta_right
+    )
+    new_right[...] = here.reshape(new_right.shape)
     grad = sum(t[...].astype(F32) for t in terms)
     new_left[...] = (left[...].astype(F32) - eta_left * grad).astype(BF)
 
@@ -197,12 +201,14 @@
         q_own, q_other, parts = over_row(q, parts)
         theirs, mine, terms = stage(parts, q_own, q_other, recorded)
         pair = (mine + exchanged(theirs, "row", 1).astype(F32)).astype(BF)
-        total = lax.dynamic_index_in_dim(pair, chip, 0, False).astype(F32)
+        sums = [lax.dynamic_index_in_dim(pair, chip, 0, False)]
         for d in range(1, pair.shape[0]):
             sent = lax.dynamic_index_in_dim(pair, chip ^ d, 0, False)
-            total = total + exchanged(sent, "row", 2 * d).astype(F32)
-        w_own = total.astype(BF)
+            sums.append(exchanged(sent, "row", 2 * d))
         terms = [terms[0]] + [exchanged(terms[d], "col", d) for d in range(1, blocks)]
+        early = slice(2, 3) if step + 1 < ITERS else slice(1, 3)
+        sums, terms[early] = lax.optimization_barrier((sums, terms[early]))
+        w_own = sum(part.astype(F32) for part in sums).astype(BF)
         if step + 1 < ITERS:
             beside = [passed_along(w_own, "col", by) for by in (1, -1)]
             terms, w_own = lax.optimization_barrier((terms, w_own))

time: 85.3 us -> 78 us (0.914)
  starting transfers between devices: 36.2 us -> 32.1 us
  waiting for transfers between devices: 24.2 us -> 20.7 us
    ppermute x22, waiting for transfers between devices: 22.7 us -> 17.3 us  [exchanged(): return lax.ppermute(shard, axis, [(i, i ^ flip) for i in range(size)])]
    ppermute x22, starting transfers between devices: 27.8 us -> 24.8 us  [exchanged(): return lax.ppermute(shard, axis, [(i, i ^ flip) for i in range(size)])]
    ppermute x4, waiting for transfers between devices: 1.51 us -> 3.4 us  [passed_along(): lax.ppermute(shard, axis, [(i, (i + by) % size) for i in range(size)])]
    ppermute x4, starting transfers between devices: 8.45 us -> 7.24 us  [passed_along(): lax.ppermute(shard, axis, [(i, (i + by) % size) for i in range(size)])]
  transfers between devices with their start and end apart: 26 -> 26, of which waited for: 9 -> 10; matrix products, arithmetic and copies ran while one was open for 1% -> 1% of each run, Pallas kernels for 1% -> 1%
where the time goes in v5:
time: 78 us; the launch traced here: 77.8 us
  starting transfers between devices  32.1 us (41%)
  waiting for transfers between devices  20.7 us (27%)
  blocking collectives  18 us (23%)
  Pallas kernels  4.5 us (6%)
  local copies, waits for them, and re-layouts  0.87 us (1%)
  between operations  0.87 us (1%)
    ppermute x22, starting transfers between devices, exchanged(): return lax.ppermute(shard, axis, [(i, i ^ flip) for i in range(size)])  24.8 us
    all_gather x2, blocking collectives, over_row(): half = lax.all_gather(q, 'row', axis=0, axis_index_groups=same_core())  18 us
    ppermute x22, waiting for transfers between devices, exchanged(): return lax.ppermute(shard, axis, [(i, i ^ flip) for i in range(size)])  17.3 us
    ppermute x4, starting transfers between devices, passed_along(): lax.ppermute(shard, axis, [(i, (i + by) % size) for i in range(size)])  7.24 us
    ppermute x4, waiting for transfers between devices, passed_along(): lax.ppermute(shard, axis, [(i, (i + by) % size) for i in range(size)])  3.4 us
    pallas_call x2, Pallas kernels, stage(): theirs, mine, *terms = call(*left_parts, q_own, q_other, rec)  2.79 us
  transfers between devices with their start and end apart: 26, of which 10 were waited for; matrix products, arithmetic and copies ran while one was open for 1% of the time, Pallas kernels for 1%

profile of v5, /device:TPU:0, one launch (start us, length us, event | category | flops | bytes accessed | tf_op | source)
XLA Modules:
  0.0 77.8 jit_solution(10802217952267551328)
XLA Ops:
  0.6 5.1 %collective-permute-start = (bf16[2,64,256]{2,1,0:T(8,128)(2,1)}, bf16[2,64,256]{2,1,0:T(8,128)(2,1)S(1)}, u32[]{:S(2)}, u32[]{:S(2)}) collective-permute-start(bf16[2,64,256]{2,1,0:T(8,128)(2,1)} %right.3), channel_id=1, source_target_pairs={{0,3},{1,0},{2,1},{3,2},{4,7},{5,4},{6,5},{7,6},{8,11},{9,8},{10,9... | collective-permute-start | bytes 196616 | tf_op jit(solution)/shard_map/ppermute | solution.py:24
  7.0 1.5 %collective-permute-done.right_next = bf16[2,64,256]{2,1,0:T(8,128)(2,1)S(1)} collective-permute-done((bf16[2,64,256]{2,1,0:T(8,128)(2,1)}, bf16[2,64,256]{2,1,0:T(8,128)(2,1)S(1)}, u32[]{:S(2)}, u32[]{:S(2)}) %collective-permute-start) | collective-permute-done | bytes 65568 | tf_op jit(solution)/shard_map/ppermute | solution.py:24
  8.5 4.2 %collective-permute-start.3 = (bf16[2,128,256]{2,1,0:T(8,128)(2,1)S(1)}, bf16[2,128,256]{2,1,0:T(8,128)(2,1)S(1)}, u32[]{:S(2)}, u32[]{:S(2)}) collective-permute-start(bf16[2,128,256]{2,1,0:T(8,128)(2,1)S(1)} %copy-done.1), channel_id=1, source_target_pairs={{0,3},{1,2},{2,1},{3,0},{4,7},{5,6},{6,5},{7,4},{8,11},{9,10},{10,... | collective-permute-start | bytes 393224 | tf_op jit(solution)/shard_map/ppermute | solution.py:19
  13.0 9.3 %all-gather = bf16[8,64,256]{2,1,0:T(8,128)(2,1)S(1)} all-gather(bf16[2,64,256]{2,1,0:T(8,128)(2,1)S(1)} %shard_map.69), channel_id=2, replica_groups={{0,8,16,24},{4,12,20,28},{1,9,17,25},{5,13,21,29},{2,10,18,26},{6,14,22..., dimensions={0}, use_global_device_ids=true | all-gather | bytes 327680 | tf_op jit(solution)/shard_map/all_gather | solution.py:190
  22.3 1.5 %collective-permute-done.4.refs_5_ = bf16[4,2,64,256]{3,2,1,0:T(8,128)(2,1)S(1)} collective-permute-done((bf16[4,2,64,256]{3,2,1,0:T(8,128)(2,1)S(1)}, bf16[4,2,64,256]{3,2,1,0:T(8,128)(2,1)S(1)}, u32[]{:S(2)}, u32[]{:S(2)}) %collective-permute-start.4) | collective-permute-done | bytes 262176 | tf_op jit(solution)/shard_map/ppermute | solution.py:19
  23.8 1.4 %shard_map.70 = (bf16[4,2,64,256]{3,2,1,0:T(8,128)(2,1)S(1)}, f32[4,2,64,256]{3,2,1,0:T(8,128)S(1)}, f32[2,128,256]{2,1,0:T(8,128)S(1)}, bf16[2,128,256]{2,1,0:T...) custom-call(bf16[2,128,256]{2,1,0:T(8,128)(2,1)S(1)} %copy-done.1, ...), custom_call_target="tpu_custom_call" | custom-call | flops 805306368 | bytes 1048576 | tf_op jit(solution)/shard_map/pallas_call | solution.py:103
  25.5 2.7 %collective-permute-start.10 = (bf16[2,128,256]{2,1,0:T(8,128)(2,1)S(1)}, bf16[2,128,256]{2,1,0:T(8,128)(2,1)S(1)}, u32[]{:S(2)}, u32[]{:S(2)}) collective-permute-start(bf16[2,128,256]{2,1,0:T(8,128)(2,1)S(1)} %get-tuple-element.58), channel_id=1, source_target_pairs={{0,2},{1,3},{2,0},{3,1},{4,6},{5,7},{6,4},{7,5},{8,10},{9,11},{10,... | collective-permute-start | bytes 393224 | tf_op jit(solution)/shard_map/ppermute | solution.py:19
  28.3 1.5 %collective-permute-start.9 = (bf16[2,64,256]{2,1,0:T(8,128)(2,1)S(1)}, bf16[2,64,256]{2,1,0:T(8,128)(2,1)S(1)}, u32[]{:S(2)}, u32[]{:S(2)}) collective-permute-start(bf16[2,64,256]{2,1,0:T(8,128)(2,1)S(1)} %get-tuple-element.98), channel_id=1, source_target_pairs={{0,24},{4,28},{8,16},{12,20},{16,8},{20,12},{24,0},{28,4},{1,25},{... | collective-permute-start | bytes 196616 | tf_op jit(solution)/shard_map/ppermute | solution.py:19
  29.8 1.4 %collective-permute-start.8 = (bf16[2,64,256]{2,1,0:T(8,128)(2,1)S(1)}, bf16[2,64,256]{2,1,0:T(8,128)(2,1)S(1)}, u32[]{:S(2)}, u32[]{:S(2)}) collective-permute-start(bf16[2,64,256]{2,1,0:T(8,128)(2,1)S(1)} %get-tuple-element.99), channel_id=1, source_target_pairs={{0,16},{4,20},{8,24},{12,28},{16,0},{20,4},{24,8},{28,12},{1,17},{... | collective-permute-start | bytes 196616 | tf_op jit(solution)/shard_map/ppermute | solution.py:19
  31.9 3.2 %collective-permute-done.10 = bf16[2,128,256]{2,1,0:T(8,128)(2,1)S(1)} collective-permute-done((bf16[2,128,256]{2,1,0:T(8,128)(2,1)S(1)}, bf16[2,128,256]{2,1,0:T(8,128)(2,1)S(1)}, u32[]{:S(2)}, u32[]{:S(2)}) %collective-permute-start.10) | collective-permute-done | bytes 131104 | tf_op jit(solution)/shard_map/ppermute | solution.py:19
  35.0 1.8 %collective-permute-start.11 = (bf16[2,128,256]{2,1,0:T(8,128)(2,1)S(1)}, bf16[2,128,256]{2,1,0:T(8,128)(2,1)S(1)}, u32[]{:S(2)}, u32[]{:S(2)}) collective-permute-start(bf16[2,128,256]{2,1,0:T(8,128)(2,1)S(1)} %get-tuple-element.60), channel_id=1, source_target_pairs={{0,3},{1,2},{2,1},{3,0},{4,7},{5,6},{6,5},{7,4},{8,11},{9,10},{10,... | collective-permute-start | bytes 393224 | tf_op jit(solution)/shard_map/ppermute | solution.py:19
  36.9 2.0 %collective-permute-start.13 = (bf16[2,64,256]{2,1,0:T(8,128)(2,1)S(1)}, bf16[2,64,256]{2,1,0:T(8,128)(2,1)S(1)}, u32[]{:S(2)}, u32[]{:S(2)}) collective-permute-start(bf16[2,64,256]{2,1,0:T(8,128)(2,1)S(1)} %add_convert_fusion.3.w_own), channel_id=1, source_target_pairs={{0,3},{1,0},{2,1},{3,2},{4,7},{5,4},{6,5},{7,6},{8,11},{9,8},{10,9... | collective-permute-start | bytes 196616 | tf_op jit(solution)/shard_map/ppermute | solution.py:24
  39.0 4.1 %collective-permute-done.11 = bf16[2,128,256]{2,1,0:T(8,128)(2,1)S(1)} collective-permute-done((bf16[2,128,256]{2,1,0:T(8,128)(2,1)S(1)}, bf16[2,128,256]{2,1,0:T(8,128)(2,1)S(1)}, u32[]{:S(2)}, u32[]{:S(2)}) %collective-permute-start.11) | collective-permute-done | bytes 131104 | tf_op jit(solution)/shard_map/ppermute | solution.py:19
  43.2 1.4 %collective-permute-start.16 = (bf16[2,128,256]{2,1,0:T(8,128)(2,1)S(1)}, bf16[2,128,256]{2,1,0:T(8,128)(2,1)S(1)}, u32[]{:S(2)}, u32[]{:S(2)}) collective-permute-start(bf16[2,128,256]{2,1,0:T(8,128)(2,1)S(1)} %subtract_convert_fusion.refs_0_.left), channel_id=1, source_target_pairs={{0,3},{1,2},{2,1},{3,0},{4,7},{5,6},{6,5},{7,4},{8,11},{9,10},{10,... | collective-permute-start | bytes 393224 | tf_op jit(solution)/shard_map/ppermute | solution.py:19
  45.1 2.6 %collective-permute-start.14 = (bf16[2,128,256]{2,1,0:T(8,128)(2,1)S(1)}, bf16[2,128,256]{2,1,0:T(8,128)(2,1)S(1)}, u32[]{:S(2)}, u32[]{:S(2)}) collective-permute-start(bf16[2,128,256]{2,1,0:T(8,128)(2,1)S(1)} %subtract_convert_fusion.refs_0_.left), channel_id=1, source_target_pairs={{0,1},{1,0},{2,3},{3,2},{4,5},{5,4},{6,7},{7,6},{8,9},{9,8},{10,11... | collective-permute-start | bytes 393224 | tf_op jit(solution)/shard_map/ppermute | solution.py:19
  48.2 8.7 %all-gather.1 = bf16[8,64,256]{2,1,0:T(8,128)(2,1)S(1)} all-gather(bf16[2,64,256]{2,1,0:T(8,128)(2,1)S(1)} %get-tuple-element.73), channel_id=3, replica_groups={{0,8,16,24},{4,12,20,28},{1,9,17,25},{5,13,21,29},{2,10,18,26},{6,14,22..., dimensions={0}, use_global_device_ids=true | all-gather | bytes 327680 | tf_op jit(solution)/shard_map/all_gather | solution.py:190
  57.0 1.5 %collective-permute-done.17.refs_5_ = bf16[4,2,64,256]{3,2,1,0:T(8,128)(2,1)S(1)} collective-permute-done((bf16[4,2,64,256]{3,2,1,0:T(8,128)(2,1)S(1)}, bf16[4,2,64,256]{3,2,1,0:T(8,128)(2,1)S(1)}, u32[]{:S(2)}, u32[]{:S(2)}) %collective-permute-start.17) | collective-permute-done | bytes 262176 | tf_op jit(solution)/shard_map/ppermute | solution.py:19
  58.5 1.4 %shard_map.72 = (bf16[4,2,64,256]{3,2,1,0:T(8,128)(2,1)S(1)}, f32[4,2,64,256]{3,2,1,0:T(8,128)S(1)}, f32[2,128,256]{2,1,0:T(8,128)S(1)}, bf16[2,128,256]{2,1,0:T...) custom-call(bf16[2,128,256]{2,1,0:T(8,128)(2,1)S(1)} %subtract_convert_fusion.refs_0_.left, ...), custom_call_target="tpu_custom_call" | custom-call | flops 805306368 | bytes 1048576 | tf_op jit(solution)/shard_map/pallas_call | solution.py:103
  60.5 2.0 %collective-permute-start.23 = (bf16[2,128,256]{2,1,0:T(8,128)(2,1)S(1)}, bf16[2,128,256]{2,1,0:T(8,128)(2,1)S(1)}, u32[]{:S(2)}, u32[]{:S(2)}) collective-permute-start(bf16[2,128,256]{2,1,0:T(8,128)(2,1)S(1)} %get-tuple-element.83), channel_id=1, source_target_pairs={{0,2},{1,3},{2,0},{3,1},{4,6},{5,7},{6,4},{7,5},{8,10},{9,11},{10,... | collective-permute-start | bytes 393224 | tf_op jit(solution)/shard_map/ppermute | solution.py:19
  62.6 1.5 %collective-permute-start.21 = (bf16[2,64,256]{2,1,0:T(8,128)(2,1)S(1)}, bf16[2,64,256]{2,1,0:T(8,128)(2,1)S(1)}, u32[]{:S(2)}, u32[]{:S(2)}) collective-permute-start(bf16[2,64,256]{2,1,0:T(8,128)(2,1)S(1)} %get-tuple-element.94), channel_id=1, source_target_pairs={{0,24},{4,28},{8,16},{12,20},{16,8},{20,12},{24,0},{28,4},{1,25},{... | collective-permute-start | bytes 196616 | tf_op jit(solution)/shard_map/ppermute | solution.py:19
  64.1 1.9 %collective-permute-start.20 = (bf16[2,64,256]{2,1,0:T(8,128)(2,1)S(1)}, bf16[2,64,256]{2,1,0:T(8,128)(2,1)S(1)}, u32[]{:S(2)}, u32[]{:S(2)}) collective-permute-start(bf16[2,64,256]{2,1,0:T(8,128)(2,1)S(1)} %get-tuple-element.95), channel_id=1, source_target_pairs={{0,16},{4,20},{8,24},{12,28},{16,0},{20,4},{24,8},{28,12},{1,17},{... | collective-permute-start | bytes 196616 | tf_op jit(solution)/shard_map/ppermute | solution.py:19
  66.2 1.7 %collective-permute-done.22.refs_1_ = bf16[2,128,256]{2,1,0:T(8,128)(2,1)S(1)} collective-permute-done((bf16[2,128,256]{2,1,0:T(8,128)(2,1)S(1)}, bf16[2,128,256]{2,1,0:T(8,128)(2,1)S(1)}, u32[]{:S(2)}, u32[]{:S(2)}) %collective-permute-start.22) | collective-permute-done | bytes 131104 | tf_op jit(solution)/shard_map/ppermute | solution.py:19
  67.9 2.1 %collective-permute-start.25 = (bf16[2,128,256]{2,1,0:T(8,128)(2,1)S(1)}, bf16[2,128,256]{2,1,0:T(8,128)(2,1)S(1)}, u32[]{:S(2)}, u32[]{:S(2)}) collective-permute-start(bf16[2,128,256]{2,1,0:T(8,128)(2,1)S(1)} %get-tuple-element.91), channel_id=1, source_target_pairs={{0,3},{1,2},{2,1},{3,0},{4,7},{5,6},{6,5},{7,4},{8,11},{9,10},{10,... | collective-permute-start | bytes 393224 | tf_op jit(solution)/shard_map/ppermute | solution.py:19
  70.7 4.8 %collective-permute-done.25.refs_3_ = bf16[2,128,256]{2,1,0:T(8,128)(2,1)S(1)} collective-permute-done((bf16[2,128,256]{2,1,0:T(8,128)(2,1)S(1)}, bf16[2,128,256]{2,1,0:T(8,128)(2,1)S(1)}, u32[]{:S(2)}, u32[]{:S(2)}) %collective-permute-start.25) | collective-permute-done | bytes 131104 | tf_op jit(solution)/shard_map/ppermute | solution.py:19
  (63 shorter events, 7.5 us)
Async XLA Ops:
  0.6 7.9 %collective-permute-start = (bf16[2,64,256]{2,1,0:T(8,128)(2,1)}, bf16[2,64,256]{2,1,0:T(8,128)(2,1)S(1)}, u32[]{:S(2)}, u32[]{:S(2)}) collective-permute-start(bf16[2,64,256]{2,1,0:T(8,128)(2,1)} %right.3), channel_id=1, source_target_pairs={{0,3},{1,0},{2,1},{3,2},{4,7},{5,4},{6,5},{7,6},{8,11},{9,8},{10,9... | collective-permute-start | bytes 196616 | tf_op jit(solution)/shard_map/ppermute | solution.py:24
  5.7 16.5 %collective-permute-start.1 = (bf16[2,128,256]{2,1,0:T(8,128)(2,1)}, bf16[2,128,256]{2,1,0:T(8,128)(2,1)S(1)}, u32[]{:S(2)}, u32[]{:S(2)}) collective-permute-start(bf16[2,128,256]{2,1,0:T(8,128)(2,1)} %refs_0_), channel_id=1, source_target_pairs={{0,1},{1,0},{2,3},{3,2},{4,5},{5,4},{6,7},{7,6},{8,9},{9,8},{10,11... | collective-permute-start | bytes 393224 | tf_op jit(solution)/shard_map/ppermute | solution.py:19
  8.5 13.7 %collective-permute-start.3 = (bf16[2,128,256]{2,1,0:T(8,128)(2,1)S(1)}, bf16[2,128,256]{2,1,0:T(8,128)(2,1)S(1)}, u32[]{:S(2)}, u32[]{:S(2)}) collective-permute-start(bf16[2,128,256]{2,1,0:T(8,128)(2,1)S(1)} %copy-done.1), channel_id=1, source_target_pairs={{0,3},{1,2},{2,1},{3,0},{4,7},{5,6},{6,5},{7,4},{8,11},{9,10},{10,... | collective-permute-start | bytes 393224 | tf_op jit(solution)/shard_map/ppermute | solution.py:19
  12.7 9.5 %collective-permute-start.2 = (bf16[2,128,256]{2,1,0:T(8,128)(2,1)S(1)}, bf16[2,128,256]{2,1,0:T(8,128)(2,1)S(1)}, u32[]{:S(2)}, u32[]{:S(2)}) collective-permute-start(bf16[2,128,256]{2,1,0:T(8,128)(2,1)S(1)} %copy-done.1), channel_id=1, source_target_pairs={{0,2},{1,3},{2,0},{3,1},{4,6},{5,7},{6,4},{7,5},{8,10},{9,11},{10,... | collective-permute-start | bytes 393224 | tf_op jit(solution)/shard_map/ppermute | solution.py:19
  25.2 2.9 %collective-permute-start.6 = (bf16[4,2,64,256]{3,2,1,0:T(8,128)(2,1)S(1)}, bf16[4,2,64,256]{3,2,1,0:T(8,128)(2,1)S(1)}, u32[]{:S(2)}, u32[]{:S(2)}) collective-permute-start(bf16[4,2,64,256]{3,2,1,0:T(8,128)(2,1)S(1)} %get-tuple-element.57), channel_id=1, source_target_pairs={{0,4},{4,0},{8,12},{12,8},{16,20},{20,16},{24,28},{28,24},{1,5},{5... | collective-permute-start | bytes 786440 | tf_op jit(solution)/shard_map/ppermute | solution.py:19
  25.5 9.6 %collective-permute-start.10 = (bf16[2,128,256]{2,1,0:T(8,128)(2,1)S(1)}, bf16[2,128,256]{2,1,0:T(8,128)(2,1)S(1)}, u32[]{:S(2)}, u32[]{:S(2)}) collective-permute-start(bf16[2,128,256]{2,1,0:T(8,128)(2,1)S(1)} %get-tuple-element.58), channel_id=1, source_target_pairs={{0,2},{1,3},{2,0},{3,1},{4,6},{5,7},{6,4},{7,5},{8,10},{9,11},{10,... | collective-permute-start | bytes 393224 | tf_op jit(solution)/shard_map/ppermute | solution.py:19
  28.3 8.6 %collective-permute-start.9 = (bf16[2,64,256]{2,1,0:T(8,128)(2,1)S(1)}, bf16[2,64,256]{2,1,0:T(8,128)(2,1)S(1)}, u32[]{:S(2)}, u32[]{:S(2)}) collective-permute-start(bf16[2,64,256]{2,1,0:T(8,128)(2,1)S(1)} %get-tuple-element.98), channel_id=1, source_target_pairs={{0,24},{4,28},{8,16},{12,20},{16,8},{20,12},{24,0},{28,4},{1,25},{... | collective-permute-start | bytes 196616 | tf_op jit(solution)/shard_map/ppermute | solution.py:19
  29.8 7.0 %collective-permute-start.8 = (bf16[2,64,256]{2,1,0:T(8,128)(2,1)S(1)}, bf16[2,64,256]{2,1,0:T(8,128)(2,1)S(1)}, u32[]{:S(2)}, u32[]{:S(2)}) collective-permute-start(bf16[2,64,256]{2,1,0:T(8,128)(2,1)S(1)} %get-tuple-element.99), channel_id=1, source_target_pairs={{0,16},{4,20},{8,24},{12,28},{16,0},{20,4},{24,8},{28,12},{1,17},{... | collective-permute-start | bytes 196616 | tf_op jit(solution)/shard_map/ppermute | solution.py:19
  31.3 5.6 %collective-permute-start.7 = (bf16[2,64,256]{2,1,0:T(8,128)(2,1)S(1)}, bf16[2,64,256]{2,1,0:T(8,128)(2,1)S(1)}, u32[]{:S(2)}, u32[]{:S(2)}) collective-permute-start(bf16[2,64,256]{2,1,0:T(8,128)(2,1)S(1)} %get-tuple-element.100), channel_id=1, source_target_pairs={{0,8},{4,12},{8,0},{12,4},{16,24},{20,28},{24,16},{28,20},{1,9},{5... | collective-permute-start | bytes 196616 | tf_op jit(solution)/shard_map/ppermute | solution.py:19
  31.9 7.2 %collective-permute-start.5 = (bf16[2,128,256]{2,1,0:T(8,128)(2,1)S(1)}, bf16[2,128,256]{2,1,0:T(8,128)(2,1)S(1)}, u32[]{:S(2)}, u32[]{:S(2)}) collective-permute-start(bf16[2,128,256]{2,1,0:T(8,128)(2,1)S(1)} %get-tuple-element.55), channel_id=1, source_target_pairs={{0,1},{1,0},{2,3},{3,2},{4,5},{5,4},{6,7},{7,6},{8,9},{9,8},{10,11... | collective-permute-start | bytes 393224 | tf_op jit(solution)/shard_map/ppermute | solution.py:19
  35.0 8.1 %collective-permute-start.11 = (bf16[2,128,256]{2,1,0:T(8,128)(2,1)S(1)}, bf16[2,128,256]{2,1,0:T(8,128)(2,1)S(1)}, u32[]{:S(2)}, u32[]{:S(2)}) collective-permute-start(bf16[2,128,256]{2,1,0:T(8,128)(2,1)S(1)} %get-tuple-element.60), channel_id=1, source_target_pairs={{0,3},{1,2},{2,1},{3,0},{4,7},{5,6},{6,5},{7,4},{8,11},{9,10},{10,... | collective-permute-start | bytes 393224 | tf_op jit(solution)/shard_map/ppermute | solution.py:19
  36.9 7.6 %collective-permute-start.13 = (bf16[2,64,256]{2,1,0:T(8,128)(2,1)S(1)}, bf16[2,64,256]{2,1,0:T(8,128)(2,1)S(1)}, u32[]{:S(2)}, u32[]{:S(2)}) collective-permute-start(bf16[2,64,256]{2,1,0:T(8,128)(2,1)S(1)} %add_convert_fusion.3.w_own), channel_id=1, source_target_pairs={{0,3},{1,0},{2,1},{3,2},{4,7},{5,4},{6,5},{7,6},{8,11},{9,8},{10,9... | collective-permute-start | bytes 196616 | tf_op jit(solution)/shard_map/ppermute | solution.py:24
  39.0 6.1 %collective-permute-start.12 = (bf16[2,64,256]{2,1,0:T(8,128)(2,1)S(1)}, bf16[2,64,256]{2,1,0:T(8,128)(2,1)S(1)}, u32[]{:S(2)}, u32[]{:S(2)}) collective-permute-start(bf16[2,64,256]{2,1,0:T(8,128)(2,1)S(1)} %add_convert_fusion.3.w_own), channel_id=1, source_target_pairs={{0,1},{1,2},{2,3},{3,0},{4,5},{5,6},{6,7},{7,4},{8,9},{9,10},{10,1... | collective-permute-start | bytes 196616 | tf_op jit(solution)/shard_map/ppermute | solution.py:24
  43.2 13.7 %collective-permute-start.16 = (bf16[2,128,256]{2,1,0:T(8,128)(2,1)S(1)}, bf16[2,128,256]{2,1,0:T(8,128)(2,1)S(1)}, u32[]{:S(2)}, u32[]{:S(2)}) collective-permute-start(bf16[2,128,256]{2,1,0:T(8,128)(2,1)S(1)} %subtract_convert_fusion.refs_0_.left), channel_id=1, source_target_pairs={{0,3},{1,2},{2,1},{3,0},{4,7},{5,6},{6,5},{7,4},{8,11},{9,10},{10,... | collective-permute-start | bytes 393224 | tf_op jit(solution)/shard_map/ppermute | solution.py:19
  44.5 12.4 %collective-permute-start.15 = (bf16[2,128,256]{2,1,0:T(8,128)(2,1)S(1)}, bf16[2,128,256]{2,1,0:T(8,128)(2,1)S(1)}, u32[]{:S(2)}, u32[]{:S(2)}) collective-permute-start(bf16[2,128,256]{2,1,0:T(8,128)(2,1)S(1)} %subtract_convert_fusion.refs_0_.left), channel_id=1, source_target_pairs={{0,2},{1,3},{2,0},{3,1},{4,6},{5,7},{6,4},{7,5},{8,10},{9,11},{10,... | collective-permute-start | bytes 393224 | tf_op jit(solution)/shard_map/ppermute | solution.py:19
  45.1 11.8 %collective-permute-start.14 = (bf16[2,128,256]{2,1,0:T(8,128)(2,1)S(1)}, bf16[2,128,256]{2,1,0:T(8,128)(2,1)S(1)}, u32[]{:S(2)}, u32[]{:S(2)}) collective-permute-start(bf16[2,128,256]{2,1,0:T(8,128)(2,1)S(1)} %subtract_convert_fusion.refs_0_.left), channel_id=1, source_target_pairs={{0,1},{1,0},{2,3},{3,2},{4,5},{5,4},{6,7},{7,6},{8,9},{9,8},{10,11... | collective-permute-start | bytes 393224 | tf_op jit(solution)/shard_map/ppermute | solution.py:19
  59.9 2.6 %collective-permute-start.18 = (bf16[4,2,64,256]{3,2,1,0:T(8,128)(2,1)S(1)}, bf16[4,2,64,256]{3,2,1,0:T(8,128)(2,1)S(1)}, u32[]{:S(2)}, u32[]{:S(2)}) collective-permute-start(bf16[4,2,64,256]{3,2,1,0:T(8,128)(2,1)S(1)} %get-tuple-element.81), channel_id=1, source_target_pairs={{0,4},{4,0},{8,12},{12,8},{16,20},{20,16},{24,28},{28,24},{1,5},{5... | collective-permute-start | bytes 786440 | tf_op jit(solution)/shard_map/ppermute | solution.py:19
  60.2 7.7 %collective-permute-start.22 = (bf16[2,128,256]{2,1,0:T(8,128)(2,1)S(1)}, bf16[2,128,256]{2,1,0:T(8,128)(2,1)S(1)}, u32[]{:S(2)}, u32[]{:S(2)}) collective-permute-start(bf16[2,128,256]{2,1,0:T(8,128)(2,1)S(1)} %get-tuple-element.82), channel_id=1, source_target_pairs={{0,1},{1,0},{2,3},{3,2},{4,5},{5,4},{6,7},{7,6},{8,9},{9,8},{10,11... | collective-permute-start | bytes 393224 | tf_op jit(solution)/shard_map/ppermute | solution.py:19
  60.5 10.0 %collective-permute-start.23 = (bf16[2,128,256]{2,1,0:T(8,128)(2,1)S(1)}, bf16[2,128,256]{2,1,0:T(8,128)(2,1)S(1)}, u32[]{:S(2)}, u32[]{:S(2)}) collective-permute-start(bf16[2,128,256]{2,1,0:T(8,128)(2,1)S(1)} %get-tuple-element.83), channel_id=1, source_target_pairs={{0,2},{1,3},{2,0},{3,1},{4,6},{5,7},{6,4},{7,5},{8,10},{9,11},{10,... | collective-permute-start | bytes 393224 | tf_op jit(solution)/shard_map/ppermute | solution.py:19
  62.6 7.9 %collective-permute-start.21 = (bf16[2,64,256]{2,1,0:T(8,128)(2,1)S(1)}, bf16[2,64,256]{2,1,0:T(8,128)(2,1)S(1)}, u32[]{:S(2)}, u32[]{:S(2)}) collective-permute-start(bf16[2,64,256]{2,1,0:T(8,128)(2,1)S(1)} %get-tuple-element.94), channel_id=1, source_target_pairs={{0,24},{4,28},{8,16},{12,20},{16,8},{20,12},{24,0},{28,4},{1,25},{... | collective-permute-start | bytes 196616 | tf_op jit(solution)/shard_map/ppermute | solution.py:19
  64.1 6.4 %collective-permute-start.20 = (bf16[2,64,256]{2,1,0:T(8,128)(2,1)S(1)}, bf16[2,64,256]{2,1,0:T(8,128)(2,1)S(1)}, u32[]{:S(2)}, u32[]{:S(2)}) collective-permute-start(bf16[2,64,256]{2,1,0:T(8,128)(2,1)S(1)} %get-tuple-element.95), channel_id=1, source_target_pairs={{0,16},{4,20},{8,24},{12,28},{16,0},{20,4},{24,8},{28,12},{1,17},{... | collective-permute-start | bytes 196616 | tf_op jit(solution)/shard_map/ppermute | solution.py:19
  66.1 4.5 %collective-permute-start.19 = (bf16[2,64,256]{2,1,0:T(8,128)(2,1)S(1)}, bf16[2,64,256]{2,1,0:T(8,128)(2,1)S(1)}, u32[]{:S(2)}, u32[]{:S(2)}) collective-permute-start(bf16[2,64,256]{2,1,0:T(8,128)(2,1)S(1)} %get-tuple-element.96), channel_id=1, source_target_pairs={{0,8},{4,12},{8,0},{12,4},{16,24},{20,28},{24,16},{28,20},{1,9},{5... | collective-permute-start | bytes 196616 | tf_op jit(solution)/shard_map/ppermute | solution.py:19
  67.9 7.6 %collective-permute-start.25 = (bf16[2,128,256]{2,1,0:T(8,128)(2,1)S(1)}, bf16[2,128,256]{2,1,0:T(8,128)(2,1)S(1)}, u32[]{:S(2)}, u32[]{:S(2)}) collective-permute-start(bf16[2,128,256]{2,1,0:T(8,128)(2,1)S(1)} %get-tuple-element.91), channel_id=1, source_target_pairs={{0,3},{1,2},{2,1},{3,0},{4,7},{5,6},{6,5},{7,4},{8,11},{9,10},{10,... | collective-permute-start | bytes 393224 | tf_op jit(solution)/shard_map/ppermute | solution.py:19
  70.6 6.2 %collective-permute-start.24 = (bf16[2,64,256]{2,1,0:T(8,128)(2,1)S(1)}, bf16[2,64,256]{2,1,0:T(8,128)(2,1)S(1)}, u32[]{:S(2)}, u32[]{:S(2)}) collective-permute-start(bf16[2,64,256]{2,1,0:T(8,128)(2,1)S(1)} %add_convert_fusion.2.w_own), channel_id=1, source_target_pairs={{0,1},{1,2},{2,3},{3,0},{4,5},{5,6},{6,7},{7,4},{8,9},{9,10},{10,1... | collective-permute-start | bytes 196616 | tf_op jit(solution)/shard_map/ppermute | solution.py:24
  (7 other events, 24.2 us)

commit v6 on v5

--- a/solution.py
+++ b/solution.py
@@ -22,11 +22,6 @@
 def passed_along(shard, axis, by):
     size = lax.axis_size(axis)
     return lax.ppermute(shard, axis, [(i, (i + by) % size) for i in range(size)])
-
-
-def same_core():
-    size = lax.axis_size("row")
-    return [list(range(core, size, 2)) for core in range(2)]
 
 
 def gathered_left(shard, small, near_waits):
@@ -54,10 +49,10 @@
 
 def stage_kernel(cols, *refs):
     left_refs, refs = refs[:cols], refs[cols:]
-    q_own, q_other, rec, theirs, mine, *refs = refs
+    q, rec, theirs, mine, *refs = refs
     left_outs, (lbuf, qbuf, wbuf, gbuf) = refs[:cols], refs[cols:]
     me, core = lax.axis_index("col"), lax.axis_index("row") & 1
-    wide, narrow, chips = left_refs[0].shape[1], q_own.shape[2], q_own.shape[0]
+    wide, narrow, chips = left_refs[0].shape[1], q.shape[2], q.shape[0] // 2
 
     def left_rows(d):
         return pl.ds(pl.multiple_of((me ^ d) * wide, wide), wide)
@@ -67,9 +62,8 @@
 
     for d in range(cols):
         lbuf[:, left_rows(d), :] = left_refs[d][...]
-    for chip in range(chips):
-        qbuf[:, right_rows(chip, core), :] = q_own[chip]
-        qbuf[:, right_rows(chip, core ^ 1), :] = q_other[chip]
+    for device in range(2 * chips):
+        qbuf[:, device * narrow : (device + 1) * narrow, :] = q[device]
     br = dot(lbuf[0], qbuf[0], 0, 0) + dot(lbuf[1], qbuf[1], 0, 0) - rec[0].astype(F32)
     bi = dot(lbuf[1], qbuf[0], 0, 0) - dot(lbuf[0], qbuf[1], 0, 0) - rec[1].astype(F32)
     br, bi = br.astype(BF), bi.astype(BF)
@@ -84,14 +78,15 @@
         left_outs[d][...] = gbuf[:, left_rows(d), :].astype(left_outs[d].dtype)
 
 
-def stage(left_parts, q_own, q_other, rec):
+def stage(left_parts, q, rec):
     cols = len(left_parts)
     two, wide, rows = left_parts[0].shape
-    shots = q_own.shape[3]
+    devices, two, narrow, shots = q.shape
     rank = wide * cols
     part = jax.ShapeDtypeStruct((two, wide, rows), F32)
     sent = jax.ShapeDtypeStruct((two, wide, rows), BF)
-    outs = [jax.ShapeDtypeStruct(q_own.shape, BF), jax.ShapeDtypeStruct(q_own.shape, F32), part]
+    halves = (devices // 2, two, narrow, shots)
+    outs = [jax.ShapeDtypeStruct(halves, BF), jax.ShapeDtypeStruct(halves, F32), part]
     outs += [sent] * (cols - 1)
     scratch = [
         pltpu.VMEM((two, rank, rows), BF),
@@ -100,7 +95,7 @@
         pltpu.VMEM((two, rank, rows), F32),
     ]
     call = on_chip(functools.partial(stage_kernel, cols), outs, scratch, 24 * rank * rows * shots)
-    theirs, mine, *terms = call(*left_parts, q_own, q_other, rec)
+    theirs, mine, *terms = call(*left_parts, q, rec)
     return theirs, mine, terms
 
 
@@ -186,11 +181,6 @@
     table = jnp.stack([jnp.cos(theta), jnp.sin(theta)], axis=1).reshape(6, shots_dev)
     table = on_chip(table_kernel, jax.ShapeDtypeStruct(table.shape, F32), cost=1 << 30)(table)
 
-    def over_row(q, parts):
-        half = lax.all_gather(q, "row", axis=0, axis_index_groups=same_core())
-        half, parts = lax.optimization_barrier((half, parts))
-        return half, exchanged(half, "row", 1), parts
-
     shard = jax.ShapeDtypeStruct(right_factor.shape, BF)
     chip = lax.axis_index("row") >> 1
     left, right = left_factor, right_factor
@@ -198,16 +188,19 @@
     parts, right_next = gathered_left(left, right_next, False)
     q = on_chip(first_kernel, shard)(right, right_next, near, table)
     for step in range(ITERS):
-        q_own, q_other, parts = over_row(q, parts)
-        theirs, mine, terms = stage(parts, q_own, q_other, recorded)
+        q = lax.all_gather(q, "row", axis=0)
+        q, parts = lax.optimization_barrier((q, parts))
+        theirs, mine, terms = stage(parts, q, recorded)
         pair = (mine + exchanged(theirs, "row", 1).astype(F32)).astype(BF)
         sums = [lax.dynamic_index_in_dim(pair, chip, 0, False)]
         for d in range(1, pair.shape[0]):
             sent = lax.dynamic_index_in_dim(pair, chip ^ d, 0, False)
             sums.append(exchanged(sent, "row", 2 * d))
         terms = [terms[0]] + [exchanged(terms[d], "col", d) for d in range(1, blocks)]
-        early = slice(2, 3) if step + 1 < ITERS else slice(1, 3)
-        sums, terms[early] = lax.optimization_barrier((sums, terms[early]))
+        early = [d for d in ((1, 3) if step + 1 < ITERS else (1, 2)) if d < blocks]
+        sums, held = lax.optimization_barrier((sums, [terms[d] for d in early]))
+        for d, term in zip(early, held):
+            terms[d] = term
         w_own = sum(part.astype(F32) for part in sums).astype(BF)
         if step + 1 < ITERS:
             beside = [passed_along(w_own, "col", by) for by in (1, -1)]

time: 78 us -> 76 us (0.974)
  waiting for transfers between devices: 20.7 us -> 14.6 us
  starting transfers between devices: 32.1 us -> 34.5 us
  blocking collectives: 18 us -> 19.8 us
    ppermute x22 -> x20, waiting for transfers between devices: 17.3 us -> 12.4 us  [exchanged(): return lax.ppermute(shard, axis, [(i, i ^ flip) for i in range(size)])]
    ppermute x22 -> x20, starting transfers between devices: 24.8 us -> 27.1 us  [exchanged(): return lax.ppermute(shard, axis, [(i, i ^ flip) for i in range(size)])]
    all_gather x2, blocking collectives: 18 us -> 19.8 us  [on_device(): q = lax.all_gather(q, 'row', axis=0)]
    ppermute x4, waiting for transfers between devices: 3.4 us -> 2.22 us  [passed_along(): lax.ppermute(shard, axis, [(i, (i + by) % size) for i in range(size)])]
  transfers between devices with their start and end apart: 26 -> 24, of which waited for: 10 -> 8; matrix products, arithmetic and copies ran while one was open for 1% -> 1% of each run, Pallas kernels for 1% -> 1%
where the time goes in v6:
time: 76 us; the launch traced here: 75.8 us
  starting transfers between devices  34.5 us (45%)
  blocking collectives  19.8 us (26%)
  waiting for transfers between devices  14.6 us (19%)
  Pallas kernels  4.45 us (6%)
  local copies, waits for them, and re-layouts  0.87 us (1%)
  between operations  0.83 us (1%)
    ppermute x20, starting transfers between devices, exchanged(): return lax.ppermute(shard, axis, [(i, i ^ flip) for i in range(size)])  27.1 us
    all_gather x2, blocking collectives, on_device(): q = lax.all_gather(q, 'row', axis=0)  19.8 us
    ppermute x20, waiting for transfers between devices, exchanged(): return lax.ppermute(shard, axis, [(i, i ^ flip) for i in range(size)])  12.4 us
    ppermute x4, starting transfers between devices, passed_along(): lax.ppermute(shard, axis, [(i, (i + by) % size) for i in range(size)])  7.42 us
    pallas_call x2, Pallas kernels, stage(): theirs, mine, *terms = call(*left_parts, q, rec)  2.74 us
    ppermute x4, waiting for transfers between devices, passed_along(): lax.ppermute(shard, axis, [(i, (i + by) % size) for i in range(size)])  2.22 us
  transfers between devices with their start and end apart: 24, of which 8 were waited for; matrix products, arithmetic and copies ran while one was open for 1% of the time, Pallas kernels for 1%

profile of v6, /device:TPU:0, one launch (start us, length us, event | category | flops | bytes accessed | tf_op | source)
XLA Modules:
  0.0 75.8 jit_solution(14243668888502661839)
XLA Ops:
  0.6 5.1 %collective-permute-start = (bf16[2,64,256]{2,1,0:T(8,128)(2,1)}, bf16[2,64,256]{2,1,0:T(8,128)(2,1)S(1)}, u32[]{:S(2)}, u32[]{:S(2)}) collective-permute-start(bf16[2,64,256]{2,1,0:T(8,128)(2,1)} %right.3), channel_id=1, source_target_pairs={{0,3},{1,0},{2,1},{3,2},{4,7},{5,4},{6,5},{7,6},{8,11},{9,8},{10,9... | collective-permute-start | bytes 196616 | tf_op jit(solution)/shard_map/ppermute | solution.py:24
  7.0 1.5 %collective-permute-done.right_next = bf16[2,64,256]{2,1,0:T(8,128)(2,1)S(1)} collective-permute-done((bf16[2,64,256]{2,1,0:T(8,128)(2,1)}, bf16[2,64,256]{2,1,0:T(8,128)(2,1)S(1)}, u32[]{:S(2)}, u32[]{:S(2)}) %collective-permute-start) | collective-permute-done | bytes 65568 | tf_op jit(solution)/shard_map/ppermute | solution.py:24
  8.5 4.2 %collective-permute-start.3 = (bf16[2,128,256]{2,1,0:T(8,128)(2,1)S(1)}, bf16[2,128,256]{2,1,0:T(8,128)(2,1)S(1)}, u32[]{:S(2)}, u32[]{:S(2)}) collective-permute-start(bf16[2,128,256]{2,1,0:T(8,128)(2,1)S(1)} %copy-done.1), channel_id=1, source_target_pairs={{0,3},{1,2},{2,1},{3,0},{4,7},{5,6},{6,5},{7,4},{8,11},{9,10},{10,... | collective-permute-start | bytes 393224 | tf_op jit(solution)/shard_map/ppermute | solution.py:19
  13.0 10.0 %all-gather = bf16[16,64,256]{2,1,0:T(8,128)(2,1)S(1)} all-gather(bf16[2,64,256]{2,1,0:T(8,128)(2,1)S(1)} %shard_map.69), channel_id=2, replica_groups=mesh['row'=8,'col'=4] {'row'}, dimensions={0}, use_global_device_ids=true | all-gather | bytes 589824 | tf_op jit(solution)/shard_map/all_gather | solution.py:191
  23.0 1.4 %shard_map.70 = (bf16[4,2,64,256]{3,2,1,0:T(8,128)(2,1)S(1)}, f32[4,2,64,256]{3,2,1,0:T(8,128)S(1)}, f32[2,128,256]{2,1,0:T(8,128)S(1)}, bf16[2,128,256]{2,1,0:T...) custom-call(bf16[2,128,256]{2,1,0:T(8,128)(2,1)S(1)} %copy-done.1, ...), custom_call_target="tpu_custom_call" | custom-call | flops 805306368 | bytes 1048576 | tf_op jit(solution)/shard_map/pallas_call | solution.py:98
  25.4 3.8 %collective-permute-start.9 = (bf16[2,128,256]{2,1,0:T(8,128)(2,1)S(1)}, bf16[2,128,256]{2,1,0:T(8,128)(2,1)S(1)}, u32[]{:S(2)}, u32[]{:S(2)}) collective-permute-start(bf16[2,128,256]{2,1,0:T(8,128)(2,1)S(1)} %get-tuple-element.59), channel_id=1, source_target_pairs={{0,3},{1,2},{2,1},{3,0},{4,7},{5,6},{6,5},{7,4},{8,11},{9,10},{10,... | collective-permute-start | bytes 393224 | tf_op jit(solution)/shard_map/ppermute | solution.py:19
  29.3 1.5 %collective-permute-start.7 = (bf16[2,64,256]{2,1,0:T(8,128)(2,1)S(1)}, bf16[2,64,256]{2,1,0:T(8,128)(2,1)S(1)}, u32[]{:S(2)}, u32[]{:S(2)}) collective-permute-start(bf16[2,64,256]{2,1,0:T(8,128)(2,1)S(1)} %get-tuple-element.100), channel_id=1, source_target_pairs={{0,24},{4,28},{8,16},{12,20},{16,8},{20,12},{24,0},{28,4},{1,25},{... | collective-permute-start | bytes 196616 | tf_op jit(solution)/shard_map/ppermute | solution.py:19
  30.8 1.5 %collective-permute-start.6 = (bf16[2,64,256]{2,1,0:T(8,128)(2,1)S(1)}, bf16[2,64,256]{2,1,0:T(8,128)(2,1)S(1)}, u32[]{:S(2)}, u32[]{:S(2)}) collective-permute-start(bf16[2,64,256]{2,1,0:T(8,128)(2,1)S(1)} %get-tuple-element.101), channel_id=1, source_target_pairs={{0,16},{4,20},{8,24},{12,28},{16,0},{20,4},{24,8},{28,12},{1,17},{... | collective-permute-start | bytes 196616 | tf_op jit(solution)/shard_map/ppermute | solution.py:19
  32.9 1.2 %collective-permute-start.10 = (bf16[2,128,256]{2,1,0:T(8,128)(2,1)S(1)}, bf16[2,128,256]{2,1,0:T(8,128)(2,1)S(1)}, u32[]{:S(2)}, u32[]{:S(2)}) collective-permute-start(bf16[2,128,256]{2,1,0:T(8,128)(2,1)S(1)} %get-tuple-element.61), channel_id=1, source_target_pairs={{0,2},{1,3},{2,0},{3,1},{4,6},{5,7},{6,4},{7,5},{8,10},{9,11},{10,... | collective-permute-start | bytes 393224 | tf_op jit(solution)/shard_map/ppermute | solution.py:19
  34.1 2.3 %collective-permute-done.9 = bf16[2,128,256]{2,1,0:T(8,128)(2,1)S(1)} collective-permute-done((bf16[2,128,256]{2,1,0:T(8,128)(2,1)S(1)}, bf16[2,128,256]{2,1,0:T(8,128)(2,1)S(1)}, u32[]{:S(2)}, u32[]{:S(2)}) %collective-permute-start.9) | collective-permute-done | bytes 131104 | tf_op jit(solution)/shard_map/ppermute | solution.py:19
  36.7 2.0 %collective-permute-start.11 = (bf16[2,64,256]{2,1,0:T(8,128)(2,1)S(1)}, bf16[2,64,256]{2,1,0:T(8,128)(2,1)S(1)}, u32[]{:S(2)}, u32[]{:S(2)}) collective-permute-start(bf16[2,64,256]{2,1,0:T(8,128)(2,1)S(1)} %add_convert_fusion.3.w_own), channel_id=1, source_target_pairs={{0,1},{1,2},{2,3},{3,0},{4,5},{5,6},{6,7},{7,4},{8,9},{9,10},{10,1... | collective-permute-start | bytes 196616 | tf_op jit(solution)/shard_map/ppermute | solution.py:24
  38.7 3.2 %collective-permute-done.10 = bf16[2,128,256]{2,1,0:T(8,128)(2,1)S(1)} collective-permute-done((bf16[2,128,256]{2,1,0:T(8,128)(2,1)S(1)}, bf16[2,128,256]{2,1,0:T(8,128)(2,1)S(1)}, u32[]{:S(2)}, u32[]{:S(2)}) %collective-permute-start.10) | collective-permute-done | bytes 131104 | tf_op jit(solution)/shard_map/ppermute | solution.py:19
  42.1 2.8 %collective-permute-start.15 = (bf16[2,128,256]{2,1,0:T(8,128)(2,1)S(1)}, bf16[2,128,256]{2,1,0:T(8,128)(2,1)S(1)}, u32[]{:S(2)}, u32[]{:S(2)}) collective-permute-start(bf16[2,128,256]{2,1,0:T(8,128)(2,1)S(1)} %subtract_convert_fusion.refs_0_.left), channel_id=1, source_target_pairs={{0,3},{1,2},{2,1},{3,0},{4,7},{5,6},{6,5},{7,4},{8,11},{9,10},{10,... | collective-permute-start | bytes 393224 | tf_op jit(solution)/shard_map/ppermute | solution.py:19
  44.8 1.7 %collective-permute-start.13 = (bf16[2,128,256]{2,1,0:T(8,128)(2,1)S(1)}, bf16[2,128,256]{2,1,0:T(8,128)(2,1)S(1)}, u32[]{:S(2)}, u32[]{:S(2)}) collective-permute-start(bf16[2,128,256]{2,1,0:T(8,128)(2,1)S(1)} %subtract_convert_fusion.refs_0_.left), channel_id=1, source_target_pairs={{0,1},{1,0},{2,3},{3,2},{4,5},{5,4},{6,7},{7,6},{8,9},{9,8},{10,11... | collective-permute-start | bytes 393224 | tf_op jit(solution)/shard_map/ppermute | solution.py:19
  47.0 9.8 %all-gather.1 = bf16[16,64,256]{2,1,0:T(8,128)(2,1)S(1)} all-gather(bf16[2,64,256]{2,1,0:T(8,128)(2,1)S(1)} %get-tuple-element.75), channel_id=3, replica_groups=mesh['row'=8,'col'=4] {'row'}, dimensions={0}, use_global_device_ids=true | all-gather | bytes 589824 | tf_op jit(solution)/shard_map/all_gather | solution.py:191
  56.9 1.4 %shard_map.72 = (bf16[4,2,64,256]{3,2,1,0:T(8,128)(2,1)S(1)}, f32[4,2,64,256]{3,2,1,0:T(8,128)S(1)}, f32[2,128,256]{2,1,0:T(8,128)S(1)}, bf16[2,128,256]{2,1,0:T...) custom-call(bf16[2,128,256]{2,1,0:T(8,128)(2,1)S(1)} %subtract_convert_fusion.refs_0_.left, ...), custom_call_target="tpu_custom_call" | custom-call | flops 805306368 | bytes 1048576 | tf_op jit(solution)/shard_map/pallas_call | solution.py:98
  59.1 2.9 %collective-permute-start.21 = (bf16[2,128,256]{2,1,0:T(8,128)(2,1)S(1)}, bf16[2,128,256]{2,1,0:T(8,128)(2,1)S(1)}, u32[]{:S(2)}, u32[]{:S(2)}) collective-permute-start(bf16[2,128,256]{2,1,0:T(8,128)(2,1)S(1)} %get-tuple-element.85), channel_id=1, source_target_pairs={{0,2},{1,3},{2,0},{3,1},{4,6},{5,7},{6,4},{7,5},{8,10},{9,11},{10,... | collective-permute-start | bytes 393224 | tf_op jit(solution)/shard_map/ppermute | solution.py:19
  62.1 1.5 %collective-permute-start.19 = (bf16[2,64,256]{2,1,0:T(8,128)(2,1)S(1)}, bf16[2,64,256]{2,1,0:T(8,128)(2,1)S(1)}, u32[]{:S(2)}, u32[]{:S(2)}) collective-permute-start(bf16[2,64,256]{2,1,0:T(8,128)(2,1)S(1)} %get-tuple-element.96), channel_id=1, source_target_pairs={{0,24},{4,28},{8,16},{12,20},{16,8},{20,12},{24,0},{28,4},{1,25},{... | collective-permute-start | bytes 196616 | tf_op jit(solution)/shard_map/ppermute | solution.py:19
  64.2 1.5 %collective-permute-start.17 = (bf16[2,64,256]{2,1,0:T(8,128)(2,1)S(1)}, bf16[2,64,256]{2,1,0:T(8,128)(2,1)S(1)}, u32[]{:S(2)}, u32[]{:S(2)}) collective-permute-start(bf16[2,64,256]{2,1,0:T(8,128)(2,1)S(1)} %get-tuple-element.98), channel_id=1, source_target_pairs={{0,8},{4,12},{8,0},{12,4},{16,24},{20,28},{24,16},{28,20},{1,9},{5... | collective-permute-start | bytes 196616 | tf_op jit(solution)/shard_map/ppermute | solution.py:19
  65.6 1.1 %collective-permute-done.20.refs_1_ = bf16[2,128,256]{2,1,0:T(8,128)(2,1)S(1)} collective-permute-done((bf16[2,128,256]{2,1,0:T(8,128)(2,1)S(1)}, bf16[2,128,256]{2,1,0:T(8,128)(2,1)S(1)}, u32[]{:S(2)}, u32[]{:S(2)}) %collective-permute-start.20) | collective-permute-done | bytes 131104 | tf_op jit(solution)/shard_map/ppermute | solution.py:19
  66.8 1.6 %collective-permute-start.23 = (bf16[2,128,256]{2,1,0:T(8,128)(2,1)S(1)}, bf16[2,128,256]{2,1,0:T(8,128)(2,1)S(1)}, u32[]{:S(2)}, u32[]{:S(2)}) collective-permute-start(bf16[2,128,256]{2,1,0:T(8,128)(2,1)S(1)} %get-tuple-element.93), channel_id=1, source_target_pairs={{0,3},{1,2},{2,1},{3,0},{4,7},{5,6},{6,5},{7,4},{8,11},{9,10},{10,... | collective-permute-start | bytes 393224 | tf_op jit(solution)/shard_map/ppermute | solution.py:19
  68.8 5.3 %collective-permute-done.23.refs_3_ = bf16[2,128,256]{2,1,0:T(8,128)(2,1)S(1)} collective-permute-done((bf16[2,128,256]{2,1,0:T(8,128)(2,1)S(1)}, bf16[2,128,256]{2,1,0:T(8,128)(2,1)S(1)}, u32[]{:S(2)}, u32[]{:S(2)}) %collective-permute-start.23) | collective-permute-done | bytes 131104 | tf_op jit(solution)/shard_map/ppermute | solution.py:19
  74.1 0.7 collective-permute-done.22.w_prev
  74.8 1.0 %shard_map.73 = (bf16[2,128,256]{2,1,0:T(8,128)(2,1)}, bf16[2,64,256]{2,1,0:T(8,128)(2,1)}) custom-call(bf16[2,64,256]{2,1,0:T(8,128)(2,1)S(1)} %get-tuple-element.74.right, bf16[2,64,256]{2,1,0:T(8,128)(2,1)S(1)} %collective-permute-done.22.w_prev, bf16[2,64,256]{2,1,0:T(8,128)(2,1)S(1)} %add_convert_fusion.2.w_own, s32[3,256]{1,0:T(4,128)S(1)} %pad_add_fusion.near, ...), custom_call_target="tpu_custom_call" | custom-call | flops 1048576 | bytes 1048576 | tf_op jit(solution)/shard_map/pallas_call | solution.py:215
  (59 shorter events, 5.9 us)
Async XLA Ops:
  0.6 7.9 %collective-permute-start = (bf16[2,64,256]{2,1,0:T(8,128)(2,1)}, bf16[2,64,256]{2,1,0:T(8,128)(2,1)S(1)}, u32[]{:S(2)}, u32[]{:S(2)}) collective-permute-start(bf16[2,64,256]{2,1,0:T(8,128)(2,1)} %right.3), channel_id=1, source_target_pairs={{0,3},{1,0},{2,1},{3,2},{4,7},{5,4},{6,5},{7,6},{8,11},{9,8},{10,9... | collective-permute-start | bytes 196616 | tf_op jit(solution)/shard_map/ppermute | solution.py:24
  5.7 17.2 %collective-permute-start.1 = (bf16[2,128,256]{2,1,0:T(8,128)(2,1)}, bf16[2,128,256]{2,1,0:T(8,128)(2,1)S(1)}, u32[]{:S(2)}, u32[]{:S(2)}) collective-permute-start(bf16[2,128,256]{2,1,0:T(8,128)(2,1)} %refs_0_), channel_id=1, source_target_pairs={{0,1},{1,0},{2,3},{3,2},{4,5},{5,4},{6,7},{7,6},{8,9},{9,8},{10,11... | collective-permute-start | bytes 393224 | tf_op jit(solution)/shard_map/ppermute | solution.py:19
  8.5 14.4 %collective-permute-start.3 = (bf16[2,128,256]{2,1,0:T(8,128)(2,1)S(1)}, bf16[2,128,256]{2,1,0:T(8,128)(2,1)S(1)}, u32[]{:S(2)}, u32[]{:S(2)}) collective-permute-start(bf16[2,128,256]{2,1,0:T(8,128)(2,1)S(1)} %copy-done.1), channel_id=1, source_target_pairs={{0,3},{1,2},{2,1},{3,0},{4,7},{5,6},{6,5},{7,4},{8,11},{9,10},{10,... | collective-permute-start | bytes 393224 | tf_op jit(solution)/shard_map/ppermute | solution.py:19
  12.7 10.2 %collective-permute-start.2 = (bf16[2,128,256]{2,1,0:T(8,128)(2,1)S(1)}, bf16[2,128,256]{2,1,0:T(8,128)(2,1)S(1)}, u32[]{:S(2)}, u32[]{:S(2)}) collective-permute-start(bf16[2,128,256]{2,1,0:T(8,128)(2,1)S(1)} %copy-done.1), channel_id=1, source_target_pairs={{0,2},{1,3},{2,0},{3,1},{4,6},{5,7},{6,4},{7,5},{8,10},{9,11},{10,... | collective-permute-start | bytes 393224 | tf_op jit(solution)/shard_map/ppermute | solution.py:19
  24.4 4.8 %collective-permute-start.4 = (bf16[4,2,64,256]{3,2,1,0:T(8,128)(2,1)S(1)}, bf16[4,2,64,256]{3,2,1,0:T(8,128)(2,1)S(1)}, u32[]{:S(2)}, u32[]{:S(2)}) collective-permute-start(bf16[4,2,64,256]{3,2,1,0:T(8,128)(2,1)S(1)} %get-tuple-element.57), channel_id=1, source_target_pairs={{0,4},{4,0},{8,12},{12,8},{16,20},{20,16},{24,28},{28,24},{1,5},{5... | collective-permute-start | bytes 786440 | tf_op jit(solution)/shard_map/ppermute | solution.py:19
  24.8 8.1 %collective-permute-start.8 = (bf16[2,128,256]{2,1,0:T(8,128)(2,1)S(1)}, bf16[2,128,256]{2,1,0:T(8,128)(2,1)S(1)}, u32[]{:S(2)}, u32[]{:S(2)}) collective-permute-start(bf16[2,128,256]{2,1,0:T(8,128)(2,1)S(1)} %get-tuple-element.58), channel_id=1, source_target_pairs={{0,1},{1,0},{2,3},{3,2},{4,5},{5,4},{6,7},{7,6},{8,9},{9,8},{10,11... | collective-permute-start | bytes 393224 | tf_op jit(solution)/shard_map/ppermute | solution.py:19
  25.4 11.0 %collective-permute-start.9 = (bf16[2,128,256]{2,1,0:T(8,128)(2,1)S(1)}, bf16[2,128,256]{2,1,0:T(8,128)(2,1)S(1)}, u32[]{:S(2)}, u32[]{:S(2)}) collective-permute-start(bf16[2,128,256]{2,1,0:T(8,128)(2,1)S(1)} %get-tuple-element.59), channel_id=1, source_target_pairs={{0,3},{1,2},{2,1},{3,0},{4,7},{5,6},{6,5},{7,4},{8,11},{9,10},{10,... | collective-permute-start | bytes 393224 | tf_op jit(solution)/shard_map/ppermute | solution.py:19
  29.3 7.1 %collective-permute-start.7 = (bf16[2,64,256]{2,1,0:T(8,128)(2,1)S(1)}, bf16[2,64,256]{2,1,0:T(8,128)(2,1)S(1)}, u32[]{:S(2)}, u32[]{:S(2)}) collective-permute-start(bf16[2,64,256]{2,1,0:T(8,128)(2,1)S(1)} %get-tuple-element.100), channel_id=1, source_target_pairs={{0,24},{4,28},{8,16},{12,20},{16,8},{20,12},{24,0},{28,4},{1,25},{... | collective-permute-start | bytes 196616 | tf_op jit(solution)/shard_map/ppermute | solution.py:19
  30.8 5.6 %collective-permute-start.6 = (bf16[2,64,256]{2,1,0:T(8,128)(2,1)S(1)}, bf16[2,64,256]{2,1,0:T(8,128)(2,1)S(1)}, u32[]{:S(2)}, u32[]{:S(2)}) collective-permute-start(bf16[2,64,256]{2,1,0:T(8,128)(2,1)S(1)} %get-tuple-element.101), channel_id=1, source_target_pairs={{0,16},{4,20},{8,24},{12,28},{16,0},{20,4},{24,8},{28,12},{1,17},{... | collective-permute-start | bytes 196616 | tf_op jit(solution)/shard_map/ppermute | solution.py:19
  32.3 4.3 %collective-permute-start.5 = (bf16[2,64,256]{2,1,0:T(8,128)(2,1)S(1)}, bf16[2,64,256]{2,1,0:T(8,128)(2,1)S(1)}, u32[]{:S(2)}, u32[]{:S(2)}) collective-permute-start(bf16[2,64,256]{2,1,0:T(8,128)(2,1)S(1)} %get-tuple-element.102), channel_id=1, source_target_pairs={{0,8},{4,12},{8,0},{12,4},{16,24},{20,28},{24,16},{28,20},{1,9},{5... | collective-permute-start | bytes 196616 | tf_op jit(solution)/shard_map/ppermute | solution.py:19
  32.9 9.1 %collective-permute-start.10 = (bf16[2,128,256]{2,1,0:T(8,128)(2,1)S(1)}, bf16[2,128,256]{2,1,0:T(8,128)(2,1)S(1)}, u32[]{:S(2)}, u32[]{:S(2)}) collective-permute-start(bf16[2,128,256]{2,1,0:T(8,128)(2,1)S(1)} %get-tuple-element.61), channel_id=1, source_target_pairs={{0,2},{1,3},{2,0},{3,1},{4,6},{5,7},{6,4},{7,5},{8,10},{9,11},{10,... | collective-permute-start | bytes 393224 | tf_op jit(solution)/shard_map/ppermute | solution.py:19
  36.6 8.2 %collective-permute-start.12 = (bf16[2,64,256]{2,1,0:T(8,128)(2,1)S(1)}, bf16[2,64,256]{2,1,0:T(8,128)(2,1)S(1)}, u32[]{:S(2)}, u32[]{:S(2)}) collective-permute-start(bf16[2,64,256]{2,1,0:T(8,128)(2,1)S(1)} %add_convert_fusion.3.w_own), channel_id=1, source_target_pairs={{0,3},{1,0},{2,1},{3,2},{4,7},{5,4},{6,5},{7,6},{8,11},{9,8},{10,9... | collective-permute-start | bytes 196616 | tf_op jit(solution)/shard_map/ppermute | solution.py:24
  36.7 8.1 %collective-permute-start.11 = (bf16[2,64,256]{2,1,0:T(8,128)(2,1)S(1)}, bf16[2,64,256]{2,1,0:T(8,128)(2,1)S(1)}, u32[]{:S(2)}, u32[]{:S(2)}) collective-permute-start(bf16[2,64,256]{2,1,0:T(8,128)(2,1)S(1)} %add_convert_fusion.3.w_own), channel_id=1, source_target_pairs={{0,1},{1,2},{2,3},{3,0},{4,5},{5,6},{6,7},{7,4},{8,9},{9,10},{10,1... | collective-permute-start | bytes 196616 | tf_op jit(solution)/shard_map/ppermute | solution.py:24
  42.1 14.8 %collective-permute-start.15 = (bf16[2,128,256]{2,1,0:T(8,128)(2,1)S(1)}, bf16[2,128,256]{2,1,0:T(8,128)(2,1)S(1)}, u32[]{:S(2)}, u32[]{:S(2)}) collective-permute-start(bf16[2,128,256]{2,1,0:T(8,128)(2,1)S(1)} %subtract_convert_fusion.refs_0_.left), channel_id=1, source_target_pairs={{0,3},{1,2},{2,1},{3,0},{4,7},{5,6},{6,5},{7,4},{8,11},{9,10},{10,... | collective-permute-start | bytes 393224 | tf_op jit(solution)/shard_map/ppermute | solution.py:19
  44.8 12.0 %collective-permute-start.14 = (bf16[2,128,256]{2,1,0:T(8,128)(2,1)S(1)}, bf16[2,128,256]{2,1,0:T(8,128)(2,1)S(1)}, u32[]{:S(2)}, u32[]{:S(2)}) collective-permute-start(bf16[2,128,256]{2,1,0:T(8,128)(2,1)S(1)} %subtract_convert_fusion.refs_0_.left), channel_id=1, source_target_pairs={{0,2},{1,3},{2,0},{3,1},{4,6},{5,7},{6,4},{7,5},{8,10},{9,11},{10,... | collective-permute-start | bytes 393224 | tf_op jit(solution)/shard_map/ppermute | solution.py:19
  44.8 12.0 %collective-permute-start.13 = (bf16[2,128,256]{2,1,0:T(8,128)(2,1)S(1)}, bf16[2,128,256]{2,1,0:T(8,128)(2,1)S(1)}, u32[]{:S(2)}, u32[]{:S(2)}) collective-permute-start(bf16[2,128,256]{2,1,0:T(8,128)(2,1)S(1)} %subtract_convert_fusion.refs_0_.left), channel_id=1, source_target_pairs={{0,1},{1,0},{2,3},{3,2},{4,5},{5,4},{6,7},{7,6},{8,9},{9,8},{10,11... | collective-permute-start | bytes 393224 | tf_op jit(solution)/shard_map/ppermute | solution.py:19
  58.2 3.7 %collective-permute-start.16 = (bf16[4,2,64,256]{3,2,1,0:T(8,128)(2,1)S(1)}, bf16[4,2,64,256]{3,2,1,0:T(8,128)(2,1)S(1)}, u32[]{:S(2)}, u32[]{:S(2)}) collective-permute-start(bf16[4,2,64,256]{3,2,1,0:T(8,128)(2,1)S(1)} %get-tuple-element.83), channel_id=1, source_target_pairs={{0,4},{4,0},{8,12},{12,8},{16,20},{20,16},{24,28},{28,24},{1,5},{5... | collective-permute-start | bytes 786440 | tf_op jit(solution)/shard_map/ppermute | solution.py:19
  58.7 8.1 %collective-permute-start.20 = (bf16[2,128,256]{2,1,0:T(8,128)(2,1)S(1)}, bf16[2,128,256]{2,1,0:T(8,128)(2,1)S(1)}, u32[]{:S(2)}, u32[]{:S(2)}) collective-permute-start(bf16[2,128,256]{2,1,0:T(8,128)(2,1)S(1)} %get-tuple-element.84), channel_id=1, source_target_pairs={{0,1},{1,0},{2,3},{3,2},{4,5},{5,4},{6,7},{7,6},{8,9},{9,8},{10,11... | collective-permute-start | bytes 393224 | tf_op jit(solution)/shard_map/ppermute | solution.py:19
  59.1 9.4 %collective-permute-start.21 = (bf16[2,128,256]{2,1,0:T(8,128)(2,1)S(1)}, bf16[2,128,256]{2,1,0:T(8,128)(2,1)S(1)}, u32[]{:S(2)}, u32[]{:S(2)}) collective-permute-start(bf16[2,128,256]{2,1,0:T(8,128)(2,1)S(1)} %get-tuple-element.85), channel_id=1, source_target_pairs={{0,2},{1,3},{2,0},{3,1},{4,6},{5,7},{6,4},{7,5},{8,10},{9,11},{10,... | collective-permute-start | bytes 393224 | tf_op jit(solution)/shard_map/ppermute | solution.py:19
  62.1 6.4 %collective-permute-start.19 = (bf16[2,64,256]{2,1,0:T(8,128)(2,1)S(1)}, bf16[2,64,256]{2,1,0:T(8,128)(2,1)S(1)}, u32[]{:S(2)}, u32[]{:S(2)}) collective-permute-start(bf16[2,64,256]{2,1,0:T(8,128)(2,1)S(1)} %get-tuple-element.96), channel_id=1, source_target_pairs={{0,24},{4,28},{8,16},{12,20},{16,8},{20,12},{24,0},{28,4},{1,25},{... | collective-permute-start | bytes 196616 | tf_op jit(solution)/shard_map/ppermute | solution.py:19
  63.6 4.9 %collective-permute-start.18 = (bf16[2,64,256]{2,1,0:T(8,128)(2,1)S(1)}, bf16[2,64,256]{2,1,0:T(8,128)(2,1)S(1)}, u32[]{:S(2)}, u32[]{:S(2)}) collective-permute-start(bf16[2,64,256]{2,1,0:T(8,128)(2,1)S(1)} %get-tuple-element.97), channel_id=1, source_target_pairs={{0,16},{4,20},{8,24},{12,28},{16,0},{20,4},{24,8},{28,12},{1,17},{... | collective-permute-start | bytes 196616 | tf_op jit(solution)/shard_map/ppermute | solution.py:19
  64.2 4.3 %collective-permute-start.17 = (bf16[2,64,256]{2,1,0:T(8,128)(2,1)S(1)}, bf16[2,64,256]{2,1,0:T(8,128)(2,1)S(1)}, u32[]{:S(2)}, u32[]{:S(2)}) collective-permute-start(bf16[2,64,256]{2,1,0:T(8,128)(2,1)S(1)} %get-tuple-element.98), channel_id=1, source_target_pairs={{0,8},{4,12},{8,0},{12,4},{16,24},{20,28},{24,16},{28,20},{1,9},{5... | collective-permute-start | bytes 196616 | tf_op jit(solution)/shard_map/ppermute | solution.py:19
  66.8 7.3 %collective-permute-start.23 = (bf16[2,128,256]{2,1,0:T(8,128)(2,1)S(1)}, bf16[2,128,256]{2,1,0:T(8,128)(2,1)S(1)}, u32[]{:S(2)}, u32[]{:S(2)}) collective-permute-start(bf16[2,128,256]{2,1,0:T(8,128)(2,1)S(1)} %get-tuple-element.93), channel_id=1, source_target_pairs={{0,3},{1,2},{2,1},{3,0},{4,7},{5,6},{6,5},{7,4},{8,11},{9,10},{10,... | collective-permute-start | bytes 393224 | tf_op jit(solution)/shard_map/ppermute | solution.py:19
  68.6 6.2 %collective-permute-start.22 = (bf16[2,64,256]{2,1,0:T(8,128)(2,1)S(1)}, bf16[2,64,256]{2,1,0:T(8,128)(2,1)S(1)}, u32[]{:S(2)}, u32[]{:S(2)}) collective-permute-start(bf16[2,64,256]{2,1,0:T(8,128)(2,1)S(1)} %add_convert_fusion.2.w_own), channel_id=1, source_target_pairs={{0,1},{1,2},{2,3},{3,0},{4,5},{5,6},{6,7},{7,4},{8,9},{9,10},{10,1... | collective-permute-start | bytes 196616 | tf_op jit(solution)/shard_map/ppermute | solution.py:24
  (5 other events, 19.9 us)
